TPU v7x, 128 devices: a whole 4x4x4 slice. The times are simulated.
128 devices in a mesh: col: 32 (over x_hi, z, y), row: 4 (over x_lo, core).
Axes of the slice: x: 4 (x_hi: 2, x_lo: 2; x = x_hi * 2 + x_lo), y: 4, z: 4, core: 2. Of those that a mesh axis runs over, the one named last changes fastest.
Arguments:
- sigma_anc: float32 [64, 64, 128, 128], P('row', 'col'), as said below
- panel_u: float32 [32, 32, 128, 128], P('col'), may hold values from -0.09375 to 0.09375
- structure: int32 [32, 32], P('col'), may hold values from 0 to 63, as said below
- diag_inv: float32 [32, 128, 128], P('col'), may hold values from -0.5 to 0.5
Outputs:
- panel_out: float32 [32, 64, 128, 128], P('col', 'row')
- diag_out: float32 [32, 128, 128], P('col')
Inputs may be any that keep to these rules, and one draw needn't show every extreme that they name: `structure`: each row holds 32 different ancestor numbers in increasing order. `sigma_anc`: the matrix is symmetric: block (a, b) is the transpose of block (b, a).
All inputs are finite; a program needn't handle non-finite values.
Results may differ from a plain program's by a relative error of at most 0.0003.
Values sent between devices are 32-bit elements; how exact they have to be, the bound alone decides.
No kernel may reach another device: no remote copies, remote signals or barrier semaphores. Data moves between devices by JAX's collectives and lax.ppermute only.
A program may use at most 128 MiB of HBM per device.

v0:
```python
import jax
import jax.numpy as jnp
from jax import lax
from jax.sharding import PartitionSpec as P


def local(sigma_anc, panel_u, structure, diag_inv):
    row_count = sigma_anc.shape[0]
    col_count = sigma_anc.shape[1]
    total_anc = col_count * lax.axis_size("col")
    ancestors = jnp.arange(total_anc, dtype=jnp.int32)
    onehot = (structure[:, :, None] == ancestors[None, None, :]).astype(jnp.float32)
    row_start = lax.axis_index("row") * row_count
    dense = jnp.einsum("jka,jkxy->ajxy", onehot, panel_u, precision=lax.Precision.HIGHEST)
    local_rows = lax.dynamic_slice_in_dim(dense, row_start, row_count, 0)
    moved = lax.all_to_all(dense, "col", split_axis=0, concat_axis=1, tiled=True)
    summed = lax.psum_scatter(
        jnp.einsum("abxz,bjzy->jaxy", sigma_anc, moved, precision=lax.Precision.HIGHEST),
        "col",
        scatter_dimension=0,
        tiled=True,
    )
    local_anc = row_start + jnp.arange(row_count, dtype=jnp.int32)
    member = jnp.any(structure[:, :, None] == local_anc[None, None, :], axis=1).astype(jnp.float32)
    panel_out = -summed * member[:, :, None, None]
    share = jnp.einsum("ajzx,jazy->jxy", local_rows, panel_out, precision=lax.Precision.HIGHEST)
    update = lax.psum(share, "row")
    base = jnp.einsum("jzx,jzy->jxy", diag_inv, diag_inv, precision=lax.Precision.HIGHEST)
    return (panel_out, base - update)


def solution(mesh):
    placed = (
        P("row", "col", None, None),
        P("col", None, None, None),
        P("col", None),
        P("col", None, None),
    )
    return jax.shard_map(
        local,
        mesh=mesh,
        in_specs=placed,
        out_specs=(P("col", "row", None, None), P("col", None, None)),
        check_vma=False,
    )
```

profile of v0, /device:TPU:1, one launch (start us, length us, event | category | flops | bytes accessed | tf_op | source)
XLA Modules:
  0.0 526.7 jit_solution(13694685143304849362)
XLA Ops:
  7.2 0.0 copy-start
  7.2 0.0 reduce-scatter.2.cloned.1.call-start
  7.2 4.9 fusion.1
  12.1 0.0 copy-start.1
  12.1 2.4 copy.18
  14.6 0.0 copy-done.1
  14.6 61.2 %all_to_all.18 = f32[64,1,128,128]{3,2,1,0:T(8,128)} all-to-all(f32[64,1,128,128]{3,2,1,0:T(8,128)S(1)} %copy.18), channel_id=1, replica_groups=mesh['col'=32,'row'=4] {'col'}, dimensions={0} | all-to-all | bytes 8388608 | tf_op jit(solution)/shard_map/all_to_all | solution.py:16
  75.8 5.6 %copy.19 = f32[64,1,128,128]{2,3,0,1:T(8,128)} copy(f32[64,1,128,128]{3,2,1,0:T(8,128)} %all_to_all.18) | data formatting | bytes 8388608 | tf_op jit(solution)/shard_map/all_to_all | solution.py:16
  81.4 0.0 copy-done
  81.4 31.7 %convolution_bitcast_fusion = f32[32,16,128,128]{2,3,1,0:T(8,128)} fusion(f32[2,32,128,128,1]{2,3,0,4,1:T(8,128)} %bitcast.43, f32[16,2,128,128]{3,2,1,0:T(8,128)S(1)} %copy-done), kind=kOutput, calls=%fused_computation | convolution fusion | flops 25769803776 | bytes 39845888 | tf_op jit(solution)/shard_map/abxz,bjzy->jaxy/dot_general | solution.py:18
  113.1 0.0 copy-start.4
  113.1 0.0 reduce-scatter.2.cloned.1.call-update
  113.1 0.0 all-reduce.2.cloned.1.call-start
  113.2 0.6 copy-done.4
  113.7 0.2 compare_reduce_fusion
  113.9 364.4 %reduce-scatter.2.cloned.1.call-done = f32[1,16,128,128]{2,3,1,0:T(8,128)} async-done(((f32[32,16,128,128]{2,3,1,0:T(8,128)}), f32[1,16,128,128]{2,3,1,0:T(8,128)}) %reduce-scatter.2.cloned.1.call-update) | async-done | bytes 1048592 | tf_op jit(solution)/shard_map/reduce_scatter | solution.py:17
  478.3 0.0 copy-start.2
  478.3 2.4 fusion.12
  480.7 2.6 copy.20
  483.3 0.0 copy-start.3
  483.3 4.0 convolution_bitcast_fusion.1
  487.4 0.0 all-reduce.2.cloned.1.call-update
  487.4 0.0 copy-done.2
  487.4 1.1 negate_multiply_fusion
  488.5 2.5 copy.21
  491.0 27.1 %all-reduce.2.cloned.1.call-done = f32[1,128,128]{2,1,0:T(8,128)} async-done(((f32[1,128,128]{2,1,0:T(8,128)}), f32[1,128,128]{2,1,0:T(8,128)}) %all-reduce.2.cloned.1.call-update) | async-done | bytes 65552 | tf_op jit(solution)/shard_map/psum | solution.py:27
  518.1 0.0 copy-done.3
  518.1 1.8 fusion.3
  (2 shorter events, 0.0 us)
Async XLA Ops:
  7.2 74.2 %copy-start = (f32[16,2,128,128]{3,2,1,0:T(8,128)S(1)}, f32[16,2,128,128]{3,2,1,0:T(8,128)}, u32[]{:S(2)}) copy-start(f32[16,2,128,128]{3,2,1,0:T(8,128)} %param.4) | copy-start | bytes 6291460
  7.2 471.1 %reduce-scatter.2.cloned.1.call-start = ((), (), s32[]{:S(2)}) async-start(), calls=%async_computation.2 | async-start | bytes 34603008 | tf_op jit(solution)/shard_map/reduce_scatter | solution.py:17
  12.1 2.4 copy-start.1
  113.1 0.7 copy-start.4
  113.1 405.0 %all-reduce.2.cloned.1.call-start = ((), (), s32[]{:S(2)}) async-start(), calls=%async_computation.3 | async-start | bytes 131072 | tf_op jit(solution)/shard_map/psum | solution.py:27
  478.3 9.1 %copy-start.2 = (f32[1,16,128,128]{2,3,1,0:T(8,128)S(1)}, f32[1,16,128,128]{2,3,1,0:T(8,128)}, u32[]{:S(2)}) copy-start(f32[1,16,128,128]{2,3,1,0:T(8,128)} %reduce-scatter.2.cloned.1.call-done) | copy-start | bytes 3145732
  483.3 34.8 %copy-start.3 = (f32[1,128,128]{2,1,0:T(8,128)S(1)}, f32[1,128,128]{2,1,0:T(8,128)}, u32[]{:S(2)}) copy-start(f32[1,128,128]{2,1,0:T(8,128)} %param.7) | copy-start | bytes 196612
Sparse Core Ops, SparseCore 0:
  113.2 365.0 reduce-scatter.1
  487.5 30.5 all-reduce.1
where the time goes:
time: 527 us
  waiting for transfers between devices  391 us (74%)
  blocking collectives  61.2 us (12%)
  matrix products  42.4 us (8%)
  between operations  14.1 us (3%)
  local copies, waits for them, and re-layouts  13.8 us (3%)
    reduce_scatter x1, waiting for transfers between devices, local(): lax.psum_scatter(jnp.einsum('abxz,bjzy->jaxy', sigma_anc, moved, precisio...  364 us
    all_to_all x1, blocking collectives, local(): lax.all_to_all(dense, 'col', split_axis=0, concat_axis=1, tiled=True)  61.2 us
    dot_general x1, matrix products, local(): jnp.einsum('abxz,bjzy->jaxy', sigma_anc, moved, precision=lax.Precision.H...  31.7 us
    psum x1, waiting for transfers between devices, local(): update = lax.psum(share, 'row')  27.1 us
  transfers between devices with their start and end apart: 2, of which 2 were waited for; matrix products, arithmetic and copies ran while one was open for 1% of the time, Pallas kernels for 0%

commit v1 on v0

v1 whole, which is shorter than its diff:
```python
import functools

import jax
import jax.numpy as jnp
from jax import lax
from jax.experimental import pallas as pl
from jax.experimental.pallas import tpu as pltpu
from jax.sharding import PartitionSpec as P

AXES = ("col", "row")
CORE = 1
X1, X3 = 2, 66
Y1, Y2, Y3 = 4, 8, 12
Z1, Z2, Z3 = 16, 32, 48
B = 128
Q = 32
F32, BF16 = jnp.float32, jnp.bfloat16


def swap(x, mask):
    return lax.ppermute(x, AXES, [(i, i ^ mask) for i in range(128)])


def split(x):
    hi = x.astype(BF16)
    return hi, (x - hi.astype(F32)).astype(BF16)


def dot(a, b):
    return jnp.dot(a, b, preferred_element_type=F32)


def dot3(a, b):
    (ah, al), (bh, bl) = split(a), split(b)
    return dot(ah, bh) + (dot(ah, bl) + dot(al, bh))


def cut_kernel(where, u_ref, label_ref, first_ref, second_ref, turned):
    half = u_ref.shape[0] // 2

    def step(k, carry):
        for i, out_ref in enumerate((first_ref, second_ref)):
            turned[i] = u_ref[i * half + k].T
            out_ref[k] = turned[i, pl.ds(pl.multiple_of(where[0] * Q, Q), Q), :]
        return carry

    lax.fori_loop(0, half, step, 0)
    first_ref[half] = jnp.broadcast_to(label_ref[...].astype(F32), (Q, B))


def cut(panel, labels, row):
    return pl.pallas_call(
        cut_kernel,
        grid_spec=pltpu.PrefetchScalarGridSpec(
            num_scalar_prefetch=1,
            grid=(1,),
            in_specs=[
                pl.BlockSpec((32, B, B), lambda i, w: (0, 0, 0)),
                pl.BlockSpec((1, B), lambda i, w: (0, 0)),
            ],
            out_specs=[pl.BlockSpec((n, Q, B), lambda i, w: (0, 0, 0)) for n in (17, 16)],
            scratch_shapes=[pltpu.VMEM((2, B, B), F32)],
        ),
        out_shape=[jax.ShapeDtypeStruct((n, Q, B), F32) for n in (17, 16)],
        name="cut",
    )(row[None], panel, labels)


def spread_kernel(table, w_ref, hi_ref, lo_ref):
    first = pl.program_id(0) * hi_ref.shape[0]
    for i in range(hi_ref.shape[0]):
        for q in range(16):
            at = table[q * 64 + first + i]
            part = w_ref[jnp.maximum(at, 0)]
            part = jnp.where(at >= 0, part, 0.0)
            hi, lo = split(part)
            hi_ref[i, q * Q : (q + 1) * Q, :] = hi
            lo_ref[i, q * Q : (q + 1) * Q, :] = lo


def spread(table, pieces):
    step = 4
    block = pl.BlockSpec((step, 16 * Q, B), lambda i, t: (i, 0, 0))
    return pl.pallas_call(
        spread_kernel,
        grid_spec=pltpu.PrefetchScalarGridSpec(
            num_scalar_prefetch=1,
            grid=(64 // step,),
            in_specs=[pl.BlockSpec((528, Q, B), lambda i, t: (0, 0, 0))],
            out_specs=[block, block],
        ),
        out_shape=[jax.ShapeDtypeStruct((64, 16 * Q, B), BF16)] * 2,
        compiler_params=pltpu.CompilerParams(vmem_limit_bytes=40 << 20),
        cost_estimate=pl.CostEstimate(flops=1 << 22, bytes_accessed=24 << 20, transcendentals=0),
        name="spread",
    )(table, pieces)


def product_kernel(has_start, where, *refs):
    hi0, hi1, lo0, lo1, left0, left1, right0, right1 = refs[:8]
    out_ref, total = refs[-2:]
    step = pl.program_id(0)
    own = where[2]

    @pl.when(step == 0)
    def _():
        if has_start:
            total[:, :B] = refs[8][own]
            total[:, B:] = refs[8][1 - own]
        else:
            total[...] = jnp.zeros_like(total)

    sigma = jnp.concatenate(
        [
            jnp.concatenate([left0[0], right0[0]], axis=1),
            jnp.concatenate([left1[0], right1[0]], axis=1),
        ],
        axis=0,
    )
    high, low = split(sigma)
    wh = jnp.concatenate([hi0[0], hi1[0]], axis=1)
    wl = jnp.concatenate([lo0[0], lo1[0]], axis=1)
    total[...] += dot(wh, high) + (dot(wh, low) + dot(wl, high))

    @pl.when(step == pl.num_programs(0) - 1)
    def _():
        out_ref[own] = total[:, :B]
        out_ref[1 - own] = total[:, B:]


def product(where, hi, lo, left, right, start=None):
    rows = 16 * Q
    w0 = pl.BlockSpec((1, rows, B), lambda i, w: (w[0] + i, 0, 0))
    w1 = pl.BlockSpec((1, rows, B), lambda i, w: (w[1] + i, 0, 0))
    s = pl.BlockSpec((1, B, B), lambda i, w: (i, 0, 0))
    whole = pl.BlockSpec((2, rows, B), lambda i, w: (0, 0, 0))
    more = [] if start is None else [start]
    return pl.pallas_call(
        functools.partial(product_kernel, start is not None),
        grid_spec=pltpu.PrefetchScalarGridSpec(
            num_scalar_prefetch=1,
            grid=(16,),
            in_specs=[w0, w1, w0, w1, s, s, s, s] + [whole] * len(more),
            out_specs=whole,
            scratch_shapes=[pltpu.VMEM((rows, 2 * B), F32)],
        ),
        out_shape=jax.ShapeDtypeStruct((2, rows, B), F32),
        compiler_params=pltpu.CompilerParams(vmem_limit_bytes=40 << 20),
        cost_estimate=pl.CostEstimate(flops=6 * 512 * 4096 * 256, bytes_accessed=14 << 20, transcendentals=0),
        name="product",
    )(where, hi, hi, lo, lo, *left, *right, *more)


def finish_kernel(where, picks, u_ref, keep0, come0, keep1, come1, panel_ref, share_ref, total):
    even = where[0] == 0
    total[...] = jnp.zeros_like(total)
    for t in range(8):
        for low, (keep, come) in enumerate(((keep0, come0), (keep1, come1))):
            a = 2 * t + low
            pick = picks[a]
            parts = []
            for x in range(2):
                k, c = keep[x, t], come[x, t]
                parts += [jnp.where(even, k, c), jnp.where(even, c, k)]
            turned = jnp.concatenate(parts, axis=0)
            panel_ref[a] = jnp.where(pick >= 0, -turned.T, 0.0)

            @pl.when(pick >= 0)
            def _(turned=turned, pick=pick):
                total[...] += dot3(turned, u_ref[jnp.maximum(pick, 0)])

    share_ref[...] = total[...].T


def finish(core, picks, panel, parts):
    full = lambda *s: pl.BlockSpec(s, lambda i, w, p: (0,) * len(s))
    return pl.pallas_call(
        finish_kernel,
        grid_spec=pltpu.PrefetchScalarGridSpec(
            num_scalar_prefetch=2,
            grid=(1,),
            in_specs=[full(32, B, B)] + [full(2, 8, Q, B)] * 4,
            out_specs=[full(16, B, B), full(B, B)],
            scratch_shapes=[pltpu.VMEM((B, B), F32)],
        ),
        out_shape=[jax.ShapeDtypeStruct((16, B, B), F32), jax.ShapeDtypeStruct((B, B), F32)],
        compiler_params=pltpu.CompilerParams(vmem_limit_bytes=40 << 20),
        name="finish",
    )(core[None], picks, panel, *parts)


def gather_w(first, second):
    a = jnp.stack([first, swap(first, Z1), swap(first, Z2), swap(first, Z3)])
    b = jnp.stack([second, swap(second, Y1), swap(second, Y2), swap(second, Y3)])
    a1, a3 = swap(a, Y1), swap(a, Y3)
    b1, b3 = swap(b, Z1), swap(b, Z3)
    a2 = [swap(a3[:2], Y1), swap(a1[2:], Y3)]
    b2 = [swap(b3[:2], Z1), swap(b1[2:], Z3)]
    parts = [t.reshape(-1, Q, B) for t in (a, a1, *a2, a3, b, b1, *b2, b3)]
    return jnp.concatenate(parts)


def gather_sigma(s):
    x1, x3 = swap(s, X1), swap(s, X3)
    x2 = jnp.concatenate([swap(x3[:8], X1), swap(x1[8:], X3)])
    return [(t, swap(t, CORE)) for t in (s, x1, x3, x2)]


def local(sigma_anc, panel_u, structure, diag_inv):
    col, row = lax.axis_index("col"), lax.axis_index("row")
    x_hi, z, y = col // 16, (col // 4) % 4, col % 4
    x_lo, core = row // 2, row % 2
    panel = panel_u[0]

    gathered = [gather_sigma(sigma_anc[:, i]) for i in range(2)]
    labels = jnp.pad(structure, ((0, 0), (0, B - 32)))
    pieces = gather_w(*cut(panel, labels, row))

    node = jnp.arange(16, dtype=jnp.int32)
    dz, dy = (node // 4) ^ z, (node % 4) ^ y
    there = pieces[: 16 * 17].reshape(16, 17, Q, B)[:, 16, 0, :32].astype(jnp.int32)
    chosen = jnp.sum(jnp.where((dy * 4 + dz)[:, None, None] == node[None, :, None], there[None], 0), axis=1)
    ancestors = jnp.arange(64, dtype=jnp.int32)
    entry = jnp.arange(32, dtype=jnp.int32)
    pick = jnp.sum(jnp.where(chosen[:, :, None] == ancestors, entry[None, :, None] + 1, 0), axis=1) - 1
    first = ((dy * 4 + dz) * 17)[:, None] + pick
    second = (16 * 17 + (dz * 4 + dy) * 16)[:, None] + pick - 16
    table = jnp.where(pick < 0, -1, jnp.where(pick < 16, first, second)).reshape(-1)
    mine = jnp.sum(jnp.where(structure[0][:, None] == (16 * row + jnp.arange(16))[None, :], entry[:, None] + 1, 0), axis=0) - 1

    hi, lo = spread(table, pieces)
    own = jnp.stack([32 * x_lo + 16 * core, 32 * x_lo + 16 * (1 - core), x_hi])
    other = jnp.stack([32 * (1 - x_lo) + 16 * core, 32 * (1 - x_lo) + 16 * (1 - core), x_hi])
    groups = [
        [h * 64 + q * 4 + l * 2 + c for l in range(2) for q in range(16)] for h in range(2) for c in range(2)
    ]
    parts = []
    for s, x1, x3, x2 in gathered:
        part = product(other, hi, lo, x1, x3)
        part = product(own, hi, lo, s, x2, part)
        moved = lax.all_to_all(part.reshape(32, Q, B), AXES, 0, 0, axis_index_groups=groups, tiled=True)
        moved = moved.reshape(2, 2, 8, Q, B)
        keep = lax.dynamic_index_in_dim(moved, core, 1, keepdims=False)
        send = lax.dynamic_index_in_dim(moved, 1 - core, 1, keepdims=False)
        parts += [keep, swap(send, CORE)]

    panel_out, share = finish(core, mine, panel, parts)
    base = jnp.einsum("zx,zy->xy", diag_inv[0], diag_inv[0], precision=lax.Precision.HIGHEST)
    diag = base + jnp.sum(lax.all_gather(share, "row"), axis=0)
    return panel_out[None], diag[None]


def solution(mesh):
    return jax.shard_map(
        local,
        mesh=mesh,
        in_specs=(P("row", "col", None, None), P("col", None, None, None), P("col", None), P("col", None, None)),
        out_specs=(P("col", "row", None, None), P("col", None, None)),
        check_vma=False,
    )
```

time: 527 us -> 238 us (0.45)
  waiting for transfers between devices: 391 us -> 50.8 us
  Pallas kernels: 0 us -> 71.6 us
  blocking collectives: 61.2 us -> 6.15 us
  starting transfers between devices: 0.08 us -> 54 us
  matrix products: 42.4 us -> 0.92 us
  local copies, waits for them, and re-layouts: 13.8 us -> 47 us
  between operations: 14.1 us -> 1.04 us
    reduce_scatter x1 -> x0, waiting for transfers between devices: 364 us -> none  [local(): lax.psum_scatter(jnp.einsum('abxz,bjzy->jaxy', sigma_anc, moved, precisio...]
    pallas_call x0 -> x7, Pallas kernels: none -> 71.6 us  [the longest x4 50.7 us: product(): pl.pallas_call(functools.partial(product_kernel, start is not None), grid...]
    all_to_all x1 -> x0, blocking collectives: 61.2 us -> none  [local(): lax.all_to_all(dense, 'col', split_axis=0, concat_axis=1, tiled=True)]
    ppermute x0 -> x32, waiting for transfers between devices: none -> 42.6 us  [swap(): return lax.ppermute(x, AXES, [(i, i ^ mask) for i in range(128)])]
    dot_general x4 -> x1, matrix products: 42.4 us -> 0.92 us  [local(): jnp.einsum('zx,zy->xy', diag_inv[0], diag_inv[0], precision=lax.Precision...]
    ppermute x0 -> x32, starting transfers between devices: none -> 41.4 us  [swap(): return lax.ppermute(x, AXES, [(i, i ^ mask) for i in range(128)])]
    psum x1 -> x0, waiting for transfers between devices: 27.1 us -> none  [local(): update = lax.psum(share, 'row')]
    unnamed x11 -> x47, local copies, waits for them, and re-layouts: 3.12 us -> 30 us
  transfers between devices with their start and end apart: 2 -> 34, of which waited for: 2 -> 12; matrix products, arithmetic and copies ran while one was open for 1% -> 16% of each run, Pallas kernels for 0% -> 28%
where the time goes in v1:
time: 238 us; the launch traced here: 236 us
  Pallas kernels  71.6 us (30%)
  starting transfers between devices  54 us (23%)
  waiting for transfers between devices  50.8 us (21%)
  local copies, waits for them, and re-layouts  47 us (20%)
  blocking collectives  6.15 us (3%)
  other arithmetic  4.77 us (2%)
    pallas_call x4, Pallas kernels, product(): pl.pallas_call(functools.partial(product_kernel, start is not None), grid...  50.7 us
    ppermute x32, waiting for transfers between devices, swap(): return lax.ppermute(x, AXES, [(i, i ^ mask) for i in range(128)])  42.6 us
    ppermute x32, starting transfers between devices, swap(): return lax.ppermute(x, AXES, [(i, i ^ mask) for i in range(128)])  41.4 us
    unnamed x47, local copies, waits for them, and re-layouts  30 us
    all_to_all x2, starting transfers between devices, local(): lax.all_to_all(part.reshape(32, Q, B), AXES, 0, 0, axis_index_groups=grou...  12.6 us
    pallas_call x1, Pallas kernels, spread(): pl.pallas_call(spread_kernel, grid_spec=pltpu.PrefetchScalarGridSpec(num_...  12.3 us
    all_to_all x2, waiting for transfers between devices, local(): lax.all_to_all(part.reshape(32, Q, B), AXES, 0, 0, axis_index_groups=grou...  8.19 us
    all_gather x1, blocking collectives, local(): diag = base + jnp.sum(lax.all_gather(share, 'row'), axis=0)  6.15 us
  transfers between devices with their start and end apart: 34, of which 12 were waited for; matrix products, arithmetic and copies ran while one was open for 16% of the time, Pallas kernels for 28%

profile of v1, /device:TPU:1, one launch (start us, length us, event | category | flops | bytes accessed | tf_op | source)
XLA Modules:
  0.0 236.2 jit_solution(16256058970278397513)
XLA Ops:
  0.6 1.8 slice_bitcast_fusion
  2.4 2.1 collective-permute-start.26
  4.6 1.2 pad.4.label_ref
  5.7 4.2 %cut.1 = (f32[17,32,128]{2,1,0:T(8,128)}, f32[16,32,128]{2,1,0:T(8,128)}) custom-call(s32[1]{0:T(128)} %bitcast.6.where, f32[32,128,128]{2,1,0:T(8,128)} %bitcast.56, s32[1,128]{1,0:T(1,128)} %pad.4.label_ref), custom_call_target="tpu_custom_call" | custom-call | tf_op jit(solution)/shard_map/cut/pallas_call | solution.py:52
  9.9 1.3 collective-permute-start.7
  11.2 1.9 collective-permute-start.24
  13.3 2.6 %collective-permute-start.8 = (f32[16,32,128]{2,1,0:T(8,128)}, f32[16,32,128]{2,1,0:T(8,128)S(1)}, u32[]{:S(2)}, u32[]{:S(2)}) collective-permute-start(f32[16,32,128]{2,1,0:T(8,128)} %get-tuple-element.9), channel_id=1, source_target_pairs={{0,8},{1,9},{2,10},{3,11},{4,12},{5,13},{6,14},{7,15},{8,0},{9,1},... | collective-permute-start | bytes 786440 | tf_op jit(solution)/shard_map/ppermute | solution.py:21
  15.9 1.1 collective-permute-done.7
  17.1 2.7 %collective-permute-start.9 = (f32[16,32,128]{2,1,0:T(8,128)}, f32[16,32,128]{2,1,0:T(8,128)S(1)}, u32[]{:S(2)}, u32[]{:S(2)}) collective-permute-start(f32[16,32,128]{2,1,0:T(8,128)} %get-tuple-element.9), channel_id=1, source_target_pairs={{0,12},{1,13},{2,14},{3,15},{4,8},{5,9},{6,10},{7,11},{8,4},{9,5},... | collective-permute-start | bytes 786440 | tf_op jit(solution)/shard_map/ppermute | solution.py:21
  19.8 5.3 %collective-permute-done.8 = f32[16,32,128]{2,1,0:T(8,128)S(1)} collective-permute-done((f32[16,32,128]{2,1,0:T(8,128)}, f32[16,32,128]{2,1,0:T(8,128)S(1)}, u32[]{:S(2)}, u32[]{:S(2)}) %collective-permute-start.8) | collective-permute-done | bytes 262176 | tf_op jit(solution)/shard_map/ppermute | solution.py:21
  25.1 3.8 %collective-permute-start.2 = (f32[17,32,128]{2,1,0:T(8,128)}, f32[17,32,128]{2,1,0:T(8,128)S(1)}, u32[]{:S(2)}, u32[]{:S(2)}) collective-permute-start(f32[17,32,128]{2,1,0:T(8,128)} %get-tuple-element.8), channel_id=1, source_target_pairs={{0,48},{1,49},{2,50},{3,51},{4,52},{5,53},{6,54},{7,55},{8,56},{9,... | collective-permute-start | bytes 835592 | tf_op jit(solution)/shard_map/ppermute | solution.py:21
  28.8 2.0 collective-permute-done.9
  30.9 1.6 collective-permute-start
  32.5 1.6 collective-permute-done.2
  34.1 1.7 collective-permute-start.1
  35.8 2.7 %collective-permute-done = f32[17,32,128]{2,1,0:T(8,128)S(1)} collective-permute-done((f32[17,32,128]{2,1,0:T(8,128)}, f32[17,32,128]{2,1,0:T(8,128)S(1)}, u32[]{:S(2)}, u32[]{:S(2)}) %collective-permute-start) | collective-permute-done | bytes 278560 | tf_op jit(solution)/shard_map/ppermute | solution.py:21
  38.5 2.2 collective-permute-start.15
  40.7 2.0 pad_maximum_fusion.1
  42.7 4.9 %collective-permute-done.1 = f32[17,32,128]{2,1,0:T(8,128)S(1)} collective-permute-done((f32[17,32,128]{2,1,0:T(8,128)}, f32[17,32,128]{2,1,0:T(8,128)S(1)}, u32[]{:S(2)}, u32[]{:S(2)}) %collective-permute-start.1) | collective-permute-done | bytes 278560 | tf_op jit(solution)/shard_map/ppermute | solution.py:21
  47.6 2.0 pad_maximum_fusion
  49.7 1.0 copy-done.5
  50.6 1.1 collective-permute-start.3
  51.8 1.1 slice.53
  52.9 8.4 %collective-permute-done.15.refs_6_ = f32[16,128,128]{2,1,0:T(8,128)} collective-permute-done((f32[16,128,128]{2,1,0:T(8,128)S(1)}, f32[16,128,128]{2,1,0:T(8,128)}, u32[]{:S(2)}, u32[]{:S(2)}) %collective-permute-start.15) | collective-permute-done | bytes 1048608 | tf_op jit(solution)/shard_map/ppermute | solution.py:21
  61.4 1.1 slice.51
  62.5 7.9 %collective-permute-done.10 = f32[4,16,32,128]{3,2,1,0:T(8,128)} collective-permute-done((f32[4,16,32,128]{3,2,1,0:T(8,128)}, f32[4,16,32,128]{3,2,1,0:T(8,128)}, u32[]{:S(2)}, u32[]{:S(2)}) %collective-permute-start.10) | collective-permute-done | bytes 1048608 | tf_op jit(solution)/shard_map/ppermute | solution.py:21
  71.2 1.1 slice.54
  72.3 2.0 collective-permute-start.27
  74.3 2.4 %constant_dynamic-update-slice_fusion.14 = (f32[528,32,128]{2,1,0:T(8,128)}, f32[272,32,128]{2,1,0:T(8,128)S(1)}) fusion(f32[68,32,128]{2,1,0:T(8,128)} %bitcast.11), kind=kLoop, calls=%fused_computation.28 | loop fusion | bytes 3342336
  76.8 1.1 slice.49
  77.8 1.1 slice.50
  79.8 1.1 slice.46
  81.6 2.4 %constant_dynamic-update-slice_fusion.13 = (f32[528,32,128]{2,1,0:T(8,128)}, f32[272,32,128]{2,1,0:T(8,128)S(1)}) fusion(f32[528,32,128]{2,1,0:T(8,128)} %get-tuple-element.22, f32[68,32,128]{2,1,0:T(8,128)} %bitcast.12, f32[272,32,128]{2,1,0:T(8,128)S(1)} %get-tuple-element.23), kind=kLoop, calls=%fused_computation.27 | loop fusion | bytes 3342336
  84.0 1.1 slice.47
  85.1 2.7 %collective-permute-start.6 = (f32[2,17,32,128]{3,2,1,0:T(8,128)S(1)}, f32[2,17,32,128]{3,2,1,0:T(8,128)S(1)}, u32[]{:S(2)}, u32[]{:S(2)}) collective-permute-start(f32[2,17,32,128]{3,2,1,0:T(8,128)S(1)} %slice.47), channel_id=1, source_target_pairs={{0,12},{1,13},{2,14},{3,15},{4,8},{5,9},{6,10},{7,11},{8,4},{9,5},... | collective-permute-start | bytes 1671176 | tf_op jit(solution)/shard_map/ppermute | solution.py:21
  88.6 3.5 %collective-permute-start.23 = (f32[16,128,128]{2,1,0:T(8,128)S(1)}, f32[16,128,128]{2,1,0:T(8,128)S(1)}, u32[]{:S(2)}, u32[]{:S(2)}) collective-permute-start(f32[16,128,128]{2,1,0:T(8,128)S(1)} %get-tuple-element.16.refs_4_), channel_id=1, source_target_pairs={{0,1},{1,0},{2,3},{3,2},{4,5},{5,4},{6,7},{7,6},{8,9},{9,8},{10,11... | collective-permute-start | bytes 3145736 | tf_op jit(solution)/shard_map/ppermute | solution.py:21
  93.9 1.2 collective-permute-done.18
  95.0 4.1 %collective-permute-start.30 = (f32[16,128,128]{2,1,0:T(8,128)S(1)}, f32[16,128,128]{2,1,0:T(8,128)S(1)}, u32[]{:S(2)}, u32[]{:S(2)}) collective-permute-start(f32[16,128,128]{2,1,0:T(8,128)S(1)} %copy-done.6), channel_id=1, source_target_pairs={{0,1},{1,0},{2,3},{3,2},{4,5},{5,4},{6,7},{7,6},{8,9},{9,8},{10,11... | collective-permute-start | bytes 3145736 | tf_op jit(solution)/shard_map/ppermute | solution.py:21
  102.1 2.4 %constant_dynamic-update-slice_fusion.10 = (f32[528,32,128]{2,1,0:T(8,128)}, f32[272,32,128]{2,1,0:T(8,128)S(1)}) fusion(f32[528,32,128]{2,1,0:T(8,128)} %get-tuple-element.24, f32[68,32,128]{2,1,0:T(8,128)} %bitcast.15, f32[272,32,128]{2,1,0:T(8,128)S(1)} %get-tuple-element.25), kind=kLoop, calls=%fused_computation.24 | loop fusion | bytes 3342336
  104.8 2.3 constant_dynamic-update-slice_fusion.9
  107.1 6.5 %collective-permute-done.12 = f32[2,16,32,128]{3,2,1,0:T(8,128)S(1)} collective-permute-done((f32[2,16,32,128]{3,2,1,0:T(8,128)S(1)}, f32[2,16,32,128]{3,2,1,0:T(8,128)S(1)}, u32[]{:S(2)}, u32[]{:S(2)}) %collective-permute-start.12) | collective-permute-done | bytes 524320 | tf_op jit(solution)/shard_map/ppermute | solution.py:21
  114.3 2.3 constant_dynamic-update-slice_fusion.8
  117.4 1.0 copy-done.10
  119.0 1.0 copy-done.12
  120.0 1.0 copy-done.14
  122.4 2.5 %constant_dynamic-update-slice_fusion.5.w_ref = f32[528,32,128]{2,1,0:T(8,128)} fusion(f32[528,32,128]{2,1,0:T(8,128)} %constant_dynamic-update-slice_fusion.6, f32[64,32,128]{2,1,0:T(8,128)} %bitcast.26), kind=kLoop, calls=%fused_computation.19 | loop fusion | bytes 2097152 | tf_op jit(solution)/shard_map/concatenate | solution.py:200
  124.9 12.3 %spread.1 = (bf16[64,512,128]{2,1,0:T(8,128)(2,1)S(1)}, bf16[64,512,128]{2,1,0:T(8,128)(2,1)}) custom-call(s32[1024]{0:T(1024)S(1)} %reshape.181.table, f32[528,32,128]{2,1,0:T(8,128)} %constant_dynamic-update-slice_fusion.5.w_ref), custom_call_target="tpu_custom_call" | custom-call | flops 4194304 | bytes 25165824 | tf_op jit(solution)/shard_map/spread/pallas_call | solution.py:84
  137.3 13.5 %product.6.refs_8_ = f32[2,512,128]{2,1,0:T(8,128)S(1)} custom-call(s32[3]{0:T(128)S(1)} %get-tuple-element.33.where, bf16[64,512,128]{2,1,0:T(8,128)(2,1)S(1)} %get-tuple-element.10.refs_0_.refs_1_, bf16[64,512,128]{2,1,0:T(8,128)(2,1)S(1)} %get-tuple-element.10.refs_0_.refs_1_, bf16[64,512,128]{2,1,0:T(8,128)(2,1)} %get-tuple-element.11.refs_2_.refs_3_, ...), custom_call_target="tpu_custom_call" | custom-call | flops 3221225472 | bytes 14680064 | tf_op jit(solution)/shard_map/product/pallas_call | solution.py:138
  150.8 3.4 %copy-done.2 = bf16[64,512,128]{2,1,0:T(8,128)(2,1)S(1)} copy-done((bf16[64,512,128]{2,1,0:T(8,128)(2,1)S(1)}, bf16[64,512,128]{2,1,0:T(8,128)(2,1)}, u32[]{:S(2)}) %copy-start.2) | copy-done | bytes 8388632
  154.2 12.2 %product.7 = f32[2,512,128]{2,1,0:T(8,128)S(1)} custom-call(s32[3]{0:T(128)S(1)} %get-tuple-element.32.where, bf16[64,512,128]{2,1,0:T(8,128)(2,1)S(1)} %copy-done.2, bf16[64,512,128]{2,1,0:T(8,128)(2,1)S(1)} %copy-done.2, bf16[64,512,128]{2,1,0:T(8,128)(2,1)} %get-tuple-element.11.refs_2_.refs_3_, bf16[64,512,128]{2,1,0:T(8,128)(2,1)} %get-tuple-element.11.refs_2_.refs_3_, ...), custom_call_target="tpu_custom_call" | custom-call | flops 3221225472 | bytes 14680064 | tf_op jit(solution)/shard_map/product/pallas_call | solution.py:138
  167.2 4.9 %all-to-all-start.1 = ((f32[32,32,128]{2,1,0:T(8,128)}), f32[32,32,128]{2,1,0:T(8,128)}, u32[]{:S(2)}, u32[]{:S(2)}) async-start(f32[32,32,128]{2,1,0:T(8,128)} %bitcast.59), calls=%async_computation.1 | async-start | bytes 1048576 | tf_op jit(solution)/shard_map/all_to_all | solution.py:241
  172.2 3.4 %copy-done.3 = bf16[64,512,128]{2,1,0:T(8,128)(2,1)S(1)} copy-done((bf16[64,512,128]{2,1,0:T(8,128)(2,1)S(1)}, bf16[64,512,128]{2,1,0:T(8,128)(2,1)}, u32[]{:S(2)}) %copy-start.3) | copy-done | bytes 8388632
  175.5 12.5 %product.4.refs_8_ = f32[2,512,128]{2,1,0:T(8,128)S(1)} custom-call(s32[3]{0:T(128)S(1)} %get-tuple-element.33.where, bf16[64,512,128]{2,1,0:T(8,128)(2,1)S(1)} %copy-done.3, bf16[64,512,128]{2,1,0:T(8,128)(2,1)S(1)} %copy-done.3, bf16[64,512,128]{2,1,0:T(8,128)(2,1)} %get-tuple-element.11.refs_2_.refs_3_, ...), custom_call_target="tpu_custom_call" | custom-call | flops 3221225472 | bytes 14680064 | tf_op jit(solution)/shard_map/product/pallas_call | solution.py:138
  188.0 12.5 %product.5 = f32[2,512,128]{2,1,0:T(8,128)S(1)} custom-call(s32[3]{0:T(128)S(1)} %get-tuple-element.32.where, bf16[64,512,128]{2,1,0:T(8,128)(2,1)S(1)} %copy-done.3, bf16[64,512,128]{2,1,0:T(8,128)(2,1)S(1)} %copy-done.3, bf16[64,512,128]{2,1,0:T(8,128)(2,1)} %get-tuple-element.11.refs_2_.refs_3_, bf16[64,512,128]{2,1,0:T(8,128)(2,1)} %get-tuple-element.11.refs_2_.refs_3_, ...), custom_call_target="tpu_custom_call" | custom-call | flops 3221225472 | bytes 14680064 | tf_op jit(solution)/shard_map/product/pallas_call | solution.py:138
  201.4 7.7 %all-to-all-start = ((f32[32,32,128]{2,1,0:T(8,128)}), f32[32,32,128]{2,1,0:T(8,128)S(1)}, u32[]{:S(2)}, u32[]{:S(2)}) async-start(f32[32,32,128]{2,1,0:T(8,128)} %bitcast.58), calls=%async_computation | async-start | bytes 1048576 | tf_op jit(solution)/shard_map/all_to_all | solution.py:241
  209.1 1.1 dynamic-slice_bitcast_fusion
  210.2 0.9 collective-permute-start.31
  211.1 8.2 %all-to-all-done = f32[32,32,128]{2,1,0:T(8,128)S(1)} async-done(((f32[32,32,128]{2,1,0:T(8,128)}), f32[32,32,128]{2,1,0:T(8,128)S(1)}, u32[]{:S(2)}, u32[]{:S(2)}) %all-to-all-start) | async-done | bytes 524320 | tf_op jit(solution)/shard_map/all_to_all | solution.py:241
  220.1 1.1 dynamic-slice_bitcast_fusion.2
  221.2 2.4 %collective-permute-start.22 = (f32[2,8,32,128]{3,2,1,0:T(8,128)S(1)}, f32[2,8,32,128]{3,2,1,0:T(8,128)S(1)}, u32[]{:S(2)}, u32[]{:S(2)}) collective-permute-start(f32[2,8,32,128]{3,2,1,0:T(8,128)S(1)} %get-tuple-element.30), channel_id=1, source_target_pairs={{0,1},{1,0},{2,3},{3,2},{4,5},{5,4},{6,7},{7,6},{8,9},{9,8},{10,11... | collective-permute-start | bytes 786440 | tf_op jit(solution)/shard_map/ppermute | solution.py:21
  223.7 1.0 collective-permute-done.22.come0
  224.7 4.4 %finish.1 = (f32[16,128,128]{2,1,0:T(8,128)}, f32[128,128]{1,0:T(8,128)S(1)}) custom-call(s32[1]{0:T(128)} %bitcast.where, s32[16]{0:T(128)S(1)} %broadcast_add_fusion.picks, f32[32,128,128]{2,1,0:T(8,128)S(1)} %bitcast.57, f32[2,8,32,128]{3,2,1,0:T(8,128)S(1)} %get-tuple-element.31.keep0, f32[2,8,32,128]{3,2,1,0:T(8,128)S(1)} %collective-permute-done.22.come0, ...), custom_call_target="tpu_custom_call" | custom-call | tf_op jit(solution)/shard_map/finish/pallas_call | solution.py:177
  229.1 6.2 %all-gather = f32[512,128]{1,0:T(8,128)S(1)} all-gather(f32[128,128]{1,0:T(8,128)S(1)} %get-tuple-element.13), channel_id=2, replica_groups=mesh['col'=32,'row'=4] {'row'}, dimensions={0}, use_global_device_ids=true | all-gather | bytes 327680 | tf_op jit(solution)/shard_map/all_gather | solution.py:249
  235.3 0.9 fusion
  (90 shorter events, 14.8 us)
Async XLA Ops:
  0.6 234.6 %copy-start = (f32[1,128,128]{2,1,0:T(8,128)S(1)}, f32[1,128,128]{2,1,0:T(8,128)}, u32[]{:S(2)}) copy-start(f32[1,128,128]{2,1,0:T(8,128)} %param.7) | copy-start | bytes 196612
  2.4 45.1 %collective-permute-start.26 = (f32[16,128,128]{2,1,0:T(8,128)S(1)}, f32[16,128,128]{2,1,0:T(8,128)}, u32[]{:S(2)}, u32[]{:S(2)}) collective-permute-start(f32[16,128,128]{2,1,0:T(8,128)S(1)} %get-tuple-element.16.refs_4_), channel_id=1, source_target_pairs={{0,2},{1,3},{2,0},{3,1},{4,6},{5,7},{6,4},{7,5},{8,10},{9,11},{10,... | collective-permute-start | bytes 3145736 | tf_op jit(solution)/shard_map/ppermute | solution.py:21
  9.9 7.2 %collective-permute-start.7 = (f32[16,32,128]{2,1,0:T(8,128)}, f32[16,32,128]{2,1,0:T(8,128)S(1)}, u32[]{:S(2)}, u32[]{:S(2)}) collective-permute-start(f32[16,32,128]{2,1,0:T(8,128)} %get-tuple-element.9), channel_id=1, source_target_pairs={{0,4},{1,5},{2,6},{3,7},{4,0},{5,1},{6,2},{7,3},{8,12},{9,13},{10,... | collective-permute-start | bytes 786440 | tf_op jit(solution)/shard_map/ppermute | solution.py:21
  11.2 38.5 %collective-permute-start.24 = (f32[16,128,128]{2,1,0:T(8,128)S(1)}, f32[16,128,128]{2,1,0:T(8,128)S(1)}, u32[]{:S(2)}, u32[]{:S(2)}) collective-permute-start(f32[16,128,128]{2,1,0:T(8,128)S(1)} %get-tuple-element.16.refs_4_), channel_id=1, source_target_pairs={{0,66},{1,67},{2,64},{3,65},{4,70},{5,71},{6,68},{7,69},{8,74},{9,... | collective-permute-start | bytes 3145736 | tf_op jit(solution)/shard_map/ppermute | solution.py:21
  13.1 36.6 %collective-permute-start.17 = (f32[16,128,128]{2,1,0:T(8,128)S(1)}, f32[16,128,128]{2,1,0:T(8,128)S(1)}, u32[]{:S(2)}, u32[]{:S(2)}) collective-permute-start(f32[16,128,128]{2,1,0:T(8,128)S(1)} %get-tuple-element.17.refs_4_), channel_id=1, source_target_pairs={{0,2},{1,3},{2,0},{3,1},{4,6},{5,7},{6,4},{7,5},{8,10},{9,11},{10,... | collective-permute-start | bytes 3145736 | tf_op jit(solution)/shard_map/ppermute | solution.py:21
  13.3 11.8 %collective-permute-start.8 = (f32[16,32,128]{2,1,0:T(8,128)}, f32[16,32,128]{2,1,0:T(8,128)S(1)}, u32[]{:S(2)}, u32[]{:S(2)}) collective-permute-start(f32[16,32,128]{2,1,0:T(8,128)} %get-tuple-element.9), channel_id=1, source_target_pairs={{0,8},{1,9},{2,10},{3,11},{4,12},{5,13},{6,14},{7,15},{8,0},{9,1},... | collective-permute-start | bytes 786440 | tf_op jit(solution)/shard_map/ppermute | solution.py:21
  17.1 13.8 %collective-permute-start.9 = (f32[16,32,128]{2,1,0:T(8,128)}, f32[16,32,128]{2,1,0:T(8,128)S(1)}, u32[]{:S(2)}, u32[]{:S(2)}) collective-permute-start(f32[16,32,128]{2,1,0:T(8,128)} %get-tuple-element.9), channel_id=1, source_target_pairs={{0,12},{1,13},{2,14},{3,15},{4,8},{5,9},{6,10},{7,11},{8,4},{9,5},... | collective-permute-start | bytes 786440 | tf_op jit(solution)/shard_map/ppermute | solution.py:21
  25.1 9.0 %collective-permute-start.2 = (f32[17,32,128]{2,1,0:T(8,128)}, f32[17,32,128]{2,1,0:T(8,128)S(1)}, u32[]{:S(2)}, u32[]{:S(2)}) collective-permute-start(f32[17,32,128]{2,1,0:T(8,128)} %get-tuple-element.8), channel_id=1, source_target_pairs={{0,48},{1,49},{2,50},{3,51},{4,52},{5,53},{6,54},{7,55},{8,56},{9,... | collective-permute-start | bytes 835592 | tf_op jit(solution)/shard_map/ppermute | solution.py:21
  30.9 7.6 %collective-permute-start = (f32[17,32,128]{2,1,0:T(8,128)}, f32[17,32,128]{2,1,0:T(8,128)S(1)}, u32[]{:S(2)}, u32[]{:S(2)}) collective-permute-start(f32[17,32,128]{2,1,0:T(8,128)} %get-tuple-element.8), channel_id=1, source_target_pairs={{0,16},{1,17},{2,18},{3,19},{4,20},{5,21},{6,22},{7,23},{8,24},{9,... | collective-permute-start | bytes 835592 | tf_op jit(solution)/shard_map/ppermute | solution.py:21
  34.1 13.5 %collective-permute-start.1 = (f32[17,32,128]{2,1,0:T(8,128)}, f32[17,32,128]{2,1,0:T(8,128)S(1)}, u32[]{:S(2)}, u32[]{:S(2)}) collective-permute-start(f32[17,32,128]{2,1,0:T(8,128)} %get-tuple-element.8), channel_id=1, source_target_pairs={{0,32},{1,33},{2,34},{3,35},{4,36},{5,37},{6,38},{7,39},{8,40},{9,... | collective-permute-start | bytes 835592 | tf_op jit(solution)/shard_map/ppermute | solution.py:21
  38.5 22.8 %collective-permute-start.15 = (f32[16,128,128]{2,1,0:T(8,128)S(1)}, f32[16,128,128]{2,1,0:T(8,128)}, u32[]{:S(2)}, u32[]{:S(2)}) collective-permute-start(f32[16,128,128]{2,1,0:T(8,128)S(1)} %get-tuple-element.17.refs_4_), channel_id=1, source_target_pairs={{0,66},{1,67},{2,64},{3,65},{4,70},{5,71},{6,68},{7,69},{8,74},{9,... | collective-permute-start | bytes 3145736 | tf_op jit(solution)/shard_map/ppermute | solution.py:21
  47.6 22.8 %collective-permute-start.10 = (f32[4,16,32,128]{3,2,1,0:T(8,128)}, f32[4,16,32,128]{3,2,1,0:T(8,128)}, u32[]{:S(2)}, u32[]{:S(2)}) collective-permute-start(f32[4,16,32,128]{3,2,1,0:T(8,128)} %pad_maximum_fusion.1), channel_id=1, source_target_pairs={{0,16},{1,17},{2,18},{3,19},{4,20},{5,21},{6,22},{7,23},{8,24},{9,... | collective-permute-start | bytes 3145736 | tf_op jit(solution)/shard_map/ppermute | solution.py:21
  47.6 24.7 %collective-permute-start.11 = (f32[4,16,32,128]{3,2,1,0:T(8,128)}, f32[4,16,32,128]{3,2,1,0:T(8,128)}, u32[]{:S(2)}, u32[]{:S(2)}) collective-permute-start(f32[4,16,32,128]{3,2,1,0:T(8,128)} %pad_maximum_fusion.1), channel_id=1, source_target_pairs={{0,48},{1,49},{2,50},{3,51},{4,52},{5,53},{6,54},{7,55},{8,56},{9,... | collective-permute-start | bytes 3145736 | tf_op jit(solution)/shard_map/ppermute | solution.py:21
  49.7 1.0 copy-start.5
  49.7 29.3 %collective-permute-start.4 = (f32[4,17,32,128]{3,2,1,0:T(8,128)}, f32[4,17,32,128]{3,2,1,0:T(8,128)}, u32[]{:S(2)}, u32[]{:S(2)}) collective-permute-start(f32[4,17,32,128]{3,2,1,0:T(8,128)} %pad_maximum_fusion), channel_id=1, source_target_pairs={{0,12},{1,13},{2,14},{3,15},{4,8},{5,9},{6,10},{7,11},{8,4},{9,5},... | collective-permute-start | bytes 3342344 | tf_op jit(solution)/shard_map/ppermute | solution.py:21
  50.6 30.2 %collective-permute-start.3 = (f32[4,17,32,128]{3,2,1,0:T(8,128)}, f32[4,17,32,128]{3,2,1,0:T(8,128)}, u32[]{:S(2)}, u32[]{:S(2)}) collective-permute-start(f32[4,17,32,128]{3,2,1,0:T(8,128)} %pad_maximum_fusion), channel_id=1, source_target_pairs={{0,4},{1,5},{2,6},{3,7},{4,0},{5,1},{6,2},{7,3},{8,12},{9,13},{10,... | collective-permute-start | bytes 3342344 | tf_op jit(solution)/shard_map/ppermute | solution.py:21
  61.3 23.8 %collective-permute-start.25 = (f32[8,128,128]{2,1,0:T(8,128)S(1)}, f32[8,128,128]{2,1,0:T(8,128)S(1)}, u32[]{:S(2)}, u32[]{:S(2)}) collective-permute-start(f32[8,128,128]{2,1,0:T(8,128)S(1)} %slice.53), channel_id=1, source_target_pairs={{0,2},{1,3},{2,0},{3,1},{4,6},{5,7},{6,4},{7,5},{8,10},{9,11},{10,... | collective-permute-start | bytes 1572872 | tf_op jit(solution)/shard_map/ppermute | solution.py:21
  62.5 32.6 %copy-start.6 = (f32[16,128,128]{2,1,0:T(8,128)S(1)}, f32[16,128,128]{2,1,0:T(8,128)}, u32[]{:S(2)}) copy-start(f32[16,128,128]{2,1,0:T(8,128)} %copy-done.5) | copy-start | bytes 3145732
  70.4 18.2 %collective-permute-start.16 = (f32[8,128,128]{2,1,0:T(8,128)S(1)}, f32[8,128,128]{2,1,0:T(8,128)S(1)}, u32[]{:S(2)}, u32[]{:S(2)}) collective-permute-start(f32[8,128,128]{2,1,0:T(8,128)S(1)} %slice.51), channel_id=1, source_target_pairs={{0,2},{1,3},{2,0},{3,1},{4,6},{5,7},{6,4},{7,5},{8,10},{9,11},{10,... | collective-permute-start | bytes 1572872 | tf_op jit(solution)/shard_map/ppermute | solution.py:21
  72.3 20.7 %collective-permute-start.27 = (f32[8,128,128]{2,1,0:T(8,128)S(1)}, f32[8,128,128]{2,1,0:T(8,128)S(1)}, u32[]{:S(2)}, u32[]{:S(2)}) collective-permute-start(f32[8,128,128]{2,1,0:T(8,128)S(1)} %slice.54), channel_id=1, source_target_pairs={{0,66},{1,67},{2,64},{3,65},{4,70},{5,71},{6,68},{7,69},{8,74},{9,... | collective-permute-start | bytes 1572872 | tf_op jit(solution)/shard_map/ppermute | solution.py:21
  78.9 16.1 %collective-permute-start.18 = (f32[8,128,128]{2,1,0:T(8,128)S(1)}, f32[8,128,128]{2,1,0:T(8,128)S(1)}, u32[]{:S(2)}, u32[]{:S(2)}) collective-permute-start(f32[8,128,128]{2,1,0:T(8,128)S(1)} %slice.52), channel_id=1, source_target_pairs={{0,66},{1,67},{2,64},{3,65},{4,70},{5,71},{6,68},{7,69},{8,74},{9,... | collective-permute-start | bytes 1572872 | tf_op jit(solution)/shard_map/ppermute | solution.py:21
  80.9 19.1 %collective-permute-start.5 = (f32[2,17,32,128]{3,2,1,0:T(8,128)S(1)}, f32[2,17,32,128]{3,2,1,0:T(8,128)S(1)}, u32[]{:S(2)}, u32[]{:S(2)}) collective-permute-start(f32[2,17,32,128]{3,2,1,0:T(8,128)S(1)} %slice.46), channel_id=1, source_target_pairs={{0,4},{1,5},{2,6},{3,7},{4,0},{5,1},{6,2},{7,3},{8,12},{9,13},{10,... | collective-permute-start | bytes 1671176 | tf_op jit(solution)/shard_map/ppermute | solution.py:21
  85.1 16.1 %collective-permute-start.6 = (f32[2,17,32,128]{3,2,1,0:T(8,128)S(1)}, f32[2,17,32,128]{3,2,1,0:T(8,128)S(1)}, u32[]{:S(2)}, u32[]{:S(2)}) collective-permute-start(f32[2,17,32,128]{3,2,1,0:T(8,128)S(1)} %slice.47), channel_id=1, source_target_pairs={{0,12},{1,13},{2,14},{3,15},{4,8},{5,9},{6,10},{7,11},{8,4},{9,5},... | collective-permute-start | bytes 1671176 | tf_op jit(solution)/shard_map/ppermute | solution.py:21
  88.6 28.8 %collective-permute-start.23 = (f32[16,128,128]{2,1,0:T(8,128)S(1)}, f32[16,128,128]{2,1,0:T(8,128)S(1)}, u32[]{:S(2)}, u32[]{:S(2)}) collective-permute-start(f32[16,128,128]{2,1,0:T(8,128)S(1)} %get-tuple-element.16.refs_4_), channel_id=1, source_target_pairs={{0,1},{1,0},{2,3},{3,2},{4,5},{5,4},{6,7},{7,6},{8,9},{9,8},{10,11... | collective-permute-start | bytes 3145736 | tf_op jit(solution)/shard_map/ppermute | solution.py:21
  93.0 26.0 %collective-permute-start.29 = (f32[16,128,128]{2,1,0:T(8,128)}, f32[16,128,128]{2,1,0:T(8,128)S(1)}, u32[]{:S(2)}, u32[]{:S(2)}) collective-permute-start(f32[16,128,128]{2,1,0:T(8,128)} %collective-permute-done.26.refs_4_), channel_id=1, source_target_pairs={{0,1},{1,0},{2,3},{3,2},{4,5},{5,4},{6,7},{7,6},{8,9},{9,8},{10,11... | collective-permute-start | bytes 3145736 | tf_op jit(solution)/shard_map/ppermute | solution.py:21
  95.0 24.9 %collective-permute-start.30 = (f32[16,128,128]{2,1,0:T(8,128)S(1)}, f32[16,128,128]{2,1,0:T(8,128)S(1)}, u32[]{:S(2)}, u32[]{:S(2)}) collective-permute-start(f32[16,128,128]{2,1,0:T(8,128)S(1)} %copy-done.6), channel_id=1, source_target_pairs={{0,1},{1,0},{2,3},{3,2},{4,5},{5,4},{6,7},{7,6},{8,9},{9,8},{10,11... | collective-permute-start | bytes 3145736 | tf_op jit(solution)/shard_map/ppermute | solution.py:21
  100.0 13.6 %collective-permute-start.12 = (f32[2,16,32,128]{3,2,1,0:T(8,128)S(1)}, f32[2,16,32,128]{3,2,1,0:T(8,128)S(1)}, u32[]{:S(2)}, u32[]{:S(2)}) collective-permute-start(f32[2,16,32,128]{3,2,1,0:T(8,128)S(1)} %slice.49), channel_id=1, source_target_pairs={{0,16},{1,17},{2,18},{3,19},{4,20},{5,21},{6,22},{7,23},{8,24},{9,... | collective-permute-start | bytes 1572872 | tf_op jit(solution)/shard_map/ppermute | solution.py:21
  101.2 17.3 %collective-permute-start.13 = (f32[2,16,32,128]{3,2,1,0:T(8,128)S(1)}, f32[2,16,32,128]{3,2,1,0:T(8,128)S(1)}, u32[]{:S(2)}, u32[]{:S(2)}) collective-permute-start(f32[2,16,32,128]{3,2,1,0:T(8,128)S(1)} %slice.50), channel_id=1, source_target_pairs={{0,48},{1,49},{2,50},{3,51},{4,52},{5,53},{6,54},{7,55},{8,56},{9,... | collective-permute-start | bytes 1572872 | tf_op jit(solution)/shard_map/ppermute | solution.py:21
  113.6 37.2 %collective-permute-start.28 = (f32[16,128,128]{2,1,0:T(8,128)}, f32[16,128,128]{2,1,0:T(8,128)}, u32[]{:S(2)}, u32[]{:S(2)}) collective-permute-start(f32[16,128,128]{2,1,0:T(8,128)} %constant_dynamic-update-slice_fusion.17.refs_6_), channel_id=1, source_target_pairs={{0,1},{1,0},{2,3},{3,2},{4,5},{5,4},{6,7},{7,6},{8,9},{9,8},{10,11... | collective-permute-start | bytes 3145736 | tf_op jit(solution)/shard_map/ppermute | solution.py:21
  117.4 1.0 copy-start.10
  118.4 53.7 %collective-permute-start.20 = (f32[16,128,128]{2,1,0:T(8,128)S(1)}, f32[16,128,128]{2,1,0:T(8,128)}, u32[]{:S(2)}, u32[]{:S(2)}) collective-permute-start(f32[16,128,128]{2,1,0:T(8,128)S(1)} %collective-permute-done.17.refs_4_), channel_id=1, source_target_pairs={{0,1},{1,0},{2,3},{3,2},{4,5},{5,4},{6,7},{7,6},{8,9},{9,8},{10,11... | collective-permute-start | bytes 3145736 | tf_op jit(solution)/shard_map/ppermute | solution.py:21
  118.4 53.7 %collective-permute-start.21 = (f32[16,128,128]{2,1,0:T(8,128)}, f32[16,128,128]{2,1,0:T(8,128)}, u32[]{:S(2)}, u32[]{:S(2)}) collective-permute-start(f32[16,128,128]{2,1,0:T(8,128)} %collective-permute-done.15.refs_6_), channel_id=1, source_target_pairs={{0,1},{1,0},{2,3},{3,2},{4,5},{5,4},{6,7},{7,6},{8,9},{9,8},{10,11... | collective-permute-start | bytes 3145736 | tf_op jit(solution)/shard_map/ppermute | solution.py:21
  119.0 1.0 copy-start.12
  120.0 68.1 %collective-permute-start.14 = (f32[16,128,128]{2,1,0:T(8,128)S(1)}, f32[16,128,128]{2,1,0:T(8,128)}, u32[]{:S(2)}, u32[]{:S(2)}) collective-permute-start(f32[16,128,128]{2,1,0:T(8,128)S(1)} %get-tuple-element.17.refs_4_), channel_id=1, source_target_pairs={{0,1},{1,0},{2,3},{3,2},{4,5},{5,4},{6,7},{7,6},{8,9},{9,8},{10,11... | collective-permute-start | bytes 3145736 | tf_op jit(solution)/shard_map/ppermute | solution.py:21
  120.0 1.0 copy-start.14
  121.0 67.1 %collective-permute-start.19 = (f32[16,128,128]{2,1,0:T(8,128)}, f32[16,128,128]{2,1,0:T(8,128)}, u32[]{:S(2)}, u32[]{:S(2)}) collective-permute-start(f32[16,128,128]{2,1,0:T(8,128)} %constant_dynamic-update-slice_fusion.15.refs_6_), channel_id=1, source_target_pairs={{0,1},{1,0},{2,3},{3,2},{4,5},{5,4},{6,7},{7,6},{8,9},{9,8},{10,11... | collective-permute-start | bytes 3145736 | tf_op jit(solution)/shard_map/ppermute | solution.py:21
  122.4 14.8 %copy-start.7 = (f32[16,128,128]{2,1,0:T(8,128)S(1)}, f32[16,128,128]{2,1,0:T(8,128)}, u32[]{:S(2)}) copy-start(f32[16,128,128]{2,1,0:T(8,128)} %copy-done.5) | copy-start | bytes 3145732
  122.4 14.8 %copy-start.13 = (f32[16,128,128]{2,1,0:T(8,128)S(1)}, f32[16,128,128]{2,1,0:T(8,128)}, u32[]{:S(2)}) copy-start(f32[16,128,128]{2,1,0:T(8,128)} %copy-done.12) | copy-start | bytes 3145732
  122.4 14.8 %copy-start.15 = (f32[16,128,128]{2,1,0:T(8,128)S(1)}, f32[16,128,128]{2,1,0:T(8,128)}, u32[]{:S(2)}) copy-start(f32[16,128,128]{2,1,0:T(8,128)} %copy-done.14) | copy-start | bytes 3145732
  137.2 13.5 %copy-start.1 = (bf16[64,512,128]{2,1,0:T(8,128)(2,1)}, bf16[64,512,128]{2,1,0:T(8,128)(2,1)S(1)}, u32[]{:S(2)}) copy-start(bf16[64,512,128]{2,1,0:T(8,128)(2,1)S(1)} %get-tuple-element.10.refs_0_.refs_1_) | copy-start | bytes 25165828
  137.3 13.5 %copy-start.11 = (f32[16,128,128]{2,1,0:T(8,128)S(1)}, f32[16,128,128]{2,1,0:T(8,128)}, u32[]{:S(2)}) copy-start(f32[16,128,128]{2,1,0:T(8,128)} %copy-done.10) | copy-start | bytes 3145732
  150.8 3.4 %copy-start.2 = (bf16[64,512,128]{2,1,0:T(8,128)(2,1)S(1)}, bf16[64,512,128]{2,1,0:T(8,128)(2,1)}, u32[]{:S(2)}) copy-start(bf16[64,512,128]{2,1,0:T(8,128)(2,1)} %copy-done.1) | copy-start | bytes 25165828
  166.4 0.8 copy-start.9
  167.2 34.2 %all-to-all-start.1 = ((f32[32,32,128]{2,1,0:T(8,128)}), f32[32,32,128]{2,1,0:T(8,128)}, u32[]{:S(2)}, u32[]{:S(2)}) async-start(f32[32,32,128]{2,1,0:T(8,128)} %bitcast.59), calls=%async_computation.1 | async-start | bytes 1048576 | tf_op jit(solution)/shard_map/all_to_all | solution.py:241
  172.1 3.4 %copy-start.3 = (bf16[64,512,128]{2,1,0:T(8,128)(2,1)S(1)}, bf16[64,512,128]{2,1,0:T(8,128)(2,1)}, u32[]{:S(2)}) copy-start(bf16[64,512,128]{2,1,0:T(8,128)(2,1)} %copy-done.1) | copy-start | bytes 25165828
  188.0 35.5 %copy-start.17 = (s32[1,32]{1,0:T(1,128)S(1)}, s32[1,32]{1,0:T(1,128)}, u32[]{:S(2)}) copy-start(s32[1,32]{1,0:T(1,128)} %param.6) | copy-start | bytes 388
  188.0 36.7 %copy-start.4 = (f32[1,32,128,128]{3,2,1,0:T(8,128)S(1)}, f32[1,32,128,128]{3,2,1,0:T(8,128)}, u32[]{:S(2)}) copy-start(f32[1,32,128,128]{3,2,1,0:T(8,128)} %param.5) | copy-start | bytes 6291460
  200.6 0.8 copy-start.8
  201.4 17.9 %all-to-all-start = ((f32[32,32,128]{2,1,0:T(8,128)}), f32[32,32,128]{2,1,0:T(8,128)S(1)}, u32[]{:S(2)}, u32[]{:S(2)}) async-start(f32[32,32,128]{2,1,0:T(8,128)} %bitcast.58), calls=%async_computation | async-start | bytes 1048576 | tf_op jit(solution)/shard_map/all_to_all | solution.py:241
  210.2 13.5 %collective-permute-start.31 = (f32[2,8,32,128]{3,2,1,0:T(8,128)S(1)}, f32[2,8,32,128]{3,2,1,0:T(8,128)S(1)}, u32[]{:S(2)}, u32[]{:S(2)}) collective-permute-start(f32[2,8,32,128]{3,2,1,0:T(8,128)S(1)} %get-tuple-element.28), channel_id=1, source_target_pairs={{0,1},{1,0},{2,3},{3,2},{4,5},{5,4},{6,7},{7,6},{8,9},{9,8},{10,11... | collective-permute-start | bytes 786440 | tf_op jit(solution)/shard_map/ppermute | solution.py:21
  219.3 0.8 copy-start.16
  221.2 3.5 %collective-permute-start.22 = (f32[2,8,32,128]{3,2,1,0:T(8,128)S(1)}, f32[2,8,32,128]{3,2,1,0:T(8,128)S(1)}, u32[]{:S(2)}, u32[]{:S(2)}) collective-permute-start(f32[2,8,32,128]{3,2,1,0:T(8,128)S(1)} %get-tuple-element.30), channel_id=1, source_target_pairs={{0,1},{1,0},{2,3},{3,2},{4,5},{5,4},{6,7},{7,6},{8,9},{9,8},{10,11... | collective-permute-start | bytes 786440 | tf_op jit(solution)/shard_map/ppermute | solution.py:21

commit v2 on v0

v2 whole, which is shorter than its diff:
```python
import functools

import jax
import jax.numpy as jnp
from jax import lax
from jax.experimental import pallas as pl
from jax.experimental.pallas import tpu as pltpu
from jax.sharding import PartitionSpec as P

AXES = ("col", "row")
CORE = 1
X1, X3 = 2, 66
Y1, Y3 = 4, 12
Z1, Z3 = 16, 48
B = 128
Q = 32
F32, BF16 = jnp.float32, jnp.bfloat16
MANY = 4


def swap(x, even, odd=None):
    odd = even if odd is None else odd
    return lax.ppermute(x, AXES, [(i, i ^ (odd if i % 2 else even)) for i in range(128)])


def ring(x, one, three):
    first = swap(x, one, three)
    second = swap(x, three, one)
    return first, second, swap(second, one, three)


def split(x):
    hi = x.astype(BF16)
    return hi, (x - hi.astype(F32)).astype(BF16)


def dot(a, b):
    return jnp.dot(a, b, preferred_element_type=F32)


def dot3(a, b):
    (ah, al), (bh, bl) = split(a), split(b)
    return dot(ah, bh) + (dot(ah, bl) + dot(al, bh))


def cut_kernel(where, u_ref, label_ref, first_ref, second_ref, turned):
    half = u_ref.shape[0] // 2

    def step(k, carry):
        for i, out_ref in enumerate((first_ref, second_ref)):
            turned[i] = u_ref[i * half + k].T
            out_ref[k] = turned[i, pl.ds(pl.multiple_of(where[0] * Q, Q), Q), :]
        return carry

    lax.fori_loop(0, half, step, 0, unroll=4)
    for out_ref in (first_ref, second_ref):
        out_ref[half] = jnp.zeros_like(out_ref[half])
        out_ref[half, :, :32] = jnp.broadcast_to(label_ref[...].astype(F32), (Q, 32))


def cut(panel, labels, row):
    return pl.pallas_call(
        cut_kernel,
        grid_spec=pltpu.PrefetchScalarGridSpec(
            num_scalar_prefetch=1,
            grid=(1,),
            in_specs=[
                pl.BlockSpec((32, B, B), lambda i, w: (0, 0, 0)),
                pl.BlockSpec((1, 32), lambda i, w: (0, 0)),
            ],
            out_specs=[pl.BlockSpec((17, Q, B), lambda i, w: (0, 0, 0))] * 2,
            scratch_shapes=[pltpu.VMEM((2, B, B), F32)],
        ),
        out_shape=[jax.ShapeDtypeStruct((17, Q, B), F32)] * 2,
        name="cut",
    )(row[None], panel, labels)


ON_CHIP = pl.BlockSpec(memory_space=pltpu.VMEM)
SCALARS = pl.BlockSpec(memory_space=pltpu.SMEM)


def gained(weights, blocks, sides):
    tall = [
        jnp.concatenate([blocks[side][core][i, low] for side in range(sides) for low in range(2)], axis=1)
        for core in range(2)
        for i in range(MANY)
    ]
    high, low = split(jnp.concatenate(tall, axis=0))
    wh, wl = (jnp.concatenate(t, axis=1) for t in weights)
    return dot(wh, high) + (dot(wh, low) + dot(wl, high))


def first_kernel(nodes, where, *refs):
    parts, sigmas = refs[:8], refs[8:14]
    out_ref, hi_out, lo_out, hi_ref, lo_ref, held, total, labels, arrived, left, read = refs[14:]
    texts = [
        pltpu.make_async_copy(t.at[:, 16, pl.ds(0, 8)], labels.at[i], read.at[i]) for i, t in enumerate(parts)
    ]
    for copy in texts:
        copy.start()
    copies = [pltpu.make_async_copy(t, held.at[i], arrived.at[i]) for i, t in enumerate(sigmas)]
    for copy in copies:
        copy.start()

    def clear(b, carry):
        hi_ref[b] = jnp.zeros_like(hi_ref[b])
        lo_ref[b] = jnp.zeros_like(lo_ref[b])
        return carry

    lax.fori_loop(0, hi_ref.shape[0], clear, 0)
    for copy in texts:
        copy.wait()
    for i, part in enumerate(parts):
        def node(n, carry, i=i, part=part):
            rows = pl.ds(pl.multiple_of(nodes[i * 4 + n] * Q, Q), Q)
            for k in range(16):
                at = labels[i, n, 0, i // 4 * 16 + k].astype(jnp.int32)
                hi, lo = split(part[n, k])
                hi_ref[at, rows, :] = hi
                lo_ref[at, rows, :] = lo
            return carry

        lax.fori_loop(0, 4, node, 0)

    outward = [
        pltpu.make_async_copy(ref.at[pl.ds(where[2 + core], 16)], out.at[pl.ds(16 * core, 16)], left.at[2 * i + core])
        for i, (ref, out) in enumerate(((hi_ref, hi_out), (lo_ref, lo_out)))
        for core in range(2)
    ]
    for copy in outward:
        copy.start()
    for copy in copies:
        copy.wait()

    def run(first, sides, blocks):
        def step(t, carry):
            k = pl.multiple_of(t * MANY, MANY)
            weights = [
                [ref[where[first + core] + k + i] for core in range(2) for i in range(MANY)] for ref in (hi_ref, lo_ref)
            ]
            here = [[held.at[i, pl.ds(k, MANY)] for i in side] for side in blocks]
            total[:, : 2 * sides * B] += gained(weights, here, sides)
            return carry

        lax.fori_loop(0, 16 // MANY, step, 0)

    total[...] = jnp.zeros_like(total)
    run(0, 2, [(0, 1), (2, 3)])
    at = where[4]
    for n in range(4):
        out_ref[at ^ (n // 2), :, n % 2] = total[:, n * B : (n + 1) * B].reshape(16, Q, B)
    total[...] = jnp.zeros_like(total)
    run(2, 1, [(4, 5)])
    for n in range(2):
        out_ref[where[5], :, n] += total[:, n * B : (n + 1) * B].reshape(16, Q, B)
    for copy in outward:
        copy.wait()


def first_sums(nodes, where, parts, sigmas):
    whole = pl.BlockSpec(memory_space=pl.ANY)
    rows = 16 * Q
    return pl.pallas_call(
        first_kernel,
        in_specs=[SCALARS] * 2 + [ON_CHIP] * 8 + [whole] * 6,
        out_specs=[ON_CHIP, whole, whole],
        out_shape=[jax.ShapeDtypeStruct((2, 16, 2, Q, B), F32)] + [jax.ShapeDtypeStruct((32, rows, B), BF16)] * 2,
        scratch_shapes=[
            pltpu.VMEM((64, rows, B), BF16),
            pltpu.VMEM((64, rows, B), BF16),
            pltpu.VMEM((6, 16, 2, B, B), F32),
            pltpu.VMEM((rows, 4 * B), F32),
            pltpu.SMEM((8, 4, 8, B), F32),
            pltpu.SemaphoreType.DMA((6,)),
            pltpu.SemaphoreType.DMA((4,)),
            pltpu.SemaphoreType.DMA((8,)),
        ],
        compiler_params=pltpu.CompilerParams(vmem_limit_bytes=38 << 20),
        cost_estimate=pl.CostEstimate(flops=9 << 31, bytes_accessed=32 << 20, transcendentals=0),
        name="first_sums",
    )(nodes, where, *parts, *sigmas)


def last_kernel(where, hi0, hi1, lo0, lo1, far0, far1, start, out_ref, total):
    step, at = pl.program_id(0), where[0]

    @pl.when(step == 0)
    def _():
        for n in range(2):
            total[:, n * B : (n + 1) * B] = start[at, :, n].reshape(16 * Q, B)

    weights = [[t[i] for t in pair for i in range(MANY)] for pair in ((hi0, hi1), (lo0, lo1))]
    total[...] += gained(weights, [(far0, far1)], 1)

    @pl.when(step == pl.num_programs(0) - 1)
    def _():
        for n in range(2):
            out_ref[at, :, n] = total[:, n * B : (n + 1) * B].reshape(16, Q, B)
        out_ref[1 - at] = start[1 - at]


def last_sums(at, hi, lo, far, start):
    rows = 16 * Q
    w = [pl.BlockSpec((MANY, rows, B), lambda i, w, core=core: (core * (16 // MANY) + i, 0, 0)) for core in range(2)]
    s = pl.BlockSpec((MANY, 2, B, B), lambda i, w: (i, 0, 0, 0))
    whole = pl.BlockSpec(start.shape, lambda i, w: (0,) * 5)
    return pl.pallas_call(
        last_kernel,
        grid_spec=pltpu.PrefetchScalarGridSpec(
            num_scalar_prefetch=1,
            grid=(16 // MANY,),
            in_specs=w + w + [s, s, whole],
            out_specs=whole,
            scratch_shapes=[pltpu.VMEM((rows, 2 * B), F32)],
        ),
        out_shape=jax.ShapeDtypeStruct(start.shape, F32),
        compiler_params=pltpu.CompilerParams(vmem_limit_bytes=56 << 20),
        cost_estimate=pl.CostEstimate(flops=3 << 31, bytes_accessed=14 << 20, transcendentals=0),
        name="last_sums",
    )(at[None], hi, hi, lo, lo, *far, start)


def rows_of(core, a, kept, came):
    parts = []
    for x in range(2):
        k, c = kept[x, core, a // 2, a % 2], came[x, core, a // 2, a % 2]
        parts += [jnp.where(core == 0, k, c), jnp.where(core == 0, c, k)]
    return jnp.concatenate(parts, axis=0)


def share_kernel(where, picks, u_ref, kept, came, out_ref, total):
    total[...] = jnp.zeros_like(total)
    for a in range(16):
        pick = picks[a]

        @pl.when(pick >= 0)
        def _(a=a, pick=pick):
            total[...] += dot3(rows_of(where[0], a, kept, came), u_ref[jnp.maximum(pick, 0)])

    out_ref[...] = total[...].T


def panel_kernel(where, picks, kept, came, panel_ref):
    for a in range(16):
        panel_ref[a] = jnp.where(picks[a] >= 0, -rows_of(where[0], a, kept, came).T, 0.0)


def on_one(kernel, name, core, picks, arrays, shape, scratch=(), flops=0):
    full = lambda s: pl.BlockSpec(s, lambda i, w, p: (0,) * len(s))
    return pl.pallas_call(
        kernel,
        grid_spec=pltpu.PrefetchScalarGridSpec(
            num_scalar_prefetch=2,
            grid=(1,),
            in_specs=[full(t.shape) for t in arrays],
            out_specs=full(shape),
            scratch_shapes=scratch,
        ),
        out_shape=jax.ShapeDtypeStruct(shape, F32),
        compiler_params=pltpu.CompilerParams(vmem_limit_bytes=16 << 20),
        cost_estimate=pl.CostEstimate(flops=flops, bytes_accessed=4 << 20, transcendentals=0),
        name=name,
    )(core[None], picks, *arrays)


def after(x, *earlier):
    return lax.optimization_barrier((x, *earlier))[0]


def gather(sigma, first, second):
    sigma, first, second = lax.optimization_barrier((sigma, first, second))
    x1 = swap(sigma, X1, X3)
    a = jnp.stack([first, *ring(first, Z1, Z3)])
    b = jnp.stack([second, *ring(second, Y1, Y3)])
    sigma, x1, a, b = lax.optimization_barrier((sigma, x1, a, b))
    x2 = swap(sigma, X3, X1)
    a2, b2 = swap(a, Y3, Y1), swap(b, Z3, Z1)
    a1, b1 = swap(after(a, a2), Y1, Y3), swap(after(b, b2), Z1, Z3)
    a3, b3 = swap(a2, Y1, Y3), swap(b2, Z1, Z3)
    sigma_other, x1_other = swap(sigma, CORE), swap(x1, CORE)
    x3 = swap(after(x2, a2, b2, sigma_other, x1_other), X1, X3)
    sigmas = (x1, swap(x2, CORE), x2, x1_other, sigma, sigma_other)
    return sigmas, (x3, swap(x3, CORE)), (a, a1, a2, a3, b, b1, b2, b3)


def local(sigma_anc, panel_u, structure, diag_inv):
    col, row = lax.axis_index("col"), lax.axis_index("row")
    x_hi, z, y = col // 16, (col // 4) % 4, col % 4
    x_lo, core = row // 2, row % 2
    panel = panel_u[0]

    sigmas, far, pieces = gather(sigma_anc, *cut(panel, structure, row))

    away = jnp.stack([0 * core, 1 + 2 * core, 3 - 2 * core, 2 + 0 * core]).astype(jnp.int32)
    there_z, there_y = z ^ away, y ^ away
    nodes = jnp.stack([there_y[:, None] + there_z * 4, there_z[:, None] * 4 + there_y]).reshape(-1)
    entry = jnp.arange(32, dtype=jnp.int32)
    mine = jnp.sum(jnp.where(structure[0][:, None] == (16 * row + jnp.arange(16))[None, :], entry[:, None] + 1, 0), axis=0) - 1

    base = lambda x: [32 * x + 16 * core, 32 * x + 16 * (1 - core)]
    where = jnp.stack(base(1 - x_lo) + base(x_lo) + [x_hi ^ core, x_hi])
    part, hi, lo = first_sums(nodes, where, pieces, sigmas)
    part = last_sums(1 - x_hi, hi, lo, far, part)
    groups = [
        [h * 64 + q * 4 + l * 2 + c for l in range(2) for q in range(16)] for h in range(2) for c in range(2)
    ]
    moved = lax.all_to_all(part.reshape(32, 2, Q, B), AXES, 0, 0, axis_index_groups=groups, tiled=True)
    parts = [t.reshape(2, 2, 8, 2, Q, B) for t in (moved, swap(moved, CORE))]
    share = on_one(share_kernel, "share", core, mine, [panel, *parts], (B, B), [pltpu.VMEM((B, B), F32)], 1 << 27)

    square = jnp.einsum("zx,zy->xy", diag_inv[0], diag_inv[0], precision=lax.Precision.HIGHEST)
    others = [swap(share, mask) for mask in (CORE, X1, X1 + CORE)]
    panel_out = on_one(panel_kernel, "panel", core, mine, parts, (16, B, B))
    diag = square + share + (others[0] + (others[1] + others[2]))
    return panel_out[None], diag[None]


def solution(mesh):
    return jax.shard_map(
        local,
        mesh=mesh,
        in_specs=(P("row", "col", None, None), P("col", None, None, None), P("col", None), P("col", None, None)),
        out_specs=(P("col", "row", None, None), P("col", None, None)),
        check_vma=False,
    )
```

time: 527 us -> 163 us (0.31)
  waiting for transfers between devices: 391 us -> 46.8 us
  starting transfers between devices: 0.08 us -> 47.7 us
  matrix products: 42.4 us -> 0.92 us
  blocking collectives: 61.2 us -> 20.9 us
  Pallas kernels: 0 us -> 36.2 us
  between operations: 14.1 us -> 0.72 us
  local copies, waits for them, and re-layouts: 13.8 us -> 7.65 us
    reduce_scatter x1 -> x0, waiting for transfers between devices: 364 us -> none  [local(): lax.psum_scatter(jnp.einsum('abxz,bjzy->jaxy', sigma_anc, moved, precisio...]
    ppermute x0 -> x23, starting transfers between devices: none -> 47.7 us  [swap(): lax.ppermute(x, AXES, [(i, i ^ (odd if i % 2 else even)) for i in range(1...]
    ppermute x0 -> x23, waiting for transfers between devices: none -> 46.8 us  [swap(): lax.ppermute(x, AXES, [(i, i ^ (odd if i % 2 else even)) for i in range(1...]
    dot_general x4 -> x1, matrix products: 42.4 us -> 0.92 us  [local(): jnp.einsum('zx,zy->xy', diag_inv[0], diag_inv[0], precision=lax.Precision...]
    all_to_all x1, blocking collectives: 61.2 us -> 20.9 us  [local(): lax.all_to_all(part.reshape(32, 2, Q, B), AXES, 0, 0, axis_index_groups=g...]
    pallas_call x0 -> x5, Pallas kernels: none -> 36.2 us  [the longest x1 18.4 us: first_sums(): pl.pallas_call(first_kernel, in_specs=[SCALARS] * 2 + [ON_CHIP] * 8 + [wh...]
    psum x1 -> x0, waiting for transfers between devices: 27.1 us -> none  [local(): update = lax.psum(share, 'row')]
    all_to_all x1 -> x0, local copies, waits for them, and re-layouts: 5.61 us -> none  [local(): lax.all_to_all(dense, 'col', split_axis=0, concat_axis=1, tiled=True)]
  transfers between devices with their start and end apart: 2 -> 23, of which waited for: 2 -> 13; matrix products, arithmetic and copies ran while one was open for 1% -> 1% of each run, Pallas kernels for 0% -> 13%
where the time goes in v2:
time: 163 us; the launch traced here: 162 us
  starting transfers between devices  47.7 us (29%)
  waiting for transfers between devices  46.8 us (29%)
  Pallas kernels  36.2 us (22%)
  blocking collectives  20.9 us (13%)
  local copies, waits for them, and re-layouts  7.65 us (5%)
    ppermute x23, starting transfers between devices, swap(): lax.ppermute(x, AXES, [(i, i ^ (odd if i % 2 else even)) for i in range(1...  47.7 us
    ppermute x23, waiting for transfers between devices, swap(): lax.ppermute(x, AXES, [(i, i ^ (odd if i % 2 else even)) for i in range(1...  46.8 us
    all_to_all x1, blocking collectives, local(): lax.all_to_all(part.reshape(32, 2, Q, B), AXES, 0, 0, axis_index_groups=g...  20.9 us
    pallas_call x1, Pallas kernels, first_sums(): pl.pallas_call(first_kernel, in_specs=[SCALARS] * 2 + [ON_CHIP] * 8 + [wh...  18.4 us
    pallas_call x1, Pallas kernels, last_sums(): pl.pallas_call(last_kernel, grid_spec=pltpu.PrefetchScalarGridSpec(num_sc...  8.63 us
    unnamed x22, local copies, waits for them, and re-layouts  7.48 us
    pallas_call x2, Pallas kernels, on_one(): pl.pallas_call(kernel, grid_spec=pltpu.PrefetchScalarGridSpec(num_scalar_...  5.88 us
    pallas_call x1, Pallas kernels, cut(): pl.pallas_call(cut_kernel, grid_spec=pltpu.PrefetchScalarGridSpec(num_sca...  3.26 us
  transfers between devices with their start and end apart: 23, of which 13 were waited for; matrix products, arithmetic and copies ran while one was open for 1% of the time, Pallas kernels for 13%

profile of v2, /device:TPU:1, one launch (start us, length us, event | category | flops | bytes accessed | tf_op | source)
XLA Modules:
  0.0 162.4 jit_solution(2408024693067586502)
XLA Ops:
  0.6 0.0 copy-start
  0.6 3.3 %cut.1 = (f32[17,32,128]{2,1,0:T(8,128)}, f32[17,32,128]{2,1,0:T(8,128)}) custom-call(s32[1]{0:T(128)} %bitcast.11.where, f32[32,128,128]{2,1,0:T(8,128)} %bitcast.32, s32[1,32]{1,0:T(1,128)} %label_ref.1), custom_call_target="tpu_custom_call" | custom-call | tf_op jit(solution)/shard_map/cut/pallas_call | solution.py:62
  3.9 3.4 %collective-permute-start = (f32[16,2,128,128]{3,2,1,0:T(8,128)}, f32[16,2,128,128]{3,2,1,0:T(8,128)S(1)}, u32[]{:S(2)}, u32[]{:S(2)}) collective-permute-start(f32[16,2,128,128]{3,2,1,0:T(8,128)} %refs_12_), channel_id=1, source_target_pairs={{0,2},{1,67},{2,0},{3,65},{4,6},{5,71},{6,4},{7,69},{8,10},{9,75},... | collective-permute-start | bytes 6291464 | tf_op jit(solution)/shard_map/ppermute | solution.py:23
  7.3 1.6 %collective-permute-start.2 = (f32[17,32,128]{2,1,0:T(8,128)}, f32[17,32,128]{2,1,0:T(8,128)S(1)}, u32[]{:S(2)}, u32[]{:S(2)}) collective-permute-start(f32[17,32,128]{2,1,0:T(8,128)} %get-tuple-element.20), channel_id=1, source_target_pairs={{0,48},{1,17},{2,50},{3,19},{4,52},{5,21},{6,54},{7,23},{8,56},{9,... | collective-permute-start | bytes 835592 | tf_op jit(solution)/shard_map/ppermute | solution.py:23
  8.9 1.3 collective-permute-start.5
  10.2 2.2 %collective-permute-start.1 = (f32[17,32,128]{2,1,0:T(8,128)}, f32[17,32,128]{2,1,0:T(8,128)S(1)}, u32[]{:S(2)}, u32[]{:S(2)}) collective-permute-start(f32[17,32,128]{2,1,0:T(8,128)} %get-tuple-element.20), channel_id=1, source_target_pairs={{0,16},{1,49},{2,18},{3,51},{4,20},{5,53},{6,22},{7,55},{8,24},{9,... | collective-permute-start | bytes 835592 | tf_op jit(solution)/shard_map/ppermute | solution.py:23
  12.4 0.9 collective-permute-done.2
  13.3 3.6 %collective-permute-start.3 = (f32[17,32,128]{2,1,0:T(8,128)S(1)}, f32[17,32,128]{2,1,0:T(8,128)S(1)}, u32[]{:S(2)}, u32[]{:S(2)}) collective-permute-start(f32[17,32,128]{2,1,0:T(8,128)S(1)} %collective-permute-done.2), channel_id=1, source_target_pairs={{0,16},{1,49},{2,18},{3,51},{4,20},{5,53},{6,22},{7,55},{8,24},{9,... | collective-permute-start | bytes 835592 | tf_op jit(solution)/shard_map/ppermute | solution.py:23
  16.9 5.4 %collective-permute-start.4 = (f32[17,32,128]{2,1,0:T(8,128)}, f32[17,32,128]{2,1,0:T(8,128)S(1)}, u32[]{:S(2)}, u32[]{:S(2)}) collective-permute-start(f32[17,32,128]{2,1,0:T(8,128)} %get-tuple-element.21), channel_id=1, source_target_pairs={{0,4},{1,13},{2,6},{3,15},{4,0},{5,9},{6,2},{7,11},{8,12},{9,5},{1... | collective-permute-start | bytes 835592 | tf_op jit(solution)/shard_map/ppermute | solution.py:23
  22.3 0.0 collective-permute-done.5
  22.3 0.0 collective-permute-start.6
  22.4 0.0 collective-permute-done.1
  22.4 0.0 collective-permute-done.3
  22.4 1.1 pad_maximum_fusion.refs_0_
  23.4 3.0 %collective-permute-done.4 = f32[17,32,128]{2,1,0:T(8,128)S(1)} collective-permute-done((f32[17,32,128]{2,1,0:T(8,128)}, f32[17,32,128]{2,1,0:T(8,128)S(1)}, u32[]{:S(2)}, u32[]{:S(2)}) %collective-permute-start.4) | collective-permute-done | bytes 278560 | tf_op jit(solution)/shard_map/ppermute | solution.py:23
  26.5 3.0 %collective-permute-done.6 = f32[17,32,128]{2,1,0:T(8,128)S(1)} collective-permute-done((f32[17,32,128]{2,1,0:T(8,128)S(1)}, f32[17,32,128]{2,1,0:T(8,128)S(1)}, u32[]{:S(2)}, u32[]{:S(2)}) %collective-permute-start.6) | collective-permute-done | bytes 278560 | tf_op jit(solution)/shard_map/ppermute | solution.py:23
  29.5 0.1 pad_maximum_fusion.1.refs_4_
  29.5 1.4 collective-permute-done.refs_8_
  30.9 0.5 collective-permute-start.13
  31.4 3.0 %collective-permute-start.15 = (f32[16,2,128,128]{3,2,1,0:T(8,128)S(1)}, f32[16,2,128,128]{3,2,1,0:T(8,128)S(1)}, u32[]{:S(2)}, u32[]{:S(2)}) collective-permute-start(f32[16,2,128,128]{3,2,1,0:T(8,128)S(1)} %collective-permute-done.refs_8_), channel_id=1, source_target_pairs={{0,1},{1,0},{2,3},{3,2},{4,5},{5,4},{6,7},{7,6},{8,9},{9,8},{10,11... | collective-permute-start | bytes 6291464 | tf_op jit(solution)/shard_map/ppermute | solution.py:23
  34.4 1.3 copy-done.2
  35.8 0.0 collective-permute-start.16
  35.8 1.3 collective-permute-start.7
  37.1 1.6 %collective-permute-start.10 = (f32[4,17,32,128]{3,2,1,0:T(8,128)S(1)}, f32[4,17,32,128]{3,2,1,0:T(8,128)}, u32[]{:S(2)}, u32[]{:S(2)}) collective-permute-start(f32[4,17,32,128]{3,2,1,0:T(8,128)S(1)} %pad_maximum_fusion.1.refs_4_), channel_id=1, source_target_pairs={{0,48},{1,17},{2,50},{3,19},{4,52},{5,21},{6,54},{7,23},{8,56},{9,... | collective-permute-start | bytes 3342344 | tf_op jit(solution)/shard_map/ppermute | solution.py:23
  38.7 11.8 %collective-permute-done.7.refs_2_ = f32[4,17,32,128]{3,2,1,0:T(8,128)S(1)} collective-permute-done((f32[4,17,32,128]{3,2,1,0:T(8,128)S(1)}, f32[4,17,32,128]{3,2,1,0:T(8,128)S(1)}, u32[]{:S(2)}, u32[]{:S(2)}) %collective-permute-start.7) | collective-permute-done | bytes 1114144 | tf_op jit(solution)/shard_map/ppermute | solution.py:23
  50.5 1.5 collective-permute-done.10.refs_6_
  52.0 4.4 %collective-permute-done.13.refs_10_ = f32[16,2,128,128]{3,2,1,0:T(8,128)} collective-permute-done((f32[16,2,128,128]{3,2,1,0:T(8,128)}, f32[16,2,128,128]{3,2,1,0:T(8,128)}, u32[]{:S(2)}, u32[]{:S(2)}) %collective-permute-start.13) | collective-permute-done | bytes 2097184 | tf_op jit(solution)/shard_map/ppermute | solution.py:23
  56.4 0.0 collective-permute-done.15.refs_11_
  56.4 0.0 collective-permute-done.16.refs_13_
  56.4 1.3 copy-done.9
  57.7 2.7 %collective-permute-start.17 = (f32[16,2,128,128]{3,2,1,0:T(8,128)}, f32[16,2,128,128]{3,2,1,0:T(8,128)}, u32[]{:S(2)}, u32[]{:S(2)}) collective-permute-start(f32[16,2,128,128]{3,2,1,0:T(8,128)} %collective-permute-done.13.refs_10_), channel_id=1, source_target_pairs={{0,2},{1,67},{2,0},{3,65},{4,6},{5,71},{6,4},{7,69},{8,10},{9,75},... | collective-permute-start | bytes 6291464 | tf_op jit(solution)/shard_map/ppermute | solution.py:23
  60.4 2.7 %collective-permute-start.8 = (f32[4,17,32,128]{3,2,1,0:T(8,128)S(1)}, f32[4,17,32,128]{3,2,1,0:T(8,128)S(1)}, u32[]{:S(2)}, u32[]{:S(2)}) collective-permute-start(f32[4,17,32,128]{3,2,1,0:T(8,128)S(1)} %pad_maximum_fusion.refs_0_), channel_id=1, source_target_pairs={{0,4},{1,13},{2,6},{3,15},{4,0},{5,9},{6,2},{7,11},{8,12},{9,5},{1... | collective-permute-start | bytes 3342344 | tf_op jit(solution)/shard_map/ppermute | solution.py:23
  63.1 0.0 collective-permute-start.14
  63.1 3.8 %collective-permute-start.11 = (f32[4,17,32,128]{3,2,1,0:T(8,128)S(1)}, f32[4,17,32,128]{3,2,1,0:T(8,128)}, u32[]{:S(2)}, u32[]{:S(2)}) collective-permute-start(f32[4,17,32,128]{3,2,1,0:T(8,128)S(1)} %pad_maximum_fusion.1.refs_4_), channel_id=1, source_target_pairs={{0,16},{1,49},{2,18},{3,51},{4,20},{5,53},{6,22},{7,55},{8,24},{9,... | collective-permute-start | bytes 3342344 | tf_op jit(solution)/shard_map/ppermute | solution.py:23
  66.9 1.2 collective-permute-start.9
  68.1 7.9 %collective-permute-done.8.refs_1_ = f32[4,17,32,128]{3,2,1,0:T(8,128)S(1)} collective-permute-done((f32[4,17,32,128]{3,2,1,0:T(8,128)S(1)}, f32[4,17,32,128]{3,2,1,0:T(8,128)S(1)}, u32[]{:S(2)}, u32[]{:S(2)}) %collective-permute-start.8) | collective-permute-done | bytes 1114144 | tf_op jit(solution)/shard_map/ppermute | solution.py:23
  76.0 1.0 copy-done.4
  77.0 3.8 %collective-permute-start.12 = (f32[4,17,32,128]{3,2,1,0:T(8,128)}, f32[4,17,32,128]{3,2,1,0:T(8,128)}, u32[]{:S(2)}, u32[]{:S(2)}) collective-permute-start(f32[4,17,32,128]{3,2,1,0:T(8,128)} %collective-permute-done.10.refs_6_), channel_id=1, source_target_pairs={{0,16},{1,49},{2,18},{3,51},{4,20},{5,53},{6,22},{7,55},{8,24},{9,... | collective-permute-start | bytes 3342344 | tf_op jit(solution)/shard_map/ppermute | solution.py:23
  80.8 0.1 xor_multiply_fusion
  80.9 3.3 %collective-permute-done.17.far0 = f32[16,2,128,128]{3,2,1,0:T(8,128)} collective-permute-done((f32[16,2,128,128]{3,2,1,0:T(8,128)}, f32[16,2,128,128]{3,2,1,0:T(8,128)}, u32[]{:S(2)}, u32[]{:S(2)}) %collective-permute-start.17) | collective-permute-done | bytes 2097184 | tf_op jit(solution)/shard_map/ppermute | solution.py:23
  84.1 2.7 %collective-permute-start.18 = (f32[16,2,128,128]{3,2,1,0:T(8,128)}, f32[16,2,128,128]{3,2,1,0:T(8,128)}, u32[]{:S(2)}, u32[]{:S(2)}) collective-permute-start(f32[16,2,128,128]{3,2,1,0:T(8,128)} %collective-permute-done.17.far0), channel_id=1, source_target_pairs={{0,1},{1,0},{2,3},{3,2},{4,5},{5,4},{6,7},{7,6},{8,9},{9,8},{10,11... | collective-permute-start | bytes 6291464 | tf_op jit(solution)/shard_map/ppermute | solution.py:23
  86.8 0.1 broadcast_add_fusion.1
  86.9 0.1 reshape.231.nodes
  87.0 0.1 stack.75.where
  87.0 1.0 collective-permute-done.9.refs_3_
  88.0 0.0 collective-permute-done.11.refs_5_
  88.0 5.9 %collective-permute-done.12.refs_7_ = f32[4,17,32,128]{3,2,1,0:T(8,128)} collective-permute-done((f32[4,17,32,128]{3,2,1,0:T(8,128)}, f32[4,17,32,128]{3,2,1,0:T(8,128)}, u32[]{:S(2)}, u32[]{:S(2)}) %collective-permute-start.12) | collective-permute-done | bytes 1114144 | tf_op jit(solution)/shard_map/ppermute | solution.py:23
  94.0 1.6 copy-done.3
  95.6 1.2 copy-done.5
  96.8 18.4 %first_sums.1 = (f32[2,16,2,32,128]{4,3,2,1,0:T(8,128)S(1)}, bf16[32,512,128]{2,1,0:T(8,128)(2,1)}, bf16[32,512,128]{2,1,0:T(8,128)(2,1)}) custom-call(s32[32]{0:T(128)S(1)} %reshape.231.nodes, s32[6]{0:T(128)S(1)} %stack.75.where, f32[4,17,32,128]{3,2,1,0:T(8,128)S(1)} %pad_maximum_fusion.refs_0_, f32[4,17,32,128]{3,2,1,0:T(8,128)S(1)} %copy-done.5, ...), custom_call_target="tpu_custom_call" | custom-call | flops 19327352832 | bytes 33554432 | tf_op jit(solution)/shard_map/first_sums/pallas_call | solution.py:164
  115.2 0.0 copy-start.6
  115.2 1.0 copy-done.6
  116.2 8.6 %last_sums.1 = f32[2,16,2,32,128]{4,3,2,1,0:T(8,128)} custom-call(s32[1]{0:T(128)} %bitcast.2.where, bf16[32,512,128]{2,1,0:T(8,128)(2,1)} %get-tuple-element.28.hi0.hi1, bf16[32,512,128]{2,1,0:T(8,128)(2,1)} %get-tuple-element.28.hi0.hi1, bf16[32,512,128]{2,1,0:T(8,128)(2,1)} %get-tuple-element.29.lo0.lo1, bf16[32,512,128]{2,1,0:T(8,128)(2,1)} %get-tuple-element.29.lo0.lo1, ...), custom_call_target="tpu_custom_call" | custom-call | flops 6442450944 | bytes 14680064 | tf_op jit(solution)/shard_map/last_sums/pallas_call | solution.py:208
  124.8 20.9 %all_to_all.5 = f32[32,2,32,128]{3,2,1,0:T(8,128)S(1)} all-to-all(f32[32,2,32,128]{3,2,1,0:T(8,128)} %bitcast.35), channel_id=1, replica_groups={{0,4,8,12,16,20,24,28,32,36,40,44,48,52,56,60,2,6,10,14,18,22,26,30,34,..., dimensions={0} | all-to-all | bytes 2097152 | tf_op jit(solution)/shard_map/all_to_all | solution.py:308
  145.7 3.8 %collective-permute-start.19 = (f32[32,2,32,128]{3,2,1,0:T(8,128)S(1)}, f32[32,2,32,128]{3,2,1,0:T(8,128)}, u32[]{:S(2)}, u32[]{:S(2)}) collective-permute-start(f32[32,2,32,128]{3,2,1,0:T(8,128)S(1)} %all_to_all.5), channel_id=1, source_target_pairs={{0,1},{1,0},{2,3},{3,2},{4,5},{5,4},{6,7},{7,6},{8,9},{9,8},{10,11... | collective-permute-start | bytes 3145736 | tf_op jit(solution)/shard_map/ppermute | solution.py:23
  149.5 0.2 select_reduce_fusion
  149.7 2.2 %collective-permute-done.19 = f32[32,2,32,128]{3,2,1,0:T(8,128)} collective-permute-done((f32[32,2,32,128]{3,2,1,0:T(8,128)S(1)}, f32[32,2,32,128]{3,2,1,0:T(8,128)}, u32[]{:S(2)}, u32[]{:S(2)}) %collective-permute-start.19) | collective-permute-done | bytes 1048608 | tf_op jit(solution)/shard_map/ppermute | solution.py:23
  151.9 2.8 %share.1 = f32[128,128]{1,0:T(8,128)S(1)} custom-call(s32[1]{0:T(128)} %bitcast.where, s32[16]{0:T(128)S(1)} %broadcast_add_fusion.2.picks, f32[32,128,128]{2,1,0:T(8,128)S(1)} %bitcast.33, f32[2,2,8,2,32,128]{5,4,3,2,1,0:T(8,128)S(1)} %bitcast.30, f32[2,2,8,2,32,128]{5,4,3,2,1,0:T(8,128)} %bitcast.23.came), custom_call_target="tpu_custom_call" | custom-call | flops 134217728 | bytes 4194304 | tf_op jit(solution)/shard_map/share/pallas_call | solution.py:251
  154.7 1.5 collective-permute-start.20
  156.2 0.4 collective-permute-start.21
  156.6 1.4 collective-permute-start.22
  157.9 3.1 %panel.1 = f32[16,128,128]{2,1,0:T(8,128)} custom-call(s32[1]{0:T(128)} %bitcast.where, s32[16]{0:T(128)S(1)} %broadcast_add_fusion.2.picks, f32[2,2,8,2,32,128]{5,4,3,2,1,0:T(8,128)S(1)} %bitcast.31, f32[2,2,8,2,32,128]{5,4,3,2,1,0:T(8,128)} %bitcast.23.came), custom_call_target="tpu_custom_call" | custom-call | bytes 4194304 | tf_op jit(solution)/shard_map/panel/pallas_call | solution.py:251
  161.0 0.4 collective-permute-done.22
  161.4 0.9 fusion.1
  (23 shorter events, 0.1 us)
Async XLA Ops:
  0.6 160.8 %copy-start = (f32[1,128,128]{2,1,0:T(8,128)S(1)}, f32[1,128,128]{2,1,0:T(8,128)}, u32[]{:S(2)}) copy-start(f32[1,128,128]{2,1,0:T(8,128)} %param.7) | copy-start | bytes 196612
  3.9 27.0 %collective-permute-start = (f32[16,2,128,128]{3,2,1,0:T(8,128)}, f32[16,2,128,128]{3,2,1,0:T(8,128)S(1)}, u32[]{:S(2)}, u32[]{:S(2)}) collective-permute-start(f32[16,2,128,128]{3,2,1,0:T(8,128)} %refs_12_), channel_id=1, source_target_pairs={{0,2},{1,67},{2,0},{3,65},{4,6},{5,71},{6,4},{7,69},{8,10},{9,75},... | collective-permute-start | bytes 6291464 | tf_op jit(solution)/shard_map/ppermute | solution.py:23
  7.3 6.1 %collective-permute-start.2 = (f32[17,32,128]{2,1,0:T(8,128)}, f32[17,32,128]{2,1,0:T(8,128)S(1)}, u32[]{:S(2)}, u32[]{:S(2)}) collective-permute-start(f32[17,32,128]{2,1,0:T(8,128)} %get-tuple-element.20), channel_id=1, source_target_pairs={{0,48},{1,17},{2,50},{3,19},{4,52},{5,21},{6,54},{7,23},{8,56},{9,... | collective-permute-start | bytes 835592 | tf_op jit(solution)/shard_map/ppermute | solution.py:23
  8.9 13.4 %collective-permute-start.5 = (f32[17,32,128]{2,1,0:T(8,128)}, f32[17,32,128]{2,1,0:T(8,128)S(1)}, u32[]{:S(2)}, u32[]{:S(2)}) collective-permute-start(f32[17,32,128]{2,1,0:T(8,128)} %get-tuple-element.21), channel_id=1, source_target_pairs={{0,12},{1,5},{2,14},{3,7},{4,8},{5,1},{6,10},{7,3},{8,4},{9,13},{1... | collective-permute-start | bytes 835592 | tf_op jit(solution)/shard_map/ppermute | solution.py:23
  10.2 12.2 %collective-permute-start.1 = (f32[17,32,128]{2,1,0:T(8,128)}, f32[17,32,128]{2,1,0:T(8,128)S(1)}, u32[]{:S(2)}, u32[]{:S(2)}) collective-permute-start(f32[17,32,128]{2,1,0:T(8,128)} %get-tuple-element.20), channel_id=1, source_target_pairs={{0,16},{1,49},{2,18},{3,51},{4,20},{5,53},{6,22},{7,55},{8,24},{9,... | collective-permute-start | bytes 835592 | tf_op jit(solution)/shard_map/ppermute | solution.py:23
  13.3 9.0 %collective-permute-start.3 = (f32[17,32,128]{2,1,0:T(8,128)S(1)}, f32[17,32,128]{2,1,0:T(8,128)S(1)}, u32[]{:S(2)}, u32[]{:S(2)}) collective-permute-start(f32[17,32,128]{2,1,0:T(8,128)S(1)} %collective-permute-done.2), channel_id=1, source_target_pairs={{0,16},{1,49},{2,18},{3,51},{4,20},{5,53},{6,22},{7,55},{8,24},{9,... | collective-permute-start | bytes 835592 | tf_op jit(solution)/shard_map/ppermute | solution.py:23
  16.9 9.5 %collective-permute-start.4 = (f32[17,32,128]{2,1,0:T(8,128)}, f32[17,32,128]{2,1,0:T(8,128)S(1)}, u32[]{:S(2)}, u32[]{:S(2)}) collective-permute-start(f32[17,32,128]{2,1,0:T(8,128)} %get-tuple-element.21), channel_id=1, source_target_pairs={{0,4},{1,13},{2,6},{3,15},{4,0},{5,9},{6,2},{7,11},{8,12},{9,5},{1... | collective-permute-start | bytes 835592 | tf_op jit(solution)/shard_map/ppermute | solution.py:23
  22.3 7.1 %collective-permute-start.6 = (f32[17,32,128]{2,1,0:T(8,128)S(1)}, f32[17,32,128]{2,1,0:T(8,128)S(1)}, u32[]{:S(2)}, u32[]{:S(2)}) collective-permute-start(f32[17,32,128]{2,1,0:T(8,128)S(1)} %collective-permute-done.5), channel_id=1, source_target_pairs={{0,4},{1,13},{2,6},{3,15},{4,0},{5,9},{6,2},{7,11},{8,12},{9,5},{1... | collective-permute-start | bytes 835592 | tf_op jit(solution)/shard_map/ppermute | solution.py:23
  22.4 7.1 %copy-start.7 = (f32[17,32,128]{2,1,0:T(8,128)S(1)}, f32[17,32,128]{2,1,0:T(8,128)}, u32[]{:S(2)}) copy-start(f32[17,32,128]{2,1,0:T(8,128)} %get-tuple-element.21) | copy-start | bytes 835588
  30.9 25.5 %collective-permute-start.13 = (f32[16,2,128,128]{3,2,1,0:T(8,128)}, f32[16,2,128,128]{3,2,1,0:T(8,128)}, u32[]{:S(2)}, u32[]{:S(2)}) collective-permute-start(f32[16,2,128,128]{3,2,1,0:T(8,128)} %refs_12_), channel_id=1, source_target_pairs={{0,66},{1,3},{2,64},{3,1},{4,70},{5,7},{6,68},{7,5},{8,74},{9,11},... | collective-permute-start | bytes 6291464 | tf_op jit(solution)/shard_map/ppermute | solution.py:23
  31.4 25.0 %collective-permute-start.15 = (f32[16,2,128,128]{3,2,1,0:T(8,128)S(1)}, f32[16,2,128,128]{3,2,1,0:T(8,128)S(1)}, u32[]{:S(2)}, u32[]{:S(2)}) collective-permute-start(f32[16,2,128,128]{3,2,1,0:T(8,128)S(1)} %collective-permute-done.refs_8_), channel_id=1, source_target_pairs={{0,1},{1,0},{2,3},{3,2},{4,5},{5,4},{6,7},{7,6},{8,9},{9,8},{10,11... | collective-permute-start | bytes 6291464 | tf_op jit(solution)/shard_map/ppermute | solution.py:23
  34.4 1.3 copy-start.2
  35.8 20.6 %collective-permute-start.16 = (f32[16,2,128,128]{3,2,1,0:T(8,128)}, f32[16,2,128,128]{3,2,1,0:T(8,128)S(1)}, u32[]{:S(2)}, u32[]{:S(2)}) collective-permute-start(f32[16,2,128,128]{3,2,1,0:T(8,128)} %refs_12_), channel_id=1, source_target_pairs={{0,1},{1,0},{2,3},{3,2},{4,5},{5,4},{6,7},{7,6},{8,9},{9,8},{10,11... | collective-permute-start | bytes 6291464 | tf_op jit(solution)/shard_map/ppermute | solution.py:23
  35.8 14.8 %collective-permute-start.7 = (f32[4,17,32,128]{3,2,1,0:T(8,128)S(1)}, f32[4,17,32,128]{3,2,1,0:T(8,128)S(1)}, u32[]{:S(2)}, u32[]{:S(2)}) collective-permute-start(f32[4,17,32,128]{3,2,1,0:T(8,128)S(1)} %pad_maximum_fusion.refs_0_), channel_id=1, source_target_pairs={{0,12},{1,5},{2,14},{3,7},{4,8},{5,1},{6,10},{7,3},{8,4},{9,13},{1... | collective-permute-start | bytes 3342344 | tf_op jit(solution)/shard_map/ppermute | solution.py:23
  37.1 14.9 %collective-permute-start.10 = (f32[4,17,32,128]{3,2,1,0:T(8,128)S(1)}, f32[4,17,32,128]{3,2,1,0:T(8,128)}, u32[]{:S(2)}, u32[]{:S(2)}) collective-permute-start(f32[4,17,32,128]{3,2,1,0:T(8,128)S(1)} %pad_maximum_fusion.1.refs_4_), channel_id=1, source_target_pairs={{0,48},{1,17},{2,50},{3,19},{4,52},{5,21},{6,54},{7,23},{8,56},{9,... | collective-permute-start | bytes 3342344 | tf_op jit(solution)/shard_map/ppermute | solution.py:23
  56.4 1.3 copy-start.9
  57.7 18.3 %copy-start.10 = (f32[16,2,128,128]{3,2,1,0:T(8,128)}, f32[16,2,128,128]{3,2,1,0:T(8,128)S(1)}, u32[]{:S(2)}) copy-start(f32[16,2,128,128]{3,2,1,0:T(8,128)S(1)} %collective-permute-done.16.refs_13_) | copy-start | bytes 6291460
  57.7 26.4 %collective-permute-start.17 = (f32[16,2,128,128]{3,2,1,0:T(8,128)}, f32[16,2,128,128]{3,2,1,0:T(8,128)}, u32[]{:S(2)}, u32[]{:S(2)}) collective-permute-start(f32[16,2,128,128]{3,2,1,0:T(8,128)} %collective-permute-done.13.refs_10_), channel_id=1, source_target_pairs={{0,2},{1,67},{2,0},{3,65},{4,6},{5,71},{6,4},{7,69},{8,10},{9,75},... | collective-permute-start | bytes 6291464 | tf_op jit(solution)/shard_map/ppermute | solution.py:23
  60.4 15.6 %collective-permute-start.8 = (f32[4,17,32,128]{3,2,1,0:T(8,128)S(1)}, f32[4,17,32,128]{3,2,1,0:T(8,128)S(1)}, u32[]{:S(2)}, u32[]{:S(2)}) collective-permute-start(f32[4,17,32,128]{3,2,1,0:T(8,128)S(1)} %pad_maximum_fusion.refs_0_), channel_id=1, source_target_pairs={{0,4},{1,13},{2,6},{3,15},{4,0},{5,9},{6,2},{7,11},{8,12},{9,5},{1... | collective-permute-start | bytes 3342344 | tf_op jit(solution)/shard_map/ppermute | solution.py:23
  63.1 30.9 %collective-permute-start.14 = (f32[16,2,128,128]{3,2,1,0:T(8,128)}, f32[16,2,128,128]{3,2,1,0:T(8,128)}, u32[]{:S(2)}, u32[]{:S(2)}) collective-permute-start(f32[16,2,128,128]{3,2,1,0:T(8,128)} %collective-permute-done.13.refs_10_), channel_id=1, source_target_pairs={{0,1},{1,0},{2,3},{3,2},{4,5},{5,4},{6,7},{7,6},{8,9},{9,8},{10,11... | collective-permute-start | bytes 6291464 | tf_op jit(solution)/shard_map/ppermute | solution.py:23
  63.1 24.9 %collective-permute-start.11 = (f32[4,17,32,128]{3,2,1,0:T(8,128)S(1)}, f32[4,17,32,128]{3,2,1,0:T(8,128)}, u32[]{:S(2)}, u32[]{:S(2)}) collective-permute-start(f32[4,17,32,128]{3,2,1,0:T(8,128)S(1)} %pad_maximum_fusion.1.refs_4_), channel_id=1, source_target_pairs={{0,16},{1,49},{2,18},{3,51},{4,20},{5,53},{6,22},{7,55},{8,24},{9,... | collective-permute-start | bytes 3342344 | tf_op jit(solution)/shard_map/ppermute | solution.py:23
  66.9 21.2 %collective-permute-start.9 = (f32[4,17,32,128]{3,2,1,0:T(8,128)S(1)}, f32[4,17,32,128]{3,2,1,0:T(8,128)}, u32[]{:S(2)}, u32[]{:S(2)}) collective-permute-start(f32[4,17,32,128]{3,2,1,0:T(8,128)S(1)} %collective-permute-done.7.refs_2_), channel_id=1, source_target_pairs={{0,4},{1,13},{2,6},{3,15},{4,0},{5,9},{6,2},{7,11},{8,12},{9,5},{1... | collective-permute-start | bytes 3342344 | tf_op jit(solution)/shard_map/ppermute | solution.py:23
  76.0 1.0 copy-start.4
  77.0 17.0 %collective-permute-start.12 = (f32[4,17,32,128]{3,2,1,0:T(8,128)}, f32[4,17,32,128]{3,2,1,0:T(8,128)}, u32[]{:S(2)}, u32[]{:S(2)}) collective-permute-start(f32[4,17,32,128]{3,2,1,0:T(8,128)} %collective-permute-done.10.refs_6_), channel_id=1, source_target_pairs={{0,16},{1,49},{2,18},{3,51},{4,20},{5,53},{6,22},{7,55},{8,24},{9,... | collective-permute-start | bytes 3342344 | tf_op jit(solution)/shard_map/ppermute | solution.py:23
  84.1 32.1 %collective-permute-start.18 = (f32[16,2,128,128]{3,2,1,0:T(8,128)}, f32[16,2,128,128]{3,2,1,0:T(8,128)}, u32[]{:S(2)}, u32[]{:S(2)}) collective-permute-start(f32[16,2,128,128]{3,2,1,0:T(8,128)} %collective-permute-done.17.far0), channel_id=1, source_target_pairs={{0,1},{1,0},{2,3},{3,2},{4,5},{5,4},{6,7},{7,6},{8,9},{9,8},{10,11... | collective-permute-start | bytes 6291464 | tf_op jit(solution)/shard_map/ppermute | solution.py:23
  94.0 1.6 copy-start.3
  95.6 1.2 copy-start.5
  115.2 1.0 copy-start.6
  124.8 24.7 %copy-start.8 = (s32[1,32]{1,0:T(1,128)S(1)}, s32[1,32]{1,0:T(1,128)}, u32[]{:S(2)}) copy-start(s32[1,32]{1,0:T(1,128)} %label_ref.1) | copy-start | bytes 388
  124.8 27.1 %copy-start.1 = (f32[1,32,128,128]{3,2,1,0:T(8,128)S(1)}, f32[1,32,128,128]{3,2,1,0:T(8,128)}, u32[]{:S(2)}) copy-start(f32[1,32,128,128]{3,2,1,0:T(8,128)} %param.5) | copy-start | bytes 6291460
  145.7 6.2 %collective-permute-start.19 = (f32[32,2,32,128]{3,2,1,0:T(8,128)S(1)}, f32[32,2,32,128]{3,2,1,0:T(8,128)}, u32[]{:S(2)}, u32[]{:S(2)}) collective-permute-start(f32[32,2,32,128]{3,2,1,0:T(8,128)S(1)} %all_to_all.5), channel_id=1, source_target_pairs={{0,1},{1,0},{2,3},{3,2},{4,5},{5,4},{6,7},{7,6},{8,9},{9,8},{10,11... | collective-permute-start | bytes 3145736 | tf_op jit(solution)/shard_map/ppermute | solution.py:23
  154.7 6.3 %collective-permute-start.20 = (f32[128,128]{1,0:T(8,128)S(1)}, f32[128,128]{1,0:T(8,128)S(1)}, u32[]{:S(2)}, u32[]{:S(2)}) collective-permute-start(f32[128,128]{1,0:T(8,128)S(1)} %share.1), channel_id=1, source_target_pairs={{0,1},{1,0},{2,3},{3,2},{4,5},{5,4},{6,7},{7,6},{8,9},{9,8},{10,11... | collective-permute-start | bytes 196616 | tf_op jit(solution)/shard_map/ppermute | solution.py:23
  156.2 4.8 %collective-permute-start.21 = (f32[128,128]{1,0:T(8,128)S(1)}, f32[128,128]{1,0:T(8,128)S(1)}, u32[]{:S(2)}, u32[]{:S(2)}) collective-permute-start(f32[128,128]{1,0:T(8,128)S(1)} %share.1), channel_id=1, source_target_pairs={{0,2},{1,3},{2,0},{3,1},{4,6},{5,7},{6,4},{7,5},{8,10},{9,11},{10,... | collective-permute-start | bytes 196616 | tf_op jit(solution)/shard_map/ppermute | solution.py:23
  156.6 4.9 %collective-permute-start.22 = (f32[128,128]{1,0:T(8,128)S(1)}, f32[128,128]{1,0:T(8,128)S(1)}, u32[]{:S(2)}, u32[]{:S(2)}) collective-permute-start(f32[128,128]{1,0:T(8,128)S(1)} %share.1), channel_id=1, source_target_pairs={{0,3},{1,2},{2,1},{3,0},{4,7},{5,6},{6,5},{7,4},{8,11},{9,10},{10,... | collective-permute-start | bytes 196616 | tf_op jit(solution)/shard_map/ppermute | solution.py:23

commit v3 on v2

--- a/solution.py
+++ b/solution.py
@@ -91,16 +91,25 @@
     return dot(wh, high) + (dot(wh, low) + dot(wl, high))
 
 
-def first_kernel(nodes, where, *refs):
-    parts, sigmas = refs[:8], refs[8:14]
-    out_ref, hi_out, lo_out, hi_ref, lo_ref, held, total, labels, arrived, left, read = refs[14:]
+def sums_kernel(halves, more, nodes, where, *refs):
+    count = len(halves)
+    given, refs = refs[: count + 6 + 3 * more], refs[count + 6 + 3 * more :]
+    (out_ref, hi_out, lo_out), refs = refs[:3], refs[3:]
+    hi_ref, lo_ref, w, held, total, labels, landed, arrived, left, read, *own = refs
+    parts = [pltpu.make_async_copy(t, w.at[i], landed.at[i]) for i, t in enumerate(given[:count])]
     texts = [
-        pltpu.make_async_copy(t.at[:, 16, pl.ds(0, 8)], labels.at[i], read.at[i]) for i, t in enumerate(parts)
+        pltpu.make_async_copy(t.at[:, 16, pl.ds(0, 8)], labels.at[i], read.at[i]) for i, t in enumerate(given[:count])
     ]
-    for copy in texts:
-        copy.start()
-    copies = [pltpu.make_async_copy(t, held.at[i], arrived.at[i]) for i, t in enumerate(sigmas)]
-    for copy in copies:
+    copies = [pltpu.make_async_copy(t, held.at[i], arrived.at[i]) for i, t in enumerate(given[count : count + 6])]
+    inward = []
+    if more:
+        out_ref[...] = given[-1][...]
+        merged, filled = own
+        inward = [
+            pltpu.make_async_copy(t, merged.at[i, pl.ds(0, 32)], filled.at[i])
+            for i, t in enumerate(given[count + 6 : count + 8])
+        ]
+    for copy in texts + parts + copies + inward:
         copy.start()
 
     def clear(b, carry):
@@ -111,29 +120,28 @@
     lax.fori_loop(0, hi_ref.shape[0], clear, 0)
     for copy in texts:
         copy.wait()
+
+    def put(i, row_of, place_of, hi_to, lo_to):
+        def node(n, carry):
+            rows = pl.ds(pl.multiple_of(row_of(n), Q), Q)
+            for k in range(16):
+                at = place_of(labels[i, n, 0, halves[i] * 16 + k].astype(jnp.int32))
+                hi, lo = split(w[i, n, k])
+                hi_to[at, rows, :] = hi
+                lo_to[at, rows, :] = lo
+            return carry
+
+        lax.fori_loop(0, 4, node, 0)
+
     for i, part in enumerate(parts):
-        def node(n, carry, i=i, part=part):
-            rows = pl.ds(pl.multiple_of(nodes[i * 4 + n] * Q, Q), Q)
-            for k in range(16):
-                at = labels[i, n, 0, i // 4 * 16 + k].astype(jnp.int32)
-                hi, lo = split(part[n, k])
-                hi_ref[at, rows, :] = hi
-                lo_ref[at, rows, :] = lo
-            return carry
-
-        lax.fori_loop(0, 4, node, 0)
-
-    outward = [
-        pltpu.make_async_copy(ref.at[pl.ds(where[2 + core], 16)], out.at[pl.ds(16 * core, 16)], left.at[2 * i + core])
-        for i, (ref, out) in enumerate(((hi_ref, hi_out), (lo_ref, lo_out)))
-        for core in range(2)
-    ]
-    for copy in outward:
-        copy.start()
+        part.wait()
+        put(i, lambda n: (i * 4 + n if more else nodes[i * 4 + n]) * Q, lambda at: at, hi_ref, lo_ref)
     for copy in copies:
         copy.wait()
 
     def run(first, sides, blocks):
+        total[:, : 2 * sides * B] = jnp.zeros((total.shape[0], 2 * sides * B), F32)
+
         def step(t, carry):
             k = pl.multiple_of(t * MANY, MANY)
             weights = [
@@ -145,80 +153,106 @@
 
         lax.fori_loop(0, 16 // MANY, step, 0)
 
-    total[...] = jnp.zeros_like(total)
+    def add(at, columns, fresh):
+        for n in range(columns):
+            place, column = at ^ (n // 2), total.at[:, n * B : (n + 1) * B]
+            if more:
+                for i in range(4 * count):
+                    out_ref[place, nodes[i], n % 2] += column[i * Q : (i + 1) * Q]
+            elif fresh:
+                out_ref[place, :, n % 2] = column[...].reshape(16, Q, B)
+            else:
+                out_ref[place, :, n % 2] += column[...].reshape(16, Q, B)
+
     run(0, 2, [(0, 1), (2, 3)])
-    at = where[4]
-    for n in range(4):
-        out_ref[at ^ (n // 2), :, n % 2] = total[:, n * B : (n + 1) * B].reshape(16, Q, B)
-    total[...] = jnp.zeros_like(total)
+    add(where[4], 4, True)
+    half = where[6]
+    sources = [ref.at[pl.ds(half, 32)] for ref in (hi_ref, lo_ref)]
+    if more:
+        for copy in inward:
+            copy.wait()
+        inside = lambda at: jnp.where(jnp.logical_and(at >= half, at < half + 32), at - half, 32)
+        for i in range(count):
+            put(i, lambda n: nodes[i * 4 + n] * Q, inside, merged.at[0], merged.at[1])
+        sources = [merged.at[i, pl.ds(0, 32)] for i in range(2)]
+    outward = [
+        pltpu.make_async_copy(source, out, left.at[i]) for i, (source, out) in enumerate(zip(sources, (hi_out, lo_out)))
+    ]
+    for copy in outward:
+        copy.start()
     run(2, 1, [(4, 5)])
-    for n in range(2):
-        out_ref[where[5], :, n] += total[:, n * B : (n + 1) * B].reshape(16, Q, B)
+    add(where[5], 2, False)
     for copy in outward:
         copy.wait()
 
 
-def first_sums(nodes, where, parts, sigmas):
-    whole = pl.BlockSpec(memory_space=pl.ANY)
-    rows = 16 * Q
+def sums(nodes, where, parts, halves, sigmas, earlier=()):
+    whole, count, more = pl.BlockSpec(memory_space=pl.ANY), len(parts), len(earlier) > 0
+    rows = count * 4 * Q if more else 16 * Q
     return pl.pallas_call(
-        first_kernel,
-        in_specs=[SCALARS] * 2 + [ON_CHIP] * 8 + [whole] * 6,
+        functools.partial(sums_kernel, halves, more),
+        in_specs=[SCALARS] * 2 + [whole] * (count + 6 + 2 * more) + [ON_CHIP] * more,
         out_specs=[ON_CHIP, whole, whole],
-        out_shape=[jax.ShapeDtypeStruct((2, 16, 2, Q, B), F32)] + [jax.ShapeDtypeStruct((32, rows, B), BF16)] * 2,
+        out_shape=[jax.ShapeDtypeStruct((2, 16, 2, Q, B), F32)] + [jax.ShapeDtypeStruct((32, 16 * Q, B), BF16)] * 2,
         scratch_shapes=[
             pltpu.VMEM((64, rows, B), BF16),
             pltpu.VMEM((64, rows, B), BF16),
+            pltpu.VMEM((count, 4, 17, Q, B), F32),
             pltpu.VMEM((6, 16, 2, B, B), F32),
             pltpu.VMEM((rows, 4 * B), F32),
-            pltpu.SMEM((8, 4, 8, B), F32),
+            pltpu.SMEM((count, 4, 8, B), F32),
+            pltpu.SemaphoreType.DMA((count,)),
             pltpu.SemaphoreType.DMA((6,)),
-            pltpu.SemaphoreType.DMA((4,)),
-            pltpu.SemaphoreType.DMA((8,)),
-        ],
-        compiler_params=pltpu.CompilerParams(vmem_limit_bytes=38 << 20),
+            pltpu.SemaphoreType.DMA((2,)),
+            pltpu.SemaphoreType.DMA((count,)),
+        ]
+        + [pltpu.VMEM((2, 33, 16 * Q, B), BF16), pltpu.SemaphoreType.DMA((2,))] * more,
+        compiler_params=pltpu.CompilerParams(vmem_limit_bytes=48 << 20),
         cost_estimate=pl.CostEstimate(flops=9 << 31, bytes_accessed=32 << 20, transcendentals=0),
-        name="first_sums",
-    )(nodes, where, *parts, *sigmas)
-
-
-def last_kernel(where, hi0, hi1, lo0, lo1, far0, far1, start, out_ref, total):
-    step, at = pl.program_id(0), where[0]
-
-    @pl.when(step == 0)
-    def _():
-        for n in range(2):
-            total[:, n * B : (n + 1) * B] = start[at, :, n].reshape(16 * Q, B)
-
-    weights = [[t[i] for t in pair for i in range(MANY)] for pair in ((hi0, hi1), (lo0, lo1))]
-    total[...] += gained(weights, [(far0, far1)], 1)
-
-    @pl.when(step == pl.num_programs(0) - 1)
-    def _():
-        for n in range(2):
-            out_ref[at, :, n] = total[:, n * B : (n + 1) * B].reshape(16, Q, B)
-        out_ref[1 - at] = start[1 - at]
+        name="sums_of_more" if more else "sums",
+    )(nodes, where, *parts, *sigmas, *earlier)
+
+
+def last_kernel(where, hi, lo, far0, far1, start, out_ref, weights, held, total, arrived):
+    at, steps = where[0], 16 // MANY
+    copies = []
+    for t in range(steps):
+        block = lambda first: pl.ds(first + t * MANY, MANY)
+        pairs = [(ref.at[block(16 * (core ^ where[1]))], weights.at[i, block(16 * core)]) for i, ref in enumerate((hi, lo)) for core in range(2)]
+        pairs += [(ref.at[block(0)], held.at[core, block(0)]) for core, ref in enumerate((far0, far1))]
+        copies.append([pltpu.make_async_copy(*pair, arrived.at[t, i]) for i, pair in enumerate(pairs)])
+        for copy in copies[-1]:
+            copy.start()
+    out_ref[1 - at] = start[1 - at]
+    for n in range(2):
+        total[:, n * B : (n + 1) * B] = start[at, :, n].reshape(16 * Q, B)
+    for t in range(steps):
+        for copy in copies[t]:
+            copy.wait()
+        each = range(t * MANY, (t + 1) * MANY)
+        w = [[weights[i, 16 * core + k] for core in range(2) for k in each] for i in range(2)]
+        total[...] += gained(w, [[held.at[core, pl.ds(t * MANY, MANY)] for core in range(2)]], 1)
+    for n in range(2):
+        out_ref[at, :, n] = total[:, n * B : (n + 1) * B].reshape(16, Q, B)
 
 
 def last_sums(at, hi, lo, far, start):
-    rows = 16 * Q
-    w = [pl.BlockSpec((MANY, rows, B), lambda i, w, core=core: (core * (16 // MANY) + i, 0, 0)) for core in range(2)]
-    s = pl.BlockSpec((MANY, 2, B, B), lambda i, w: (i, 0, 0, 0))
-    whole = pl.BlockSpec(start.shape, lambda i, w: (0,) * 5)
+    rows, away = 16 * Q, pl.BlockSpec(memory_space=pl.ANY)
     return pl.pallas_call(
         last_kernel,
-        grid_spec=pltpu.PrefetchScalarGridSpec(
-            num_scalar_prefetch=1,
-            grid=(16 // MANY,),
-            in_specs=w + w + [s, s, whole],
-            out_specs=whole,
-            scratch_shapes=[pltpu.VMEM((rows, 2 * B), F32)],
-        ),
+        in_specs=[SCALARS] + [away] * 4 + [ON_CHIP],
+        out_specs=ON_CHIP,
+        scratch_shapes=[
+            pltpu.VMEM((2, 32, rows, B), BF16),
+            pltpu.VMEM((2, 16, 2, B, B), F32),
+            pltpu.VMEM((rows, 2 * B), F32),
+            pltpu.SemaphoreType.DMA((16 // MANY, 6)),
+        ],
         out_shape=jax.ShapeDtypeStruct(start.shape, F32),
         compiler_params=pltpu.CompilerParams(vmem_limit_bytes=56 << 20),
         cost_estimate=pl.CostEstimate(flops=3 << 31, bytes_accessed=14 << 20, transcendentals=0),
         name="last_sums",
-    )(at[None], hi, hi, lo, lo, *far, start)
+    )(at, hi, lo, *far, start)
 
 
 def rows_of(core, a, kept, came):
@@ -273,15 +307,16 @@
     x1 = swap(sigma, X1, X3)
     a = jnp.stack([first, *ring(first, Z1, Z3)])
     b = jnp.stack([second, *ring(second, Y1, Y3)])
-    sigma, x1, a, b = lax.optimization_barrier((sigma, x1, a, b))
+    other = lambda t: swap(t, CORE)
+    sigma, x1, a, b, sigma_other = lax.optimization_barrier((sigma, x1, a, b, other(sigma)))
     x2 = swap(sigma, X3, X1)
     a2, b2 = swap(a, Y3, Y1), swap(b, Z3, Z1)
-    a1, b1 = swap(after(a, a2), Y1, Y3), swap(after(b, b2), Z1, Z3)
+    a1, b1 = swap(a, Y1, Y3), swap(b, Z1, Z3)
+    x2, a1, a2, b1, b2 = lax.optimization_barrier((x2, a1, a2, b1, b2))
+    x3 = swap(x2, X1, X3)
     a3, b3 = swap(a2, Y1, Y3), swap(b2, Z1, Z3)
-    sigma_other, x1_other = swap(sigma, CORE), swap(x1, CORE)
-    x3 = swap(after(x2, a2, b2, sigma_other, x1_other), X1, X3)
-    sigmas = (x1, swap(x2, CORE), x2, x1_other, sigma, sigma_other)
-    return sigmas, (x3, swap(x3, CORE)), (a, a1, a2, a3, b, b1, b2, b3)
+    sigmas = (x1, other(x2), x2, other(x1), sigma, sigma_other)
+    return sigmas, x3, (a, a1, a2, b, b1, b2), (a3, b3)
 
 
 def local(sigma_anc, panel_u, structure, diag_inv):
@@ -290,18 +325,21 @@
     x_lo, core = row // 2, row % 2
     panel = panel_u[0]
 
-    sigmas, far, pieces = gather(sigma_anc, *cut(panel, structure, row))
+    sigmas, far, most, rest = gather(sigma_anc, *cut(panel, structure, row))
 
     away = jnp.stack([0 * core, 1 + 2 * core, 3 - 2 * core, 2 + 0 * core]).astype(jnp.int32)
     there_z, there_y = z ^ away, y ^ away
-    nodes = jnp.stack([there_y[:, None] + there_z * 4, there_z[:, None] * 4 + there_y]).reshape(-1)
+    nodes = jnp.stack([there_y[:, None] + there_z * 4, there_z[:, None] * 4 + there_y])
     entry = jnp.arange(32, dtype=jnp.int32)
     mine = jnp.sum(jnp.where(structure[0][:, None] == (16 * row + jnp.arange(16))[None, :], entry[:, None] + 1, 0), axis=0) - 1
 
     base = lambda x: [32 * x + 16 * core, 32 * x + 16 * (1 - core)]
-    where = jnp.stack(base(1 - x_lo) + base(x_lo) + [x_hi ^ core, x_hi])
-    part, hi, lo = first_sums(nodes, where, pieces, sigmas)
-    part = last_sums(1 - x_hi, hi, lo, far, part)
+    where = jnp.stack(base(1 - x_lo) + base(x_lo) + [x_hi ^ core, x_hi, 32 * x_lo])
+    part, hi, lo = sums(nodes[:, :3].reshape(-1), where, most, (0, 0, 0, 1, 1, 1), sigmas)
+    far = after(far, part)
+    far = (far, swap(far, CORE))
+    part, hi, lo = sums(nodes[:, 3].reshape(-1), where, rest, (0, 1), sigmas, (hi, lo, part))
+    part = last_sums(jnp.stack([1 - x_hi, core]), hi, lo, far, part)
     groups = [
         [h * 64 + q * 4 + l * 2 + c for l in range(2) for q in range(16)] for h in range(2) for c in range(2)
     ]

time: 163 us -> 158 us (0.969)
  Pallas kernels: 36.2 us -> 53.9 us
  waiting for transfers between devices: 46.8 us -> 32.4 us
  starting transfers between devices: 47.7 us -> 40.3 us
    pallas_call x2 -> x3, Pallas kernels: 27 us -> 44.3 us  [the longest x2 33.2 us: sums(): pl.pallas_call(functools.partial(sums_kernel, halves, more), in_specs=[SC...]
    ppermute x23, waiting for transfers between devices: 46.8 us -> 32.4 us  [swap(): lax.ppermute(x, AXES, [(i, i ^ (odd if i % 2 else even)) for i in range(1...]
    ppermute x23, starting transfers between devices: 47.7 us -> 40.3 us  [swap(): lax.ppermute(x, AXES, [(i, i ^ (odd if i % 2 else even)) for i in range(1...]
    unnamed x22 -> x24, local copies, waits for them, and re-layouts: 7.48 us -> 6.44 us
  transfers between devices with their start and end apart: 23 -> 23, of which waited for: 13 -> 11; matrix products, arithmetic and copies ran while one was open for 1% -> 2% of each run, Pallas kernels for 13% -> 23%
where the time goes in v3:
time: 158 us; the launch traced here: 157 us
  Pallas kernels  53.9 us (34%)
  starting transfers between devices  40.3 us (26%)
  waiting for transfers between devices  32.4 us (21%)
  blocking collectives  19.9 us (13%)
  local copies, waits for them, and re-layouts  6.7 us (4%)
  other arithmetic  2.14 us (1%)
    ppermute x23, starting transfers between devices, swap(): lax.ppermute(x, AXES, [(i, i ^ (odd if i % 2 else even)) for i in range(1...  40.3 us
    pallas_call x2, Pallas kernels, sums(): pl.pallas_call(functools.partial(sums_kernel, halves, more), in_specs=[SC...  33.2 us
    ppermute x23, waiting for transfers between devices, swap(): lax.ppermute(x, AXES, [(i, i ^ (odd if i % 2 else even)) for i in range(1...  32.4 us
    all_to_all x1, blocking collectives, local(): lax.all_to_all(part.reshape(32, 2, Q, B), AXES, 0, 0, axis_index_groups=g...  19.9 us
    pallas_call x1, Pallas kernels, last_sums(): pl.pallas_call(last_kernel, in_specs=[SCALARS] + [away] * 4 + [ON_CHIP],...  11.1 us
    unnamed x24, local copies, waits for them, and re-layouts  6.44 us
    pallas_call x2, Pallas kernels, on_one(): pl.pallas_call(kernel, grid_spec=pltpu.PrefetchScalarGridSpec(num_scalar_...  6.24 us
    pallas_call x1, Pallas kernels, cut(): pl.pallas_call(cut_kernel, grid_spec=pltpu.PrefetchScalarGridSpec(num_sca...  3.26 us
  transfers between devices with their start and end apart: 23, of which 11 were waited for; matrix products, arithmetic and copies ran while one was open for 2% of the time, Pallas kernels for 23%

profile of v3, /device:TPU:1, one launch (start us, length us, event | category | flops | bytes accessed | tf_op | source)
XLA Modules:
  0.0 157.0 jit_solution(10870368861081229962)
XLA Ops:
  0.6 0.0 copy-start
  0.6 3.3 %cut.1 = (f32[17,32,128]{2,1,0:T(8,128)}, f32[17,32,128]{2,1,0:T(8,128)}) custom-call(s32[1]{0:T(128)} %bitcast.12.where, f32[32,128,128]{2,1,0:T(8,128)} %bitcast.33, s32[1,32]{1,0:T(1,128)} %label_ref.1), custom_call_target="tpu_custom_call" | custom-call | tf_op jit(solution)/shard_map/cut/pallas_call | solution.py:62
  3.9 3.4 %collective-permute-start = (f32[16,2,128,128]{3,2,1,0:T(8,128)}, f32[16,2,128,128]{3,2,1,0:T(8,128)}, u32[]{:S(2)}, u32[]{:S(2)}) collective-permute-start(f32[16,2,128,128]{3,2,1,0:T(8,128)} %refs_6_), channel_id=1, source_target_pairs={{0,2},{1,67},{2,0},{3,65},{4,6},{5,71},{6,4},{7,69},{8,10},{9,75},... | collective-permute-start | bytes 6291464 | tf_op jit(solution)/shard_map/ppermute | solution.py:23
  7.3 0.0 collective-permute-start.7
  7.3 1.6 %collective-permute-start.2 = (f32[17,32,128]{2,1,0:T(8,128)}, f32[17,32,128]{2,1,0:T(8,128)S(1)}, u32[]{:S(2)}, u32[]{:S(2)}) collective-permute-start(f32[17,32,128]{2,1,0:T(8,128)} %get-tuple-element.27), channel_id=1, source_target_pairs={{0,48},{1,17},{2,50},{3,19},{4,52},{5,21},{6,54},{7,23},{8,56},{9,... | collective-permute-start | bytes 835592 | tf_op jit(solution)/shard_map/ppermute | solution.py:23
  8.9 2.2 %collective-permute-start.1 = (f32[17,32,128]{2,1,0:T(8,128)}, f32[17,32,128]{2,1,0:T(8,128)S(1)}, u32[]{:S(2)}, u32[]{:S(2)}) collective-permute-start(f32[17,32,128]{2,1,0:T(8,128)} %get-tuple-element.27), channel_id=1, source_target_pairs={{0,16},{1,49},{2,18},{3,51},{4,20},{5,53},{6,22},{7,55},{8,24},{9,... | collective-permute-start | bytes 835592 | tf_op jit(solution)/shard_map/ppermute | solution.py:23
  11.2 1.3 collective-permute-start.5
  12.4 1.0 collective-permute-done.2
  13.5 5.6 %collective-permute-start.3 = (f32[17,32,128]{2,1,0:T(8,128)S(1)}, f32[17,32,128]{2,1,0:T(8,128)S(1)}, u32[]{:S(2)}, u32[]{:S(2)}) collective-permute-start(f32[17,32,128]{2,1,0:T(8,128)S(1)} %collective-permute-done.2), channel_id=1, source_target_pairs={{0,16},{1,49},{2,18},{3,51},{4,20},{5,53},{6,22},{7,55},{8,24},{9,... | collective-permute-start | bytes 835592 | tf_op jit(solution)/shard_map/ppermute | solution.py:23
  19.1 2.7 %collective-permute-start.4 = (f32[17,32,128]{2,1,0:T(8,128)}, f32[17,32,128]{2,1,0:T(8,128)S(1)}, u32[]{:S(2)}, u32[]{:S(2)}) collective-permute-start(f32[17,32,128]{2,1,0:T(8,128)} %get-tuple-element.28), channel_id=1, source_target_pairs={{0,4},{1,13},{2,6},{3,15},{4,0},{5,9},{6,2},{7,11},{8,12},{9,5},{1... | collective-permute-start | bytes 835592 | tf_op jit(solution)/shard_map/ppermute | solution.py:23
  21.8 0.1 collective-permute-start.6
  21.9 1.1 collective-permute-done.3
  23.0 1.1 pad_maximum_fusion.refs_0_
  24.1 1.9 %collective-permute-done.4 = f32[17,32,128]{2,1,0:T(8,128)S(1)} collective-permute-done((f32[17,32,128]{2,1,0:T(8,128)}, f32[17,32,128]{2,1,0:T(8,128)S(1)}, u32[]{:S(2)}, u32[]{:S(2)}) %collective-permute-start.4) | collective-permute-done | bytes 278560 | tf_op jit(solution)/shard_map/ppermute | solution.py:23
  25.9 3.0 %collective-permute-done.6 = f32[17,32,128]{2,1,0:T(8,128)S(1)} collective-permute-done((f32[17,32,128]{2,1,0:T(8,128)S(1)}, f32[17,32,128]{2,1,0:T(8,128)S(1)}, u32[]{:S(2)}, u32[]{:S(2)}) %collective-permute-start.6) | collective-permute-done | bytes 278560 | tf_op jit(solution)/shard_map/ppermute | solution.py:23
  28.9 0.1 pad_maximum_fusion.1.refs_3_
  29.0 2.0 %collective-permute-done.refs_6_.refs_2_ = f32[16,2,128,128]{3,2,1,0:T(8,128)} collective-permute-done((f32[16,2,128,128]{3,2,1,0:T(8,128)}, f32[16,2,128,128]{3,2,1,0:T(8,128)}, u32[]{:S(2)}, u32[]{:S(2)}) %collective-permute-start) | collective-permute-done | bytes 2097184 | tf_op jit(solution)/shard_map/ppermute | solution.py:23
  31.0 0.0 collective-permute-done.7.refs_11_.refs_7_
  31.0 0.5 collective-permute-start.8
  31.5 2.7 %collective-permute-start.9 = (f32[4,17,32,128]{3,2,1,0:T(8,128)S(1)}, f32[4,17,32,128]{3,2,1,0:T(8,128)S(1)}, u32[]{:S(2)}, u32[]{:S(2)}) collective-permute-start(f32[4,17,32,128]{3,2,1,0:T(8,128)S(1)} %pad_maximum_fusion.refs_0_), channel_id=1, source_target_pairs={{0,4},{1,13},{2,6},{3,15},{4,0},{5,9},{6,2},{7,11},{8,12},{9,5},{1... | collective-permute-start | bytes 3342344 | tf_op jit(solution)/shard_map/ppermute | solution.py:23
  34.2 3.8 %collective-permute-start.11 = (f32[4,17,32,128]{3,2,1,0:T(8,128)S(1)}, f32[4,17,32,128]{3,2,1,0:T(8,128)S(1)}, u32[]{:S(2)}, u32[]{:S(2)}) collective-permute-start(f32[4,17,32,128]{3,2,1,0:T(8,128)S(1)} %pad_maximum_fusion.1.refs_3_), channel_id=1, source_target_pairs={{0,16},{1,49},{2,18},{3,51},{4,20},{5,53},{6,22},{7,55},{8,24},{9,... | collective-permute-start | bytes 3342344 | tf_op jit(solution)/shard_map/ppermute | solution.py:23
  38.0 0.0 collective-permute-start.12
  38.0 16.4 %collective-permute-done.9.refs_1_ = f32[4,17,32,128]{3,2,1,0:T(8,128)S(1)} collective-permute-done((f32[4,17,32,128]{3,2,1,0:T(8,128)S(1)}, f32[4,17,32,128]{3,2,1,0:T(8,128)S(1)}, u32[]{:S(2)}, u32[]{:S(2)}) %collective-permute-start.9) | collective-permute-done | bytes 1114144 | tf_op jit(solution)/shard_map/ppermute | solution.py:23
  54.4 1.0 copy-done.2
  55.4 6.8 %collective-permute-start.16 = (f32[16,2,128,128]{3,2,1,0:T(8,128)}, f32[16,2,128,128]{3,2,1,0:T(8,128)}, u32[]{:S(2)}, u32[]{:S(2)}) collective-permute-start(f32[16,2,128,128]{3,2,1,0:T(8,128)} %collective-permute-done.refs_6_.refs_2_), channel_id=1, source_target_pairs={{0,1},{1,0},{2,3},{3,2},{4,5},{5,4},{6,7},{7,6},{8,9},{9,8},{10,11... | collective-permute-start | bytes 6291464 | tf_op jit(solution)/shard_map/ppermute | solution.py:23
  62.2 1.6 %collective-permute-done.12.refs_5_ = f32[4,17,32,128]{3,2,1,0:T(8,128)S(1)} collective-permute-done((f32[4,17,32,128]{3,2,1,0:T(8,128)S(1)}, f32[4,17,32,128]{3,2,1,0:T(8,128)S(1)}, u32[]{:S(2)}, u32[]{:S(2)}) %collective-permute-start.12) | collective-permute-done | bytes 1114144 | tf_op jit(solution)/shard_map/ppermute | solution.py:23
  63.9 1.0 copy-done.10
  64.9 1.5 collective-permute-start.15
  66.4 0.1 xor_multiply_fusion
  66.5 0.4 collective-permute-start.17
  66.9 0.1 broadcast_add_fusion.1
  67.0 0.1 reshape.231.nodes
  67.1 0.1 stack.88.where
  67.2 0.6 collective-permute-start.13
  67.8 2.7 %collective-permute-start.14 = (f32[4,17,32,128]{3,2,1,0:T(8,128)}, f32[4,17,32,128]{3,2,1,0:T(8,128)}, u32[]{:S(2)}, u32[]{:S(2)}) collective-permute-start(f32[4,17,32,128]{3,2,1,0:T(8,128)} %copy-done.10), channel_id=1, source_target_pairs={{0,16},{1,49},{2,18},{3,51},{4,20},{5,53},{6,22},{7,55},{8,24},{9,... | collective-permute-start | bytes 3342344 | tf_op jit(solution)/shard_map/ppermute | solution.py:23
  70.5 0.1 collective-permute-done.15.refs_7_.refs_3_
  70.6 1.2 copy-done.3
  71.8 18.1 %sums.1 = (f32[2,16,2,32,128]{4,3,2,1,0:T(8,128)S(1)}, bf16[32,512,128]{2,1,0:T(8,128)(2,1)}, bf16[32,512,128]{2,1,0:T(8,128)(2,1)}) custom-call(s32[24]{0:T(128)S(1)} %reshape.231.nodes, s32[7]{0:T(128)S(1)} %stack.88.where, f32[4,17,32,128]{3,2,1,0:T(8,128)S(1)} %pad_maximum_fusion.refs_0_, f32[4,17,32,128]{3,2,1,0:T(8,128)S(1)} %copy-done.3, ...), custom_call_target="tpu_custom_call" | custom-call | flops 19327352832 | bytes 33554432 | tf_op jit(solution)/shard_map/sums/pallas_call | solution.py:192
  89.9 0.0 copy-start.5
  89.9 1.0 copy-done.5
  90.9 2.1 %collective-permute-done.17.far0 = f32[16,2,128,128]{3,2,1,0:T(8,128)} collective-permute-done((f32[16,2,128,128]{3,2,1,0:T(8,128)}, f32[16,2,128,128]{3,2,1,0:T(8,128)}, u32[]{:S(2)}, u32[]{:S(2)}) %collective-permute-start.17) | collective-permute-done | bytes 2097184 | tf_op jit(solution)/shard_map/ppermute | solution.py:23
  92.9 0.0 collective-permute-start.18
  93.0 0.1 reshape_squeeze.3.nodes
  93.1 0.6 pad_add_fusion.1.where
  93.6 0.0 collective-permute-done.13.refs_0_
  93.7 1.2 copy-done.6
  94.9 15.1 %sums_of_more.1 = (f32[2,16,2,32,128]{4,3,2,1,0:T(8,128)S(1)}, bf16[32,512,128]{2,1,0:T(8,128)(2,1)}, bf16[32,512,128]{2,1,0:T(8,128)(2,1)}) custom-call(s32[8]{0:T(128)S(1)} %reshape_squeeze.3.nodes, s32[7]{0:T(128)S(1)} %stack.88.where, f32[4,17,32,128]{3,2,1,0:T(8,128)} %collective-permute-done.13.refs_0_, ...), custom_call_target="tpu_custom_call" | custom-call | flops 19327352832 | bytes 33554432 | tf_op jit(solution)/shard_map/sums_of_more/pallas_call | solution.py:192
  110.0 0.0 copy-start.4
  110.0 1.0 copy-done.4
  111.0 0.0 collective-permute-done.18.far1
  111.0 11.1 %last_sums.1 = f32[2,16,2,32,128]{4,3,2,1,0:T(8,128)} custom-call(s32[2]{0:T(128)} %pad_add_fusion.1.where, bf16[32,512,128]{2,1,0:T(8,128)(2,1)} %get-tuple-element.42.hi, bf16[32,512,128]{2,1,0:T(8,128)(2,1)} %get-tuple-element.43.lo, f32[16,2,128,128]{3,2,1,0:T(8,128)} %collective-permute-done.17.far0, f32[16,2,128,128]{3,2,1,0:T(8,128)} %collective-permute-done.18.far1, ...), custom_call_target="tpu_custom_call" | custom-call | flops 6442450944 | bytes 14680064 | tf_op jit(solution)/shard_map/last_sums/pallas_call | solution.py:241
  122.1 0.0 copy-start.8
  122.1 0.0 copy-start.1
  122.1 19.9 %all_to_all.5 = f32[32,2,32,128]{3,2,1,0:T(8,128)S(1)} all-to-all(f32[32,2,32,128]{3,2,1,0:T(8,128)} %bitcast.36), channel_id=1, replica_groups={{0,4,8,12,16,20,24,28,32,36,40,44,48,52,56,60,2,6,10,14,18,22,26,30,34,..., dimensions={0} | all-to-all | bytes 2097152 | tf_op jit(solution)/shard_map/all_to_all | solution.py:346
  142.1 2.0 %collective-permute-start.19 = (f32[32,2,32,128]{3,2,1,0:T(8,128)S(1)}, f32[32,2,32,128]{3,2,1,0:T(8,128)}, u32[]{:S(2)}, u32[]{:S(2)}) collective-permute-start(f32[32,2,32,128]{3,2,1,0:T(8,128)S(1)} %all_to_all.5), channel_id=1, source_target_pairs={{0,1},{1,0},{2,3},{3,2},{4,5},{5,4},{6,7},{7,6},{8,9},{9,8},{10,11... | collective-permute-start | bytes 3145736 | tf_op jit(solution)/shard_map/ppermute | solution.py:23
  144.1 0.2 select_reduce_fusion
  144.3 2.2 %collective-permute-done.19 = f32[32,2,32,128]{3,2,1,0:T(8,128)} collective-permute-done((f32[32,2,32,128]{3,2,1,0:T(8,128)S(1)}, f32[32,2,32,128]{3,2,1,0:T(8,128)}, u32[]{:S(2)}, u32[]{:S(2)}) %collective-permute-start.19) | collective-permute-done | bytes 1048608 | tf_op jit(solution)/shard_map/ppermute | solution.py:23
  146.5 3.2 %share.1 = f32[128,128]{1,0:T(8,128)S(1)} custom-call(s32[1]{0:T(128)} %bitcast.where, s32[16]{0:T(128)S(1)} %broadcast_add_fusion.2.picks, f32[32,128,128]{2,1,0:T(8,128)S(1)} %bitcast.34, f32[2,2,8,2,32,128]{5,4,3,2,1,0:T(8,128)S(1)} %bitcast.31, f32[2,2,8,2,32,128]{5,4,3,2,1,0:T(8,128)} %bitcast.24.came), custom_call_target="tpu_custom_call" | custom-call | flops 134217728 | bytes 4194304 | tf_op jit(solution)/shard_map/share/pallas_call | solution.py:285
  149.7 0.4 collective-permute-start.20
  150.1 1.7 %collective-permute-start.21 = (f32[128,128]{1,0:T(8,128)S(1)}, f32[128,128]{1,0:T(8,128)S(1)}, u32[]{:S(2)}, u32[]{:S(2)}) collective-permute-start(f32[128,128]{1,0:T(8,128)S(1)} %share.1), channel_id=1, source_target_pairs={{0,2},{1,3},{2,0},{3,1},{4,6},{5,7},{6,4},{7,5},{8,10},{9,11},{10,... | collective-permute-start | bytes 196616 | tf_op jit(solution)/shard_map/ppermute | solution.py:23
  151.8 0.1 collective-permute-start.22
  151.9 3.1 %panel.1 = f32[16,128,128]{2,1,0:T(8,128)} custom-call(s32[1]{0:T(128)} %bitcast.where, s32[16]{0:T(128)S(1)} %broadcast_add_fusion.2.picks, f32[2,2,8,2,32,128]{5,4,3,2,1,0:T(8,128)S(1)} %bitcast.32, f32[2,2,8,2,32,128]{5,4,3,2,1,0:T(8,128)} %bitcast.24.came), custom_call_target="tpu_custom_call" | custom-call | bytes 4194304 | tf_op jit(solution)/shard_map/panel/pallas_call | solution.py:285
  155.0 1.0 collective-permute-done.22
  156.0 0.9 fusion.1
  (29 shorter events, 0.1 us)
Async XLA Ops:
  0.6 155.4 %copy-start = (f32[1,128,128]{2,1,0:T(8,128)S(1)}, f32[1,128,128]{2,1,0:T(8,128)}, u32[]{:S(2)}) copy-start(f32[1,128,128]{2,1,0:T(8,128)} %param.7) | copy-start | bytes 196612
  3.9 27.1 %collective-permute-start = (f32[16,2,128,128]{3,2,1,0:T(8,128)}, f32[16,2,128,128]{3,2,1,0:T(8,128)}, u32[]{:S(2)}, u32[]{:S(2)}) collective-permute-start(f32[16,2,128,128]{3,2,1,0:T(8,128)} %refs_6_), channel_id=1, source_target_pairs={{0,2},{1,67},{2,0},{3,65},{4,6},{5,71},{6,4},{7,69},{8,10},{9,75},... | collective-permute-start | bytes 6291464 | tf_op jit(solution)/shard_map/ppermute | solution.py:23
  7.3 23.7 %collective-permute-start.7 = (f32[16,2,128,128]{3,2,1,0:T(8,128)}, f32[16,2,128,128]{3,2,1,0:T(8,128)S(1)}, u32[]{:S(2)}, u32[]{:S(2)}) collective-permute-start(f32[16,2,128,128]{3,2,1,0:T(8,128)} %refs_6_), channel_id=1, source_target_pairs={{0,1},{1,0},{2,3},{3,2},{4,5},{5,4},{6,7},{7,6},{8,9},{9,8},{10,11... | collective-permute-start | bytes 6291464 | tf_op jit(solution)/shard_map/ppermute | solution.py:23
  7.3 6.2 %collective-permute-start.2 = (f32[17,32,128]{2,1,0:T(8,128)}, f32[17,32,128]{2,1,0:T(8,128)S(1)}, u32[]{:S(2)}, u32[]{:S(2)}) collective-permute-start(f32[17,32,128]{2,1,0:T(8,128)} %get-tuple-element.27), channel_id=1, source_target_pairs={{0,48},{1,17},{2,50},{3,19},{4,52},{5,21},{6,54},{7,23},{8,56},{9,... | collective-permute-start | bytes 835592 | tf_op jit(solution)/shard_map/ppermute | solution.py:23
  8.9 10.2 %collective-permute-start.1 = (f32[17,32,128]{2,1,0:T(8,128)}, f32[17,32,128]{2,1,0:T(8,128)S(1)}, u32[]{:S(2)}, u32[]{:S(2)}) collective-permute-start(f32[17,32,128]{2,1,0:T(8,128)} %get-tuple-element.27), channel_id=1, source_target_pairs={{0,16},{1,49},{2,18},{3,51},{4,20},{5,53},{6,22},{7,55},{8,24},{9,... | collective-permute-start | bytes 835592 | tf_op jit(solution)/shard_map/ppermute | solution.py:23
  11.2 10.6 %collective-permute-start.5 = (f32[17,32,128]{2,1,0:T(8,128)}, f32[17,32,128]{2,1,0:T(8,128)S(1)}, u32[]{:S(2)}, u32[]{:S(2)}) collective-permute-start(f32[17,32,128]{2,1,0:T(8,128)} %get-tuple-element.28), channel_id=1, source_target_pairs={{0,12},{1,5},{2,14},{3,7},{4,8},{5,1},{6,10},{7,3},{8,4},{9,13},{1... | collective-permute-start | bytes 835592 | tf_op jit(solution)/shard_map/ppermute | solution.py:23
  13.5 9.5 %collective-permute-start.3 = (f32[17,32,128]{2,1,0:T(8,128)S(1)}, f32[17,32,128]{2,1,0:T(8,128)S(1)}, u32[]{:S(2)}, u32[]{:S(2)}) collective-permute-start(f32[17,32,128]{2,1,0:T(8,128)S(1)} %collective-permute-done.2), channel_id=1, source_target_pairs={{0,16},{1,49},{2,18},{3,51},{4,20},{5,53},{6,22},{7,55},{8,24},{9,... | collective-permute-start | bytes 835592 | tf_op jit(solution)/shard_map/ppermute | solution.py:23
  19.1 6.9 %collective-permute-start.4 = (f32[17,32,128]{2,1,0:T(8,128)}, f32[17,32,128]{2,1,0:T(8,128)S(1)}, u32[]{:S(2)}, u32[]{:S(2)}) collective-permute-start(f32[17,32,128]{2,1,0:T(8,128)} %get-tuple-element.28), channel_id=1, source_target_pairs={{0,4},{1,13},{2,6},{3,15},{4,0},{5,9},{6,2},{7,11},{8,12},{9,5},{1... | collective-permute-start | bytes 835592 | tf_op jit(solution)/shard_map/ppermute | solution.py:23
  21.8 7.1 %collective-permute-start.6 = (f32[17,32,128]{2,1,0:T(8,128)S(1)}, f32[17,32,128]{2,1,0:T(8,128)S(1)}, u32[]{:S(2)}, u32[]{:S(2)}) collective-permute-start(f32[17,32,128]{2,1,0:T(8,128)S(1)} %collective-permute-done.5), channel_id=1, source_target_pairs={{0,4},{1,13},{2,6},{3,15},{4,0},{5,9},{6,2},{7,11},{8,12},{9,5},{1... | collective-permute-start | bytes 835592 | tf_op jit(solution)/shard_map/ppermute | solution.py:23
  23.0 5.9 %copy-start.7 = (f32[17,32,128]{2,1,0:T(8,128)S(1)}, f32[17,32,128]{2,1,0:T(8,128)}, u32[]{:S(2)}) copy-start(f32[17,32,128]{2,1,0:T(8,128)} %get-tuple-element.28) | copy-start | bytes 835588
  31.0 32.9 %copy-start.9 = (f32[16,2,128,128]{3,2,1,0:T(8,128)}, f32[16,2,128,128]{3,2,1,0:T(8,128)S(1)}, u32[]{:S(2)}) copy-start(f32[16,2,128,128]{3,2,1,0:T(8,128)S(1)} %collective-permute-done.7.refs_11_.refs_7_) | copy-start | bytes 6291460
  31.0 32.9 %collective-permute-start.8 = (f32[16,2,128,128]{3,2,1,0:T(8,128)}, f32[16,2,128,128]{3,2,1,0:T(8,128)}, u32[]{:S(2)}, u32[]{:S(2)}) collective-permute-start(f32[16,2,128,128]{3,2,1,0:T(8,128)} %refs_6_), channel_id=1, source_target_pairs={{0,66},{1,3},{2,64},{3,1},{4,70},{5,7},{6,68},{7,5},{8,74},{9,11},... | collective-permute-start | bytes 6291464 | tf_op jit(solution)/shard_map/ppermute | solution.py:23
  31.5 22.9 %collective-permute-start.9 = (f32[4,17,32,128]{3,2,1,0:T(8,128)S(1)}, f32[4,17,32,128]{3,2,1,0:T(8,128)S(1)}, u32[]{:S(2)}, u32[]{:S(2)}) collective-permute-start(f32[4,17,32,128]{3,2,1,0:T(8,128)S(1)} %pad_maximum_fusion.refs_0_), channel_id=1, source_target_pairs={{0,4},{1,13},{2,6},{3,15},{4,0},{5,9},{6,2},{7,11},{8,12},{9,5},{1... | collective-permute-start | bytes 3342344 | tf_op jit(solution)/shard_map/ppermute | solution.py:23
  34.2 28.0 %collective-permute-start.10 = (f32[4,17,32,128]{3,2,1,0:T(8,128)S(1)}, f32[4,17,32,128]{3,2,1,0:T(8,128)S(1)}, u32[]{:S(2)}, u32[]{:S(2)}) collective-permute-start(f32[4,17,32,128]{3,2,1,0:T(8,128)S(1)} %pad_maximum_fusion.refs_0_), channel_id=1, source_target_pairs={{0,12},{1,5},{2,14},{3,7},{4,8},{5,1},{6,10},{7,3},{8,4},{9,13},{1... | collective-permute-start | bytes 3342344 | tf_op jit(solution)/shard_map/ppermute | solution.py:23
  34.2 28.0 %collective-permute-start.11 = (f32[4,17,32,128]{3,2,1,0:T(8,128)S(1)}, f32[4,17,32,128]{3,2,1,0:T(8,128)S(1)}, u32[]{:S(2)}, u32[]{:S(2)}) collective-permute-start(f32[4,17,32,128]{3,2,1,0:T(8,128)S(1)} %pad_maximum_fusion.1.refs_3_), channel_id=1, source_target_pairs={{0,16},{1,49},{2,18},{3,51},{4,20},{5,53},{6,22},{7,55},{8,24},{9,... | collective-permute-start | bytes 3342344 | tf_op jit(solution)/shard_map/ppermute | solution.py:23
  38.0 25.9 %collective-permute-start.12 = (f32[4,17,32,128]{3,2,1,0:T(8,128)S(1)}, f32[4,17,32,128]{3,2,1,0:T(8,128)S(1)}, u32[]{:S(2)}, u32[]{:S(2)}) collective-permute-start(f32[4,17,32,128]{3,2,1,0:T(8,128)S(1)} %pad_maximum_fusion.1.refs_3_), channel_id=1, source_target_pairs={{0,48},{1,17},{2,50},{3,19},{4,52},{5,21},{6,54},{7,23},{8,56},{9,... | collective-permute-start | bytes 3342344 | tf_op jit(solution)/shard_map/ppermute | solution.py:23
  54.4 1.0 copy-start.2
  55.4 15.1 %collective-permute-start.16 = (f32[16,2,128,128]{3,2,1,0:T(8,128)}, f32[16,2,128,128]{3,2,1,0:T(8,128)}, u32[]{:S(2)}, u32[]{:S(2)}) collective-permute-start(f32[16,2,128,128]{3,2,1,0:T(8,128)} %collective-permute-done.refs_6_.refs_2_), channel_id=1, source_target_pairs={{0,1},{1,0},{2,3},{3,2},{4,5},{5,4},{6,7},{7,6},{8,9},{9,8},{10,11... | collective-permute-start | bytes 6291464 | tf_op jit(solution)/shard_map/ppermute | solution.py:23
  62.2 1.7 %copy-start.11 = (f32[4,17,32,128]{3,2,1,0:T(8,128)}, f32[4,17,32,128]{3,2,1,0:T(8,128)S(1)}, u32[]{:S(2)}) copy-start(f32[4,17,32,128]{3,2,1,0:T(8,128)S(1)} %collective-permute-done.11.refs_4_) | copy-start | bytes 3342340
  63.9 1.0 copy-start.10
  64.9 5.7 %collective-permute-start.15 = (f32[16,2,128,128]{3,2,1,0:T(8,128)}, f32[16,2,128,128]{3,2,1,0:T(8,128)}, u32[]{:S(2)}, u32[]{:S(2)}) collective-permute-start(f32[16,2,128,128]{3,2,1,0:T(8,128)} %collective-permute-done.8.refs_8_.refs_4_), channel_id=1, source_target_pairs={{0,1},{1,0},{2,3},{3,2},{4,5},{5,4},{6,7},{7,6},{8,9},{9,8},{10,11... | collective-permute-start | bytes 6291464 | tf_op jit(solution)/shard_map/ppermute | solution.py:23
  66.5 26.4 %collective-permute-start.17 = (f32[16,2,128,128]{3,2,1,0:T(8,128)}, f32[16,2,128,128]{3,2,1,0:T(8,128)}, u32[]{:S(2)}, u32[]{:S(2)}) collective-permute-start(f32[16,2,128,128]{3,2,1,0:T(8,128)} %collective-permute-done.8.refs_8_.refs_4_), channel_id=1, source_target_pairs={{0,2},{1,67},{2,0},{3,65},{4,6},{5,71},{6,4},{7,69},{8,10},{9,75},... | collective-permute-start | bytes 6291464 | tf_op jit(solution)/shard_map/ppermute | solution.py:23
  67.2 26.5 %collective-permute-start.13 = (f32[4,17,32,128]{3,2,1,0:T(8,128)S(1)}, f32[4,17,32,128]{3,2,1,0:T(8,128)}, u32[]{:S(2)}, u32[]{:S(2)}) collective-permute-start(f32[4,17,32,128]{3,2,1,0:T(8,128)S(1)} %collective-permute-done.10.refs_2_), channel_id=1, source_target_pairs={{0,4},{1,13},{2,6},{3,15},{4,0},{5,9},{6,2},{7,11},{8,12},{9,5},{1... | collective-permute-start | bytes 3342344 | tf_op jit(solution)/shard_map/ppermute | solution.py:23
  67.8 25.8 %collective-permute-start.14 = (f32[4,17,32,128]{3,2,1,0:T(8,128)}, f32[4,17,32,128]{3,2,1,0:T(8,128)}, u32[]{:S(2)}, u32[]{:S(2)}) collective-permute-start(f32[4,17,32,128]{3,2,1,0:T(8,128)} %copy-done.10), channel_id=1, source_target_pairs={{0,16},{1,49},{2,18},{3,51},{4,20},{5,53},{6,22},{7,55},{8,24},{9,... | collective-permute-start | bytes 3342344 | tf_op jit(solution)/shard_map/ppermute | solution.py:23
  70.6 1.2 copy-start.3
  89.9 1.0 copy-start.5
  92.9 18.0 %collective-permute-start.18 = (f32[16,2,128,128]{3,2,1,0:T(8,128)}, f32[16,2,128,128]{3,2,1,0:T(8,128)}, u32[]{:S(2)}, u32[]{:S(2)}) collective-permute-start(f32[16,2,128,128]{3,2,1,0:T(8,128)} %collective-permute-done.17.far0), channel_id=1, source_target_pairs={{0,1},{1,0},{2,3},{3,2},{4,5},{5,4},{6,7},{7,6},{8,9},{9,8},{10,11... | collective-permute-start | bytes 6291464 | tf_op jit(solution)/shard_map/ppermute | solution.py:23
  93.7 1.2 copy-start.6
  110.0 1.0 copy-start.4
  122.1 22.0 %copy-start.8 = (s32[1,32]{1,0:T(1,128)S(1)}, s32[1,32]{1,0:T(1,128)}, u32[]{:S(2)}) copy-start(s32[1,32]{1,0:T(1,128)} %label_ref.1) | copy-start | bytes 388
  122.1 24.4 %copy-start.1 = (f32[1,32,128,128]{3,2,1,0:T(8,128)S(1)}, f32[1,32,128,128]{3,2,1,0:T(8,128)}, u32[]{:S(2)}) copy-start(f32[1,32,128,128]{3,2,1,0:T(8,128)} %param.5) | copy-start | bytes 6291460
  142.1 4.4 %collective-permute-start.19 = (f32[32,2,32,128]{3,2,1,0:T(8,128)S(1)}, f32[32,2,32,128]{3,2,1,0:T(8,128)}, u32[]{:S(2)}, u32[]{:S(2)}) collective-permute-start(f32[32,2,32,128]{3,2,1,0:T(8,128)S(1)} %all_to_all.5), channel_id=1, source_target_pairs={{0,1},{1,0},{2,3},{3,2},{4,5},{5,4},{6,7},{7,6},{8,9},{9,8},{10,11... | collective-permute-start | bytes 3145736 | tf_op jit(solution)/shard_map/ppermute | solution.py:23
  149.7 5.3 %collective-permute-start.20 = (f32[128,128]{1,0:T(8,128)S(1)}, f32[128,128]{1,0:T(8,128)S(1)}, u32[]{:S(2)}, u32[]{:S(2)}) collective-permute-start(f32[128,128]{1,0:T(8,128)S(1)} %share.1), channel_id=1, source_target_pairs={{0,1},{1,0},{2,3},{3,2},{4,5},{5,4},{6,7},{7,6},{8,9},{9,8},{10,11... | collective-permute-start | bytes 196616 | tf_op jit(solution)/shard_map/ppermute | solution.py:23
  150.1 4.9 %collective-permute-start.21 = (f32[128,128]{1,0:T(8,128)S(1)}, f32[128,128]{1,0:T(8,128)S(1)}, u32[]{:S(2)}, u32[]{:S(2)}) collective-permute-start(f32[128,128]{1,0:T(8,128)S(1)} %share.1), channel_id=1, source_target_pairs={{0,2},{1,3},{2,0},{3,1},{4,6},{5,7},{6,4},{7,5},{8,10},{9,11},{10,... | collective-permute-start | bytes 196616 | tf_op jit(solution)/shard_map/ppermute | solution.py:23
  151.8 4.2 %collective-permute-start.22 = (f32[128,128]{1,0:T(8,128)S(1)}, f32[128,128]{1,0:T(8,128)S(1)}, u32[]{:S(2)}, u32[]{:S(2)}) collective-permute-start(f32[128,128]{1,0:T(8,128)S(1)} %share.1), channel_id=1, source_target_pairs={{0,3},{1,2},{2,1},{3,0},{4,7},{5,6},{6,5},{7,4},{8,11},{9,10},{10,... | collective-permute-start | bytes 196616 | tf_op jit(solution)/shard_map/ppermute | solution.py:23

commit v4 on v2

--- a/solution.py
+++ b/solution.py
@@ -92,12 +92,13 @@
 
 
 def first_kernel(nodes, where, *refs):
-    parts, sigmas = refs[:8], refs[8:14]
-    out_ref, hi_out, lo_out, hi_ref, lo_ref, held, total, labels, arrived, left, read = refs[14:]
+    out_ref, hi_out, lo_out, hi_ref, lo_ref, w, held, total, labels, landed, arrived, left, read = refs[14:]
+    parts = [pltpu.make_async_copy(t, w.at[i], landed.at[i]) for i, t in enumerate(refs[:8])]
+    sigmas = refs[8:14]
     texts = [
-        pltpu.make_async_copy(t.at[:, 16, pl.ds(0, 8)], labels.at[i], read.at[i]) for i, t in enumerate(parts)
+        pltpu.make_async_copy(t.at[:, 16, pl.ds(0, 8)], labels.at[i], read.at[i]) for i, t in enumerate(refs[:8])
     ]
-    for copy in texts:
+    for copy in texts + parts:
         copy.start()
     copies = [pltpu.make_async_copy(t, held.at[i], arrived.at[i]) for i, t in enumerate(sigmas)]
     for copy in copies:
@@ -112,11 +113,13 @@
     for copy in texts:
         copy.wait()
     for i, part in enumerate(parts):
-        def node(n, carry, i=i, part=part):
+        part.wait()
+
+        def node(n, carry, i=i):
             rows = pl.ds(pl.multiple_of(nodes[i * 4 + n] * Q, Q), Q)
             for k in range(16):
                 at = labels[i, n, 0, i // 4 * 16 + k].astype(jnp.int32)
-                hi, lo = split(part[n, k])
+                hi, lo = split(w[i, n, k])
                 hi_ref[at, rows, :] = hi
                 lo_ref[at, rows, :] = lo
             return carry
@@ -163,62 +166,67 @@
     rows = 16 * Q
     return pl.pallas_call(
         first_kernel,
-        in_specs=[SCALARS] * 2 + [ON_CHIP] * 8 + [whole] * 6,
+        in_specs=[SCALARS] * 2 + [whole] * 14,
         out_specs=[ON_CHIP, whole, whole],
         out_shape=[jax.ShapeDtypeStruct((2, 16, 2, Q, B), F32)] + [jax.ShapeDtypeStruct((32, rows, B), BF16)] * 2,
         scratch_shapes=[
             pltpu.VMEM((64, rows, B), BF16),
             pltpu.VMEM((64, rows, B), BF16),
+            pltpu.VMEM((8, 4, 17, Q, B), F32),
             pltpu.VMEM((6, 16, 2, B, B), F32),
             pltpu.VMEM((rows, 4 * B), F32),
             pltpu.SMEM((8, 4, 8, B), F32),
+            pltpu.SemaphoreType.DMA((8,)),
             pltpu.SemaphoreType.DMA((6,)),
             pltpu.SemaphoreType.DMA((4,)),
             pltpu.SemaphoreType.DMA((8,)),
         ],
-        compiler_params=pltpu.CompilerParams(vmem_limit_bytes=38 << 20),
+        compiler_params=pltpu.CompilerParams(vmem_limit_bytes=48 << 20),
         cost_estimate=pl.CostEstimate(flops=9 << 31, bytes_accessed=32 << 20, transcendentals=0),
         name="first_sums",
     )(nodes, where, *parts, *sigmas)
 
 
-def last_kernel(where, hi0, hi1, lo0, lo1, far0, far1, start, out_ref, total):
-    step, at = pl.program_id(0), where[0]
-
-    @pl.when(step == 0)
-    def _():
-        for n in range(2):
-            total[:, n * B : (n + 1) * B] = start[at, :, n].reshape(16 * Q, B)
-
-    weights = [[t[i] for t in pair for i in range(MANY)] for pair in ((hi0, hi1), (lo0, lo1))]
-    total[...] += gained(weights, [(far0, far1)], 1)
-
-    @pl.when(step == pl.num_programs(0) - 1)
-    def _():
-        for n in range(2):
-            out_ref[at, :, n] = total[:, n * B : (n + 1) * B].reshape(16, Q, B)
-        out_ref[1 - at] = start[1 - at]
+def last_kernel(where, hi, lo, far0, far1, start, out_ref, weights, held, total, arrived):
+    at, steps = where[0], 16 // MANY
+    copies = []
+    for t in range(steps):
+        block = lambda first: pl.ds(first + t * MANY, MANY)
+        pairs = [(ref.at[block(16 * core)], weights.at[i, block(16 * core)]) for i, ref in enumerate((hi, lo)) for core in range(2)]
+        pairs += [(ref.at[block(0)], held.at[core, block(0)]) for core, ref in enumerate((far0, far1))]
+        copies.append([pltpu.make_async_copy(*pair, arrived.at[t, i]) for i, pair in enumerate(pairs)])
+        for copy in copies[-1]:
+            copy.start()
+    out_ref[1 - at] = start[1 - at]
+    for n in range(2):
+        total[:, n * B : (n + 1) * B] = start[at, :, n].reshape(16 * Q, B)
+    for t in range(steps):
+        for copy in copies[t]:
+            copy.wait()
+        each = range(t * MANY, (t + 1) * MANY)
+        w = [[weights[i, 16 * core + k] for core in range(2) for k in each] for i in range(2)]
+        total[...] += gained(w, [[held.at[core, pl.ds(t * MANY, MANY)] for core in range(2)]], 1)
+    for n in range(2):
+        out_ref[at, :, n] = total[:, n * B : (n + 1) * B].reshape(16, Q, B)
 
 
 def last_sums(at, hi, lo, far, start):
-    rows = 16 * Q
-    w = [pl.BlockSpec((MANY, rows, B), lambda i, w, core=core: (core * (16 // MANY) + i, 0, 0)) for core in range(2)]
-    s = pl.BlockSpec((MANY, 2, B, B), lambda i, w: (i, 0, 0, 0))
-    whole = pl.BlockSpec(start.shape, lambda i, w: (0,) * 5)
+    rows, away = 16 * Q, pl.BlockSpec(memory_space=pl.ANY)
     return pl.pallas_call(
         last_kernel,
-        grid_spec=pltpu.PrefetchScalarGridSpec(
-            num_scalar_prefetch=1,
-            grid=(16 // MANY,),
-            in_specs=w + w + [s, s, whole],
-            out_specs=whole,
-            scratch_shapes=[pltpu.VMEM((rows, 2 * B), F32)],
-        ),
+        in_specs=[SCALARS] + [away] * 4 + [ON_CHIP],
+        out_specs=ON_CHIP,
+        scratch_shapes=[
+            pltpu.VMEM((2, 32, rows, B), BF16),
+            pltpu.VMEM((2, 16, 2, B, B), F32),
+            pltpu.VMEM((rows, 2 * B), F32),
+            pltpu.SemaphoreType.DMA((16 // MANY, 6)),
+        ],
         out_shape=jax.ShapeDtypeStruct(start.shape, F32),
         compiler_params=pltpu.CompilerParams(vmem_limit_bytes=56 << 20),
         cost_estimate=pl.CostEstimate(flops=3 << 31, bytes_accessed=14 << 20, transcendentals=0),
         name="last_sums",
-    )(at[None], hi, hi, lo, lo, *far, start)
+    )(at[None], hi, lo, *far, start)
 
 
 def rows_of(core, a, kept, came):
@@ -273,15 +281,16 @@
     x1 = swap(sigma, X1, X3)
     a = jnp.stack([first, *ring(first, Z1, Z3)])
     b = jnp.stack([second, *ring(second, Y1, Y3)])
-    sigma, x1, a, b = lax.optimization_barrier((sigma, x1, a, b))
+    other = lambda t: swap(t, CORE)
+    sigma, x1, a, b, sigma_other = lax.optimization_barrier((sigma, x1, a, b, other(sigma)))
     x2 = swap(sigma, X3, X1)
     a2, b2 = swap(a, Y3, Y1), swap(b, Z3, Z1)
-    a1, b1 = swap(after(a, a2), Y1, Y3), swap(after(b, b2), Z1, Z3)
+    a1, b1 = swap(a, Y1, Y3), swap(b, Z1, Z3)
+    x2, a1, a2, b1, b2 = lax.optimization_barrier((x2, a1, a2, b1, b2))
+    x3 = swap(x2, X1, X3)
     a3, b3 = swap(a2, Y1, Y3), swap(b2, Z1, Z3)
-    sigma_other, x1_other = swap(sigma, CORE), swap(x1, CORE)
-    x3 = swap(after(x2, a2, b2, sigma_other, x1_other), X1, X3)
-    sigmas = (x1, swap(x2, CORE), x2, x1_other, sigma, sigma_other)
-    return sigmas, (x3, swap(x3, CORE)), (a, a1, a2, a3, b, b1, b2, b3)
+    sigmas = (x1, other(x2), x2, other(x1), sigma, sigma_other)
+    return sigmas, x3, (a, a1, a2, a3, b, b1, b2, b3)
 
 
 def local(sigma_anc, panel_u, structure, diag_inv):
@@ -301,7 +310,8 @@
     base = lambda x: [32 * x + 16 * core, 32 * x + 16 * (1 - core)]
     where = jnp.stack(base(1 - x_lo) + base(x_lo) + [x_hi ^ core, x_hi])
     part, hi, lo = first_sums(nodes, where, pieces, sigmas)
-    part = last_sums(1 - x_hi, hi, lo, far, part)
+    far = after(far, part)
+    part = last_sums(1 - x_hi, hi, lo, (far, swap(far, CORE)), part)
     groups = [
         [h * 64 + q * 4 + l * 2 + c for l in range(2) for q in range(16)] for h in range(2) for c in range(2)
     ]

time: 163 us -> 156 us (0.957)
  waiting for transfers between devices: 46.8 us -> 38.2 us
  local copies, waits for them, and re-layouts: 7.65 us -> 2.53 us
  Pallas kernels: 36.2 us -> 39.9 us
  starting transfers between devices: 47.7 us -> 50.2 us
    ppermute x23, waiting for transfers between devices: 46.8 us -> 38.2 us  [swap(): lax.ppermute(x, AXES, [(i, i ^ (odd if i % 2 else even)) for i in range(1...]
    unnamed x22 -> x18, local copies, waits for them, and re-layouts: 7.48 us -> 2.36 us
    pallas_call x2, Pallas kernels: 27 us -> 30.1 us  [the longest x1 18.9 us: first_sums(): pl.pallas_call(first_kernel, in_specs=[SCALARS] * 2 + [whole] * 14, out_s...]
    ppermute x23, starting transfers between devices: 47.7 us -> 50.2 us  [swap(): lax.ppermute(x, AXES, [(i, i ^ (odd if i % 2 else even)) for i in range(1...]
  transfers between devices with their start and end apart: 23 -> 23, of which waited for: 13 -> 12; matrix products, arithmetic and copies ran while one was open for 1% -> 1% of each run, Pallas kernels for 13% -> 14%
where the time goes in v4:
time: 156 us; the launch traced here: 155 us
  starting transfers between devices  50.2 us (32%)
  Pallas kernels  39.9 us (26%)
  waiting for transfers between devices  38.2 us (24%)
  blocking collectives  21.2 us (14%)
  local copies, waits for them, and re-layouts  2.53 us (2%)
    ppermute x23, starting transfers between devices, swap(): lax.ppermute(x, AXES, [(i, i ^ (odd if i % 2 else even)) for i in range(1...  50.2 us
    ppermute x23, waiting for transfers between devices, swap(): lax.ppermute(x, AXES, [(i, i ^ (odd if i % 2 else even)) for i in range(1...  38.2 us
    all_to_all x1, blocking collectives, local(): lax.all_to_all(part.reshape(32, 2, Q, B), AXES, 0, 0, axis_index_groups=g...  21.2 us
    pallas_call x1, Pallas kernels, first_sums(): pl.pallas_call(first_kernel, in_specs=[SCALARS] * 2 + [whole] * 14, out_s...  18.9 us
    pallas_call x1, Pallas kernels, last_sums(): pl.pallas_call(last_kernel, in_specs=[SCALARS] + [away] * 4 + [ON_CHIP],...  11.1 us
    pallas_call x2, Pallas kernels, on_one(): pl.pallas_call(kernel, grid_spec=pltpu.PrefetchScalarGridSpec(num_scalar_...  6.58 us
    pallas_call x1, Pallas kernels, cut(): pl.pallas_call(cut_kernel, grid_spec=pltpu.PrefetchScalarGridSpec(num_sca...  3.27 us
  transfers between devices with their start and end apart: 23, of which 12 were waited for; matrix products, arithmetic and copies ran while one was open for 1% of the time, Pallas kernels for 14%

profile of v4, /device:TPU:1, one launch (start us, length us, event | category | flops | bytes accessed | tf_op | source)
XLA Modules:
  0.0 155.1 jit_solution(9753818120071216311)
XLA Ops:
  0.6 0.0 copy-start
  0.6 3.3 %cut.1 = (f32[17,32,128]{2,1,0:T(8,128)}, f32[17,32,128]{2,1,0:T(8,128)}) custom-call(s32[1]{0:T(128)} %bitcast.11.where, f32[32,128,128]{2,1,0:T(8,128)} %bitcast.32, s32[1,32]{1,0:T(1,128)} %label_ref.1), custom_call_target="tpu_custom_call" | custom-call | tf_op jit(solution)/shard_map/cut/pallas_call | solution.py:62
  3.9 3.4 %collective-permute-start = (f32[16,2,128,128]{3,2,1,0:T(8,128)}, f32[16,2,128,128]{3,2,1,0:T(8,128)}, u32[]{:S(2)}, u32[]{:S(2)}) collective-permute-start(f32[16,2,128,128]{3,2,1,0:T(8,128)} %refs_12_), channel_id=1, source_target_pairs={{0,2},{1,67},{2,0},{3,65},{4,6},{5,71},{6,4},{7,69},{8,10},{9,75},... | collective-permute-start | bytes 6291464 | tf_op jit(solution)/shard_map/ppermute | solution.py:23
  7.3 0.0 collective-permute-start.7
  7.3 1.3 collective-permute-start.5
  8.6 1.9 %collective-permute-start.4 = (f32[17,32,128]{2,1,0:T(8,128)}, f32[17,32,128]{2,1,0:T(8,128)S(1)}, u32[]{:S(2)}, u32[]{:S(2)}) collective-permute-start(f32[17,32,128]{2,1,0:T(8,128)} %get-tuple-element.25), channel_id=1, source_target_pairs={{0,4},{1,13},{2,6},{3,15},{4,0},{5,9},{6,2},{7,11},{8,12},{9,5},{1... | collective-permute-start | bytes 835592 | tf_op jit(solution)/shard_map/ppermute | solution.py:23
  10.5 1.6 %collective-permute-start.2 = (f32[17,32,128]{2,1,0:T(8,128)}, f32[17,32,128]{2,1,0:T(8,128)S(1)}, u32[]{:S(2)}, u32[]{:S(2)}) collective-permute-start(f32[17,32,128]{2,1,0:T(8,128)} %get-tuple-element.24), channel_id=1, source_target_pairs={{0,48},{1,17},{2,50},{3,19},{4,52},{5,21},{6,54},{7,23},{8,56},{9,... | collective-permute-start | bytes 835592 | tf_op jit(solution)/shard_map/ppermute | solution.py:23
  12.1 1.2 collective-permute-done.5
  13.3 4.5 %collective-permute-start.6 = (f32[17,32,128]{2,1,0:T(8,128)S(1)}, f32[17,32,128]{2,1,0:T(8,128)S(1)}, u32[]{:S(2)}, u32[]{:S(2)}) collective-permute-start(f32[17,32,128]{2,1,0:T(8,128)S(1)} %collective-permute-done.5), channel_id=1, source_target_pairs={{0,4},{1,13},{2,6},{3,15},{4,0},{5,9},{6,2},{7,11},{8,12},{9,5},{1... | collective-permute-start | bytes 835592 | tf_op jit(solution)/shard_map/ppermute | solution.py:23
  17.8 0.5 collective-permute-done.4
  18.3 3.8 %collective-permute-start.1 = (f32[17,32,128]{2,1,0:T(8,128)}, f32[17,32,128]{2,1,0:T(8,128)S(1)}, u32[]{:S(2)}, u32[]{:S(2)}) collective-permute-start(f32[17,32,128]{2,1,0:T(8,128)} %get-tuple-element.24), channel_id=1, source_target_pairs={{0,16},{1,49},{2,18},{3,51},{4,20},{5,53},{6,22},{7,55},{8,24},{9,... | collective-permute-start | bytes 835592 | tf_op jit(solution)/shard_map/ppermute | solution.py:23
  22.1 0.0 collective-permute-done.2
  22.1 0.0 collective-permute-start.3
  22.1 0.0 collective-permute-done.6
  22.1 1.1 pad_maximum_fusion.1.refs_4_
  23.2 3.0 %collective-permute-done.1 = f32[17,32,128]{2,1,0:T(8,128)S(1)} collective-permute-done((f32[17,32,128]{2,1,0:T(8,128)}, f32[17,32,128]{2,1,0:T(8,128)S(1)}, u32[]{:S(2)}, u32[]{:S(2)}) %collective-permute-start.1) | collective-permute-done | bytes 278560 | tf_op jit(solution)/shard_map/ppermute | solution.py:23
  26.2 3.0 %collective-permute-done.3 = f32[17,32,128]{2,1,0:T(8,128)S(1)} collective-permute-done((f32[17,32,128]{2,1,0:T(8,128)S(1)}, f32[17,32,128]{2,1,0:T(8,128)S(1)}, u32[]{:S(2)}, u32[]{:S(2)}) %collective-permute-start.3) | collective-permute-done | bytes 278560 | tf_op jit(solution)/shard_map/ppermute | solution.py:23
  29.2 0.1 pad_maximum_fusion.refs_0_
  29.3 1.7 %collective-permute-done.refs_8_ = f32[16,2,128,128]{3,2,1,0:T(8,128)} collective-permute-done((f32[16,2,128,128]{3,2,1,0:T(8,128)}, f32[16,2,128,128]{3,2,1,0:T(8,128)}, u32[]{:S(2)}, u32[]{:S(2)}) %collective-permute-start) | collective-permute-done | bytes 2097184 | tf_op jit(solution)/shard_map/ppermute | solution.py:23
  31.0 0.0 collective-permute-done.7.refs_13_
  31.0 0.5 collective-permute-start.8
  31.5 1.3 collective-permute-start.10
  32.8 3.8 %collective-permute-start.11 = (f32[4,17,32,128]{3,2,1,0:T(8,128)S(1)}, f32[4,17,32,128]{3,2,1,0:T(8,128)S(1)}, u32[]{:S(2)}, u32[]{:S(2)}) collective-permute-start(f32[4,17,32,128]{3,2,1,0:T(8,128)S(1)} %pad_maximum_fusion.1.refs_4_), channel_id=1, source_target_pairs={{0,16},{1,49},{2,18},{3,51},{4,20},{5,53},{6,22},{7,55},{8,24},{9,... | collective-permute-start | bytes 3342344 | tf_op jit(solution)/shard_map/ppermute | solution.py:23
  36.6 0.0 collective-permute-start.12
  36.6 1.9 %collective-permute-start.9 = (f32[4,17,32,128]{3,2,1,0:T(8,128)S(1)}, f32[4,17,32,128]{3,2,1,0:T(8,128)S(1)}, u32[]{:S(2)}, u32[]{:S(2)}) collective-permute-start(f32[4,17,32,128]{3,2,1,0:T(8,128)S(1)} %pad_maximum_fusion.refs_0_), channel_id=1, source_target_pairs={{0,4},{1,13},{2,6},{3,15},{4,0},{5,9},{6,2},{7,11},{8,12},{9,5},{1... | collective-permute-start | bytes 3342344 | tf_op jit(solution)/shard_map/ppermute | solution.py:23
  38.5 9.1 %collective-permute-done.10.refs_2_ = f32[4,17,32,128]{3,2,1,0:T(8,128)S(1)} collective-permute-done((f32[4,17,32,128]{3,2,1,0:T(8,128)S(1)}, f32[4,17,32,128]{3,2,1,0:T(8,128)S(1)}, u32[]{:S(2)}, u32[]{:S(2)}) %collective-permute-start.10) | collective-permute-done | bytes 1114144 | tf_op jit(solution)/shard_map/ppermute | solution.py:23
  47.6 14.2 %collective-permute-start.16 = (f32[16,2,128,128]{3,2,1,0:T(8,128)}, f32[16,2,128,128]{3,2,1,0:T(8,128)}, u32[]{:S(2)}, u32[]{:S(2)}) collective-permute-start(f32[16,2,128,128]{3,2,1,0:T(8,128)} %collective-permute-done.refs_8_), channel_id=1, source_target_pairs={{0,1},{1,0},{2,3},{3,2},{4,5},{5,4},{6,7},{7,6},{8,9},{9,8},{10,11... | collective-permute-start | bytes 6291464 | tf_op jit(solution)/shard_map/ppermute | solution.py:23
  61.8 0.0 collective-permute-done.11.refs_5_
  61.8 0.0 collective-permute-done.12.refs_6_
  61.8 0.7 collective-permute-done.9.refs_1_
  62.5 0.0 collective-permute-done.8.refs_10_
  62.5 1.1 collective-permute-start.15
  63.7 2.6 %collective-permute-start.13 = (f32[4,17,32,128]{3,2,1,0:T(8,128)S(1)}, f32[4,17,32,128]{3,2,1,0:T(8,128)}, u32[]{:S(2)}, u32[]{:S(2)}) collective-permute-start(f32[4,17,32,128]{3,2,1,0:T(8,128)S(1)} %collective-permute-done.10.refs_2_), channel_id=1, source_target_pairs={{0,4},{1,13},{2,6},{3,15},{4,0},{5,9},{6,2},{7,11},{8,12},{9,5},{1... | collective-permute-start | bytes 3342344 | tf_op jit(solution)/shard_map/ppermute | solution.py:23
  66.2 1.6 %collective-permute-start.14 = (f32[4,17,32,128]{3,2,1,0:T(8,128)}, f32[4,17,32,128]{3,2,1,0:T(8,128)}, u32[]{:S(2)}, u32[]{:S(2)}) collective-permute-start(f32[4,17,32,128]{3,2,1,0:T(8,128)} %collective-permute-done.12.refs_6_), channel_id=1, source_target_pairs={{0,16},{1,49},{2,18},{3,51},{4,20},{5,53},{6,22},{7,55},{8,24},{9,... | collective-permute-start | bytes 3342344 | tf_op jit(solution)/shard_map/ppermute | solution.py:23
  67.8 0.1 xor_multiply_fusion
  67.9 2.3 %collective-permute-start.17 = (f32[16,2,128,128]{3,2,1,0:T(8,128)}, f32[16,2,128,128]{3,2,1,0:T(8,128)}, u32[]{:S(2)}, u32[]{:S(2)}) collective-permute-start(f32[16,2,128,128]{3,2,1,0:T(8,128)} %collective-permute-done.8.refs_10_), channel_id=1, source_target_pairs={{0,2},{1,67},{2,0},{3,65},{4,6},{5,71},{6,4},{7,69},{8,10},{9,75},... | collective-permute-start | bytes 6291464 | tf_op jit(solution)/shard_map/ppermute | solution.py:23
  70.2 0.1 broadcast_add_fusion.1
  70.3 0.1 reshape.231.nodes
  70.3 0.1 stack.75.where
  70.4 0.0 collective-permute-done.16.refs_11_
  70.4 8.9 %collective-permute-done.13.refs_3_ = f32[4,17,32,128]{3,2,1,0:T(8,128)} collective-permute-done((f32[4,17,32,128]{3,2,1,0:T(8,128)S(1)}, f32[4,17,32,128]{3,2,1,0:T(8,128)}, u32[]{:S(2)}, u32[]{:S(2)}) %collective-permute-start.13) | collective-permute-done | bytes 1114144 | tf_op jit(solution)/shard_map/ppermute | solution.py:23
  79.3 2.8 %collective-permute-done.14.refs_7_ = f32[4,17,32,128]{3,2,1,0:T(8,128)} collective-permute-done((f32[4,17,32,128]{3,2,1,0:T(8,128)}, f32[4,17,32,128]{3,2,1,0:T(8,128)}, u32[]{:S(2)}, u32[]{:S(2)}) %collective-permute-start.14) | collective-permute-done | bytes 1114144 | tf_op jit(solution)/shard_map/ppermute | solution.py:23
  82.1 18.9 %first_sums.1 = (f32[2,16,2,32,128]{4,3,2,1,0:T(8,128)S(1)}, bf16[32,512,128]{2,1,0:T(8,128)(2,1)}, bf16[32,512,128]{2,1,0:T(8,128)(2,1)}) custom-call(s32[32]{0:T(128)S(1)} %reshape.231.nodes, s32[6]{0:T(128)S(1)} %stack.75.where, f32[4,17,32,128]{3,2,1,0:T(8,128)S(1)} %pad_maximum_fusion.refs_0_, f32[4,17,32,128]{3,2,1,0:T(8,128)S(1)} %collective-permute-done.9.refs_1_, ...), custom_call_target="tpu_custom_call" | custom-call | flops 19327352832 | bytes 33554432 | tf_op jit(solution)/shard_map/first_sums/pallas_call | solution.py:167
  101.1 0.0 copy-start.2
  101.1 1.0 copy-done.2
  102.0 0.0 collective-permute-done.17.far0
  102.1 0.0 collective-permute-start.18
  102.1 4.4 %collective-permute-done.18.far1 = f32[16,2,128,128]{3,2,1,0:T(8,128)S(1)} collective-permute-done((f32[16,2,128,128]{3,2,1,0:T(8,128)}, f32[16,2,128,128]{3,2,1,0:T(8,128)S(1)}, u32[]{:S(2)}, u32[]{:S(2)}) %collective-permute-start.18) | collective-permute-done | bytes 2097184 | tf_op jit(solution)/shard_map/ppermute | solution.py:23
  106.4 1.4 copy-done.7
  107.8 11.1 %last_sums.1 = f32[2,16,2,32,128]{4,3,2,1,0:T(8,128)} custom-call(s32[1]{0:T(128)} %bitcast.2.where, bf16[32,512,128]{2,1,0:T(8,128)(2,1)} %get-tuple-element.36.hi, bf16[32,512,128]{2,1,0:T(8,128)(2,1)} %get-tuple-element.37.lo, f32[16,2,128,128]{3,2,1,0:T(8,128)} %collective-permute-done.17.far0, f32[16,2,128,128]{3,2,1,0:T(8,128)} %copy-done.7, ...), custom_call_target="tpu_custom_call" | custom-call | flops 6442450944 | bytes 14680064 | tf_op jit(solution)/shard_map/last_sums/pallas_call | solution.py:215
  118.9 0.0 copy-start.5
  118.9 0.0 copy-start.1
  118.9 21.2 %all_to_all.5 = f32[32,2,32,128]{3,2,1,0:T(8,128)S(1)} all-to-all(f32[32,2,32,128]{3,2,1,0:T(8,128)} %bitcast.35), channel_id=1, replica_groups={{0,4,8,12,16,20,24,28,32,36,40,44,48,52,56,60,2,6,10,14,18,22,26,30,34,..., dimensions={0} | all-to-all | bytes 2097152 | tf_op jit(solution)/shard_map/all_to_all | solution.py:318
  140.1 2.3 %collective-permute-start.19 = (f32[32,2,32,128]{3,2,1,0:T(8,128)S(1)}, f32[32,2,32,128]{3,2,1,0:T(8,128)}, u32[]{:S(2)}, u32[]{:S(2)}) collective-permute-start(f32[32,2,32,128]{3,2,1,0:T(8,128)S(1)} %all_to_all.5), channel_id=1, source_target_pairs={{0,1},{1,0},{2,3},{3,2},{4,5},{5,4},{6,7},{7,6},{8,9},{9,8},{10,11... | collective-permute-start | bytes 3145736 | tf_op jit(solution)/shard_map/ppermute | solution.py:23
  142.4 0.2 select_reduce_fusion
  142.5 2.2 %collective-permute-done.19 = f32[32,2,32,128]{3,2,1,0:T(8,128)} collective-permute-done((f32[32,2,32,128]{3,2,1,0:T(8,128)S(1)}, f32[32,2,32,128]{3,2,1,0:T(8,128)}, u32[]{:S(2)}, u32[]{:S(2)}) %collective-permute-start.19) | collective-permute-done | bytes 1048608 | tf_op jit(solution)/shard_map/ppermute | solution.py:23
  144.8 3.5 %share.1 = f32[128,128]{1,0:T(8,128)S(1)} custom-call(s32[1]{0:T(128)} %bitcast.where, s32[16]{0:T(128)S(1)} %broadcast_add_fusion.2.picks, f32[32,128,128]{2,1,0:T(8,128)S(1)} %bitcast.33, f32[2,2,8,2,32,128]{5,4,3,2,1,0:T(8,128)S(1)} %bitcast.30, f32[2,2,8,2,32,128]{5,4,3,2,1,0:T(8,128)} %bitcast.23.came), custom_call_target="tpu_custom_call" | custom-call | flops 134217728 | bytes 4194304 | tf_op jit(solution)/shard_map/share/pallas_call | solution.py:259
  148.3 0.1 collective-permute-start.20
  148.4 1.7 %collective-permute-start.21 = (f32[128,128]{1,0:T(8,128)S(1)}, f32[128,128]{1,0:T(8,128)S(1)}, u32[]{:S(2)}, u32[]{:S(2)}) collective-permute-start(f32[128,128]{1,0:T(8,128)S(1)} %share.1), channel_id=1, source_target_pairs={{0,2},{1,3},{2,0},{3,1},{4,6},{5,7},{6,4},{7,5},{8,10},{9,11},{10,... | collective-permute-start | bytes 196616 | tf_op jit(solution)/shard_map/ppermute | solution.py:23
  150.1 0.4 collective-permute-start.22
  150.5 3.1 %panel.1 = f32[16,128,128]{2,1,0:T(8,128)} custom-call(s32[1]{0:T(128)} %bitcast.where, s32[16]{0:T(128)S(1)} %broadcast_add_fusion.2.picks, f32[2,2,8,2,32,128]{5,4,3,2,1,0:T(8,128)S(1)} %bitcast.31, f32[2,2,8,2,32,128]{5,4,3,2,1,0:T(8,128)} %bitcast.23.came), custom_call_target="tpu_custom_call" | custom-call | bytes 4194304 | tf_op jit(solution)/shard_map/panel/pallas_call | solution.py:259
  153.6 0.0 collective-permute-done.20
  153.6 0.6 collective-permute-done.22
  154.2 0.9 fusion.1
  (19 shorter events, 0.1 us)
Async XLA Ops:
  0.6 153.6 %copy-start = (f32[1,128,128]{2,1,0:T(8,128)S(1)}, f32[1,128,128]{2,1,0:T(8,128)}, u32[]{:S(2)}) copy-start(f32[1,128,128]{2,1,0:T(8,128)} %param.7) | copy-start | bytes 196612
  3.9 27.1 %collective-permute-start = (f32[16,2,128,128]{3,2,1,0:T(8,128)}, f32[16,2,128,128]{3,2,1,0:T(8,128)}, u32[]{:S(2)}, u32[]{:S(2)}) collective-permute-start(f32[16,2,128,128]{3,2,1,0:T(8,128)} %refs_12_), channel_id=1, source_target_pairs={{0,2},{1,67},{2,0},{3,65},{4,6},{5,71},{6,4},{7,69},{8,10},{9,75},... | collective-permute-start | bytes 6291464 | tf_op jit(solution)/shard_map/ppermute | solution.py:23
  7.3 23.7 %collective-permute-start.7 = (f32[16,2,128,128]{3,2,1,0:T(8,128)}, f32[16,2,128,128]{3,2,1,0:T(8,128)S(1)}, u32[]{:S(2)}, u32[]{:S(2)}) collective-permute-start(f32[16,2,128,128]{3,2,1,0:T(8,128)} %refs_12_), channel_id=1, source_target_pairs={{0,1},{1,0},{2,3},{3,2},{4,5},{5,4},{6,7},{7,6},{8,9},{9,8},{10,11... | collective-permute-start | bytes 6291464 | tf_op jit(solution)/shard_map/ppermute | solution.py:23
  7.3 6.0 %collective-permute-start.5 = (f32[17,32,128]{2,1,0:T(8,128)}, f32[17,32,128]{2,1,0:T(8,128)S(1)}, u32[]{:S(2)}, u32[]{:S(2)}) collective-permute-start(f32[17,32,128]{2,1,0:T(8,128)} %get-tuple-element.25), channel_id=1, source_target_pairs={{0,12},{1,5},{2,14},{3,7},{4,8},{5,1},{6,10},{7,3},{8,4},{9,13},{1... | collective-permute-start | bytes 835592 | tf_op jit(solution)/shard_map/ppermute | solution.py:23
  8.6 9.8 %collective-permute-start.4 = (f32[17,32,128]{2,1,0:T(8,128)}, f32[17,32,128]{2,1,0:T(8,128)S(1)}, u32[]{:S(2)}, u32[]{:S(2)}) collective-permute-start(f32[17,32,128]{2,1,0:T(8,128)} %get-tuple-element.25), channel_id=1, source_target_pairs={{0,4},{1,13},{2,6},{3,15},{4,0},{5,9},{6,2},{7,11},{8,12},{9,5},{1... | collective-permute-start | bytes 835592 | tf_op jit(solution)/shard_map/ppermute | solution.py:23
  10.5 11.6 %collective-permute-start.2 = (f32[17,32,128]{2,1,0:T(8,128)}, f32[17,32,128]{2,1,0:T(8,128)S(1)}, u32[]{:S(2)}, u32[]{:S(2)}) collective-permute-start(f32[17,32,128]{2,1,0:T(8,128)} %get-tuple-element.24), channel_id=1, source_target_pairs={{0,48},{1,17},{2,50},{3,19},{4,52},{5,21},{6,54},{7,23},{8,56},{9,... | collective-permute-start | bytes 835592 | tf_op jit(solution)/shard_map/ppermute | solution.py:23
  13.3 8.9 %collective-permute-start.6 = (f32[17,32,128]{2,1,0:T(8,128)S(1)}, f32[17,32,128]{2,1,0:T(8,128)S(1)}, u32[]{:S(2)}, u32[]{:S(2)}) collective-permute-start(f32[17,32,128]{2,1,0:T(8,128)S(1)} %collective-permute-done.5), channel_id=1, source_target_pairs={{0,4},{1,13},{2,6},{3,15},{4,0},{5,9},{6,2},{7,11},{8,12},{9,5},{1... | collective-permute-start | bytes 835592 | tf_op jit(solution)/shard_map/ppermute | solution.py:23
  18.3 7.9 %collective-permute-start.1 = (f32[17,32,128]{2,1,0:T(8,128)}, f32[17,32,128]{2,1,0:T(8,128)S(1)}, u32[]{:S(2)}, u32[]{:S(2)}) collective-permute-start(f32[17,32,128]{2,1,0:T(8,128)} %get-tuple-element.24), channel_id=1, source_target_pairs={{0,16},{1,49},{2,18},{3,51},{4,20},{5,53},{6,22},{7,55},{8,24},{9,... | collective-permute-start | bytes 835592 | tf_op jit(solution)/shard_map/ppermute | solution.py:23
  22.1 7.1 %collective-permute-start.3 = (f32[17,32,128]{2,1,0:T(8,128)S(1)}, f32[17,32,128]{2,1,0:T(8,128)S(1)}, u32[]{:S(2)}, u32[]{:S(2)}) collective-permute-start(f32[17,32,128]{2,1,0:T(8,128)S(1)} %collective-permute-done.2), channel_id=1, source_target_pairs={{0,16},{1,49},{2,18},{3,51},{4,20},{5,53},{6,22},{7,55},{8,24},{9,... | collective-permute-start | bytes 835592 | tf_op jit(solution)/shard_map/ppermute | solution.py:23
  22.1 7.1 %copy-start.4 = (f32[17,32,128]{2,1,0:T(8,128)S(1)}, f32[17,32,128]{2,1,0:T(8,128)}, u32[]{:S(2)}) copy-start(f32[17,32,128]{2,1,0:T(8,128)} %get-tuple-element.24) | copy-start | bytes 835588
  23.2 13.3 %copy-start.3 = (f32[4,17,32,128]{3,2,1,0:T(8,128)}, f32[4,17,32,128]{3,2,1,0:T(8,128)S(1)}, u32[]{:S(2)}) copy-start(f32[4,17,32,128]{3,2,1,0:T(8,128)S(1)} %pad_maximum_fusion.1.refs_4_) | copy-start | bytes 3342340
  31.0 31.5 %copy-start.6 = (f32[16,2,128,128]{3,2,1,0:T(8,128)}, f32[16,2,128,128]{3,2,1,0:T(8,128)S(1)}, u32[]{:S(2)}) copy-start(f32[16,2,128,128]{3,2,1,0:T(8,128)S(1)} %collective-permute-done.7.refs_13_) | copy-start | bytes 6291460
  31.0 31.5 %collective-permute-start.8 = (f32[16,2,128,128]{3,2,1,0:T(8,128)}, f32[16,2,128,128]{3,2,1,0:T(8,128)}, u32[]{:S(2)}, u32[]{:S(2)}) collective-permute-start(f32[16,2,128,128]{3,2,1,0:T(8,128)} %refs_12_), channel_id=1, source_target_pairs={{0,66},{1,3},{2,64},{3,1},{4,70},{5,7},{6,68},{7,5},{8,74},{9,11},... | collective-permute-start | bytes 6291464 | tf_op jit(solution)/shard_map/ppermute | solution.py:23
  31.5 16.1 %collective-permute-start.10 = (f32[4,17,32,128]{3,2,1,0:T(8,128)S(1)}, f32[4,17,32,128]{3,2,1,0:T(8,128)S(1)}, u32[]{:S(2)}, u32[]{:S(2)}) collective-permute-start(f32[4,17,32,128]{3,2,1,0:T(8,128)S(1)} %pad_maximum_fusion.refs_0_), channel_id=1, source_target_pairs={{0,12},{1,5},{2,14},{3,7},{4,8},{5,1},{6,10},{7,3},{8,4},{9,13},{1... | collective-permute-start | bytes 3342344 | tf_op jit(solution)/shard_map/ppermute | solution.py:23
  32.8 29.0 %collective-permute-start.11 = (f32[4,17,32,128]{3,2,1,0:T(8,128)S(1)}, f32[4,17,32,128]{3,2,1,0:T(8,128)S(1)}, u32[]{:S(2)}, u32[]{:S(2)}) collective-permute-start(f32[4,17,32,128]{3,2,1,0:T(8,128)S(1)} %pad_maximum_fusion.1.refs_4_), channel_id=1, source_target_pairs={{0,16},{1,49},{2,18},{3,51},{4,20},{5,53},{6,22},{7,55},{8,24},{9,... | collective-permute-start | bytes 3342344 | tf_op jit(solution)/shard_map/ppermute | solution.py:23
  36.6 25.3 %collective-permute-start.12 = (f32[4,17,32,128]{3,2,1,0:T(8,128)S(1)}, f32[4,17,32,128]{3,2,1,0:T(8,128)}, u32[]{:S(2)}, u32[]{:S(2)}) collective-permute-start(f32[4,17,32,128]{3,2,1,0:T(8,128)S(1)} %pad_maximum_fusion.1.refs_4_), channel_id=1, source_target_pairs={{0,48},{1,17},{2,50},{3,19},{4,52},{5,21},{6,54},{7,23},{8,56},{9,... | collective-permute-start | bytes 3342344 | tf_op jit(solution)/shard_map/ppermute | solution.py:23
  36.6 25.9 %collective-permute-start.9 = (f32[4,17,32,128]{3,2,1,0:T(8,128)S(1)}, f32[4,17,32,128]{3,2,1,0:T(8,128)S(1)}, u32[]{:S(2)}, u32[]{:S(2)}) collective-permute-start(f32[4,17,32,128]{3,2,1,0:T(8,128)S(1)} %pad_maximum_fusion.refs_0_), channel_id=1, source_target_pairs={{0,4},{1,13},{2,6},{3,15},{4,0},{5,9},{6,2},{7,11},{8,12},{9,5},{1... | collective-permute-start | bytes 3342344 | tf_op jit(solution)/shard_map/ppermute | solution.py:23
  47.6 22.8 %collective-permute-start.16 = (f32[16,2,128,128]{3,2,1,0:T(8,128)}, f32[16,2,128,128]{3,2,1,0:T(8,128)}, u32[]{:S(2)}, u32[]{:S(2)}) collective-permute-start(f32[16,2,128,128]{3,2,1,0:T(8,128)} %collective-permute-done.refs_8_), channel_id=1, source_target_pairs={{0,1},{1,0},{2,3},{3,2},{4,5},{5,4},{6,7},{7,6},{8,9},{9,8},{10,11... | collective-permute-start | bytes 6291464 | tf_op jit(solution)/shard_map/ppermute | solution.py:23
  61.8 1.8 %copy-start.8 = (f32[4,17,32,128]{3,2,1,0:T(8,128)}, f32[4,17,32,128]{3,2,1,0:T(8,128)S(1)}, u32[]{:S(2)}) copy-start(f32[4,17,32,128]{3,2,1,0:T(8,128)S(1)} %collective-permute-done.11.refs_5_) | copy-start | bytes 3342340
  62.5 19.6 %collective-permute-start.15 = (f32[16,2,128,128]{3,2,1,0:T(8,128)}, f32[16,2,128,128]{3,2,1,0:T(8,128)}, u32[]{:S(2)}, u32[]{:S(2)}) collective-permute-start(f32[16,2,128,128]{3,2,1,0:T(8,128)} %collective-permute-done.8.refs_10_), channel_id=1, source_target_pairs={{0,1},{1,0},{2,3},{3,2},{4,5},{5,4},{6,7},{7,6},{8,9},{9,8},{10,11... | collective-permute-start | bytes 6291464 | tf_op jit(solution)/shard_map/ppermute | solution.py:23
  63.7 15.7 %collective-permute-start.13 = (f32[4,17,32,128]{3,2,1,0:T(8,128)S(1)}, f32[4,17,32,128]{3,2,1,0:T(8,128)}, u32[]{:S(2)}, u32[]{:S(2)}) collective-permute-start(f32[4,17,32,128]{3,2,1,0:T(8,128)S(1)} %collective-permute-done.10.refs_2_), channel_id=1, source_target_pairs={{0,4},{1,13},{2,6},{3,15},{4,0},{5,9},{6,2},{7,11},{8,12},{9,5},{1... | collective-permute-start | bytes 3342344 | tf_op jit(solution)/shard_map/ppermute | solution.py:23
  66.2 15.9 %collective-permute-start.14 = (f32[4,17,32,128]{3,2,1,0:T(8,128)}, f32[4,17,32,128]{3,2,1,0:T(8,128)}, u32[]{:S(2)}, u32[]{:S(2)}) collective-permute-start(f32[4,17,32,128]{3,2,1,0:T(8,128)} %collective-permute-done.12.refs_6_), channel_id=1, source_target_pairs={{0,16},{1,49},{2,18},{3,51},{4,20},{5,53},{6,22},{7,55},{8,24},{9,... | collective-permute-start | bytes 3342344 | tf_op jit(solution)/shard_map/ppermute | solution.py:23
  67.9 34.2 %collective-permute-start.17 = (f32[16,2,128,128]{3,2,1,0:T(8,128)}, f32[16,2,128,128]{3,2,1,0:T(8,128)}, u32[]{:S(2)}, u32[]{:S(2)}) collective-permute-start(f32[16,2,128,128]{3,2,1,0:T(8,128)} %collective-permute-done.8.refs_10_), channel_id=1, source_target_pairs={{0,2},{1,67},{2,0},{3,65},{4,6},{5,71},{6,4},{7,69},{8,10},{9,75},... | collective-permute-start | bytes 6291464 | tf_op jit(solution)/shard_map/ppermute | solution.py:23
  101.1 1.0 copy-start.2
  102.1 4.4 %collective-permute-start.18 = (f32[16,2,128,128]{3,2,1,0:T(8,128)}, f32[16,2,128,128]{3,2,1,0:T(8,128)S(1)}, u32[]{:S(2)}, u32[]{:S(2)}) collective-permute-start(f32[16,2,128,128]{3,2,1,0:T(8,128)} %collective-permute-done.17.far0), channel_id=1, source_target_pairs={{0,1},{1,0},{2,3},{3,2},{4,5},{5,4},{6,7},{7,6},{8,9},{9,8},{10,11... | collective-permute-start | bytes 6291464 | tf_op jit(solution)/shard_map/ppermute | solution.py:23
  106.4 1.4 copy-start.7
  118.9 23.5 %copy-start.5 = (s32[1,32]{1,0:T(1,128)S(1)}, s32[1,32]{1,0:T(1,128)}, u32[]{:S(2)}) copy-start(s32[1,32]{1,0:T(1,128)} %label_ref.1) | copy-start | bytes 388
  118.9 25.9 %copy-start.1 = (f32[1,32,128,128]{3,2,1,0:T(8,128)S(1)}, f32[1,32,128,128]{3,2,1,0:T(8,128)}, u32[]{:S(2)}) copy-start(f32[1,32,128,128]{3,2,1,0:T(8,128)} %param.5) | copy-start | bytes 6291460
  140.1 4.7 %collective-permute-start.19 = (f32[32,2,32,128]{3,2,1,0:T(8,128)S(1)}, f32[32,2,32,128]{3,2,1,0:T(8,128)}, u32[]{:S(2)}, u32[]{:S(2)}) collective-permute-start(f32[32,2,32,128]{3,2,1,0:T(8,128)S(1)} %all_to_all.5), channel_id=1, source_target_pairs={{0,1},{1,0},{2,3},{3,2},{4,5},{5,4},{6,7},{7,6},{8,9},{9,8},{10,11... | collective-permute-start | bytes 3145736 | tf_op jit(solution)/shard_map/ppermute | solution.py:23
  148.3 5.3 %collective-permute-start.20 = (f32[128,128]{1,0:T(8,128)S(1)}, f32[128,128]{1,0:T(8,128)S(1)}, u32[]{:S(2)}, u32[]{:S(2)}) collective-permute-start(f32[128,128]{1,0:T(8,128)S(1)} %share.1), channel_id=1, source_target_pairs={{0,1},{1,0},{2,3},{3,2},{4,5},{5,4},{6,7},{7,6},{8,9},{9,8},{10,11... | collective-permute-start | bytes 196616 | tf_op jit(solution)/shard_map/ppermute | solution.py:23
  148.4 5.2 %collective-permute-start.21 = (f32[128,128]{1,0:T(8,128)S(1)}, f32[128,128]{1,0:T(8,128)S(1)}, u32[]{:S(2)}, u32[]{:S(2)}) collective-permute-start(f32[128,128]{1,0:T(8,128)S(1)} %share.1), channel_id=1, source_target_pairs={{0,2},{1,3},{2,0},{3,1},{4,6},{5,7},{6,4},{7,5},{8,10},{9,11},{10,... | collective-permute-start | bytes 196616 | tf_op jit(solution)/shard_map/ppermute | solution.py:23
  150.1 4.1 %collective-permute-start.22 = (f32[128,128]{1,0:T(8,128)S(1)}, f32[128,128]{1,0:T(8,128)S(1)}, u32[]{:S(2)}, u32[]{:S(2)}) collective-permute-start(f32[128,128]{1,0:T(8,128)S(1)} %share.1), channel_id=1, source_target_pairs={{0,3},{1,2},{2,1},{3,0},{4,7},{5,6},{6,5},{7,4},{8,11},{9,10},{10,... | collective-permute-start | bytes 196616 | tf_op jit(solution)/shard_map/ppermute | solution.py:23
